TPU v7x, 1024 devices: a whole 8x8x8 slice. The times are simulated.
1024 devices in a mesh: row: 8 (over x), col: 16 (over y, core), layer: 8 (over z).
Axes of the slice: x: 8, y: 8, z: 8, core: 2. Of those that a mesh axis runs over, the one named last changes fastest.
Arguments:
- h_blocks: float32 [2048, 20, 64, 64], P(('row', 'col', 'layer')), may hold values from -0.17 to 0.17
- h_cols: int32 [2048, 20], P(('row', 'col', 'layer')), may hold values from 0 to 2047, as said below
- z_blocks: float32 [2048, 12, 64, 64], P(('row', 'col', 'layer')), may hold values from -1.1 to 1.1
- z_cols: int32 [2048, 12], P(('row', 'col', 'layer')), may hold values from 0 to 2047, as said below
- out_cols: int32 [2048, 16], P(('row', 'col', 'layer')), may hold values from 0 to 2047, as said below
Outputs:
- orthogonal: float32 [2048, 16, 64, 64], P(('row', 'col', 'layer'))
Inputs may be any that keep to these rules, and one draw needn't show every extreme that they name: `h_cols`: row i lists 20 distinct block columns (i + s) mod 2048 with s from -10 to 10, in no particular order; s = 0, -10 and 10 are always among them. `z_cols`: row i lists 12 distinct block columns (i + s) mod 2048 with s from 0 to 12, in no particular order; s = 0 and 12 are always among them. `out_cols`: row a lists 16 distinct block columns (a + s) mod 2048 with s from -10 to 10, in no particular order; s = 0, -10 and 10 are always among them.
All inputs are finite; a program needn't handle non-finite values.
Results may differ from a plain program's by a relative error of at most 0.0003.
Values sent between devices are 32-bit elements; how exact they have to be, the bound alone decides.
No kernel may reach another device: no remote copies, remote signals or barrier semaphores. Data moves between devices by JAX's collectives and lax.ppermute only.
A program may use at most 64 MiB of HBM per device.

v0:
```python
import jax
import jax.numpy as jnp
from jax import lax
from jax.sharding import PartitionSpec as P

NH = 20
NZ = 12
NO = 16
HS = 10
ZS = 13


EXACT = lax.Precision.HIGHEST


def from_behind(shard, axis, by):
    size = lax.axis_size(axis)
    return lax.ppermute(shard, axis, [(i, (i + by) % size) for i in range(size)])


def chain_collect(package, rounds, move):
    stores = tuple((jnp.zeros((rounds,) + piece.shape, piece.dtype) for piece in package))

    def chain_one_round(round_no, carry):
        current, kept = carry
        current = move(current)
        kept = tuple(
            (
                lax.dynamic_update_index_in_dim(store, piece, round_no, 0)
                for store, piece in zip(kept, current)
            )
        )
        return (current, kept)

    _, kept = lax.fori_loop(0, rounds, chain_one_round, (package, stores))
    return kept


def spill_chain(ahead, rounds, move):

    def spill_one_round(round_no, forward):
        forward = move(forward)
        later = lax.dynamic_index_in_dim(
            ahead, jnp.maximum(rounds - 2 - round_no, 0), 0, keepdims=False
        )
        return forward + later * (round_no < rounds - 1).astype(jnp.float32)

    return lax.fori_loop(0, rounds, spill_one_round, ahead[rounds - 1])


def local(h_blocks, h_cols, z_blocks, z_cols, out_cols):
    block_rows = h_blocks.shape[0]
    block_size = h_blocks.shape[2]
    devices = lax.axis_size(("row", "col", "layer"))
    total = block_rows * devices
    first = lax.axis_index(("row", "col", "layer")) * block_rows
    row_ids = jnp.arange(block_rows, dtype=jnp.int32)
    here = first + row_ids
    h_off = (h_cols - here[:, None] + HS) % total - HS
    z_off = (z_cols - here[:, None]) % total
    o_off = (out_cols - here[:, None] + HS) % total
    band = 2 * HS + ZS
    below_rounds = -(-HS // block_rows)
    spill_rounds = -(-(ZS - 1) // block_rows)
    z_off_wire = z_off.astype(jnp.float32)

    def move_down(current):
        return from_behind(current, ("row", "col", "layer"), 1)

    low_blocks, low_offsets = chain_collect((z_blocks, z_off_wire), below_rounds, move_down)

    def move_up_listed(current):
        return from_behind(current, ("row", "col", "layer"), -1)

    up_blocks, up_offsets, up_pattern = chain_collect(
        (z_blocks, z_off_wire, o_off.astype(jnp.float32)), spill_rounds, move_up_listed
    )
    pattern_ext = jnp.concatenate(
        [o_off, up_pattern.reshape((-1, o_off.shape[1])).astype(jnp.int32)], axis=0
    )
    block_shape = z_blocks.shape[1:]
    ext_blocks = jnp.concatenate(
        [
            low_blocks[::-1].reshape((-1,) + block_shape),
            z_blocks,
            up_blocks.reshape((-1,) + block_shape),
        ],
        axis=0,
    )
    ext_offsets = jnp.concatenate(
        [low_offsets[::-1].reshape((-1, NZ)), z_off_wire, up_offsets.reshape((-1, NZ))], axis=0
    ).astype(jnp.int32)
    centre = below_rounds * block_rows + row_ids

    def add_pair(pair_no, w_band):
        h_shift = lax.dynamic_index_in_dim(h_off, pair_no, 1, keepdims=False)
        h_piece = lax.dynamic_index_in_dim(h_blocks, pair_no, 1, keepdims=False)
        picks = centre + h_shift
        z_rows = ext_blocks[picks]
        z_shift = ext_offsets[picks]
        products = jnp.einsum("rpk,rmkq->rmpq", h_piece, z_rows, precision=EXACT)
        slots = h_shift[:, None] + z_shift + HS
        return w_band.at[row_ids[:, None], slots].add(products)

    w_band = lax.fori_loop(
        0, NH, add_pair, jnp.zeros((block_rows, band, block_size, block_size), jnp.float32)
    )
    depth = block_rows * (1 + spill_rounds)
    kept_width = NO

    def add_slot(slot_no, pending):
        z_shift = lax.dynamic_index_in_dim(z_off, slot_no, 1, keepdims=False)
        z_piece = lax.dynamic_index_in_dim(z_blocks, slot_no, 1, keepdims=False)
        targets = row_ids + z_shift
        columns = z_shift[:, None] + pattern_ext[targets]
        selected = w_band[row_ids[:, None], columns]
        terms = jnp.einsum("rkp,rokq->ropq", z_piece, selected, precision=EXACT)
        return pending.at[targets].add(terms)

    pending = lax.fori_loop(
        0, NZ, add_slot, jnp.zeros((depth, kept_width, block_size, block_size), jnp.float32)
    )
    ahead = pending[block_rows:].reshape((spill_rounds, block_rows) + pending.shape[1:])

    def move_listed(forward):
        return from_behind(forward, ("row", "col", "layer"), 1)

    own = pending[:block_rows] + spill_chain(ahead, spill_rounds, move_listed)
    return own


def solution(mesh):
    return jax.shard_map(
        local,
        mesh=mesh,
        in_specs=(
            P(("row", "col", "layer"), None, None, None),
            P(("row", "col", "layer"), None),
            P(("row", "col", "layer"), None, None, None),
            P(("row", "col", "layer"), None),
            P(("row", "col", "layer"), None),
        ),
        out_specs=P(("row", "col", "layer"), None, None, None),
        check_vma=False,
    )
```

profile of v0, /device:TPU:69, one launch (start us, length us, event | category | flops | bytes accessed | tf_op | source)
XLA Modules:
  0.0 817.6 jit_solution(6267903254601934815)
XLA Ops:
  2.8 138.9 %while.86 = (s32[]{:T(128)}, f32[2,12,64,64]{3,2,1,0:T(8,128)S(1)}, f32[2,12]{1,0:T(2,128)S(1)}, f32[2,16]{1,0:T(2,128)S(1)}, f32[6,2,12,64,64]{4,3,2,1,0:T(8,12...) while((s32[]{:T(128)}, f32[2,12,64,64]{3,2,1,0:T(8,128)S(1)}, f32[2,12]{1,0:T(2,128)S(1)}, ...), condition=%wide.region_1.2_spmd, body=%wide.region_0.1_spmd.sunk | while | flops 2 | bytes 3544609 | solution.py:35
  2.8 17.7 %collective-permute-start = (f32[2,12,64,64]{3,2,1,0:T(8,128)S(1)}, f32[2,12,64,64]{3,2,1,0:T(8,128)S(1)}, u32[]{:S(2)}, u32[]{:S(2)}) collective-permute-start(f32[2,12,64,64]{3,2,1,0:T(8,128)S(1)} %get-tuple-element.964), channel_id=1, source_target_pairs={{0,1023},{1,0},{2,1},{3,2},{4,3},{5,4},{6,5},{7,6},{8,7},{9,8},{10... | collective-permute-start | bytes 1179656 | tf_op jit(solution)/shard_map/while/body/eval_jaxpr/ppermute | solution.py:18
  24.4 13.5 %collective-permute-done.1 = f32[2,12]{1,0:T(2,128)S(1)} collective-permute-done((f32[2,12]{1,0:T(2,128)S(1)}, f32[2,12]{1,0:T(2,128)S(1)}, u32[]{:S(2)}, u32[]{:S(2)}) %collective-permute-start.1) | collective-permute-done | bytes 128 | tf_op jit(solution)/shard_map/while/body/eval_jaxpr/ppermute | solution.py:18
  39.0 5.6 collective-permute-start
  48.4 9.9 %collective-permute-done.1 = f32[2,12]{1,0:T(2,128)S(1)} collective-permute-done((f32[2,12]{1,0:T(2,128)S(1)}, f32[2,12]{1,0:T(2,128)S(1)}, u32[]{:S(2)}, u32[]{:S(2)}) %collective-permute-start.1) | collective-permute-done | bytes 128 | tf_op jit(solution)/shard_map/while/body/eval_jaxpr/ppermute | solution.py:18
  59.4 5.6 collective-permute-start
  68.9 8.6 %collective-permute-done.1 = f32[2,12]{1,0:T(2,128)S(1)} collective-permute-done((f32[2,12]{1,0:T(2,128)S(1)}, f32[2,12]{1,0:T(2,128)S(1)}, u32[]{:S(2)}, u32[]{:S(2)}) %collective-permute-start.1) | collective-permute-done | bytes 128 | tf_op jit(solution)/shard_map/while/body/eval_jaxpr/ppermute | solution.py:18
  78.6 5.6 collective-permute-start
  89.9 7.5 collective-permute-done.1
  105.5 4.4 collective-permute-start.2
  109.9 8.4 %collective-permute-done.1 = f32[2,12]{1,0:T(2,128)S(1)} collective-permute-done((f32[2,12]{1,0:T(2,128)S(1)}, f32[2,12]{1,0:T(2,128)S(1)}, u32[]{:S(2)}, u32[]{:S(2)}) %collective-permute-start.1) | collective-permute-done | bytes 128 | tf_op jit(solution)/shard_map/while/body/eval_jaxpr/ppermute | solution.py:18
  129.1 11.6 %collective-permute-done.1 = f32[2,12]{1,0:T(2,128)S(1)} collective-permute-done((f32[2,12]{1,0:T(2,128)S(1)}, f32[2,12]{1,0:T(2,128)S(1)}, u32[]{:S(2)}, u32[]{:S(2)}) %collective-permute-start.1) | collective-permute-done | bytes 128 | tf_op jit(solution)/shard_map/while/body/eval_jaxpr/ppermute | solution.py:18
  141.7 115.2 %while.87 = (s32[]{:T(128)}, f32[2,12,64,64]{3,2,1,0:T(8,128)S(1)}, f32[2,12]{1,0:T(2,128)S(1)}, f32[5,2,12,64,64]{4,3,2,1,0:T(8,128)}, f32[5,2,12]{2,1,0:T(2,128)S(1)}, /*index=5*/s32[]{:T(128)}) while((s32[]{:T(128)}, f32[2,12,64,64]{3,2,1,0:T(8,128)S(1)}, f32[2,12]{1,0:T(2,128)S(1)}, f32[5,2,12,64,64]{4,3,2,1,0:T(8,128)}, ...), condition=%wide.region_3.4_spmd, body=%wide.region_2.3_spmd.sunk | while | flops 2 | bytes 3541733 | solution.py:35
  145.6 19.1 %collective-permute-done.4 = f32[2,12]{1,0:T(2,128)S(1)} collective-permute-done((f32[2,12]{1,0:T(2,128)S(1)}, f32[2,12]{1,0:T(2,128)S(1)}, u32[]{:S(2)}, u32[]{:S(2)}) %collective-permute-start.4) | collective-permute-done | bytes 128 | tf_op jit(solution)/shard_map/while/body/eval_jaxpr/ppermute | solution.py:18
  169.6 17.3 %collective-permute-done.4 = f32[2,12]{1,0:T(2,128)S(1)} collective-permute-done((f32[2,12]{1,0:T(2,128)S(1)}, f32[2,12]{1,0:T(2,128)S(1)}, u32[]{:S(2)}, u32[]{:S(2)}) %collective-permute-start.4) | collective-permute-done | bytes 128 | tf_op jit(solution)/shard_map/while/body/eval_jaxpr/ppermute | solution.py:18
  191.8 17.9 %collective-permute-done.4 = f32[2,12]{1,0:T(2,128)S(1)} collective-permute-done((f32[2,12]{1,0:T(2,128)S(1)}, f32[2,12]{1,0:T(2,128)S(1)}, u32[]{:S(2)}, u32[]{:S(2)}) %collective-permute-start.4) | collective-permute-done | bytes 128 | tf_op jit(solution)/shard_map/while/body/eval_jaxpr/ppermute | solution.py:18
  214.6 18.5 %collective-permute-done.4 = f32[2,12]{1,0:T(2,128)S(1)} collective-permute-done((f32[2,12]{1,0:T(2,128)S(1)}, f32[2,12]{1,0:T(2,128)S(1)}, u32[]{:S(2)}, u32[]{:S(2)}) %collective-permute-start.4) | collective-permute-done | bytes 128 | tf_op jit(solution)/shard_map/while/body/eval_jaxpr/ppermute | solution.py:18
  238.0 17.9 %collective-permute-done.4 = f32[2,12]{1,0:T(2,128)S(1)} collective-permute-done((f32[2,12]{1,0:T(2,128)S(1)}, f32[2,12]{1,0:T(2,128)S(1)}, u32[]{:S(2)}, u32[]{:S(2)}) %collective-permute-start.4) | collective-permute-done | bytes 128 | tf_op jit(solution)/shard_map/while/body/eval_jaxpr/ppermute | solution.py:18
  257.0 4.6 rev.7
  261.6 9.3 %pad_maximum_fusion = f32[24,12,64,64]{3,2,1,0:T(8,128)} fusion(f32[12,12,64,64]{3,2,1,0:T(8,128)} %bitcast.101, f32[2,12,64,64]{3,2,1,0:T(8,128)S(1)} %copy-done, f32[10,12,64,64]{3,2,1,0:T(8,128)} %bitcast.100), kind=kLoop, calls=%fused_computation.50 | loop fusion | flops 2359296 | bytes 9437184 | tf_op jit(solution)/shard_map/concatenate | solution.py:82
  272.6 258.2 %while.89 = (s32[]{:T(128)}, f32[2,33,64,64]{3,2,1,0:T(8,128)}, s32[2,20]{0,1:T(8,128)S(1)}, s32[24,12]{1,0:T(8,128)S(1)}, f32[24,12,64,64]{3,2,1,0:T(8,128)}, /*index=5*/f32[2,20,64,64]{3,2,1,0:T(8,128)}, s32[]{:T(128)}) while((s32[]{:T(128)}, f32[2,33,64,64]{3,2,1,0:T(8,128)}, s32[2,20]{0,1:T(8,128)S(1)}, ...), condition=%wide.region_6.7_spmd.clone, body=%wide.region_4.6_spmd.clone.sunk | while | flops 75597080 | bytes 3610013 | solution.py:105
  273.4 4.3 gather_fusion.1
  280.2 5.4 scatter_fusion
  286.4 4.3 gather_fusion.1
  293.2 5.3 scatter_fusion
  299.2 4.3 gather_fusion.1
  306.0 5.3 scatter_fusion
  312.1 4.3 gather_fusion.1
  318.9 5.3 scatter_fusion
  325.0 4.3 gather_fusion.1
  331.8 5.3 scatter_fusion
  337.9 4.3 gather_fusion.1
  344.7 5.3 scatter_fusion
  350.8 4.3 gather_fusion.1
  357.6 5.4 scatter_fusion
  363.8 4.3 gather_fusion.1
  370.6 5.3 scatter_fusion
  376.7 4.3 gather_fusion.1
  383.5 5.3 scatter_fusion
  389.6 4.3 gather_fusion.1
  396.4 5.4 scatter_fusion
  402.5 4.3 gather_fusion.1
  409.3 5.3 scatter_fusion
  422.2 5.4 scatter_fusion
  435.1 5.3 scatter_fusion
  448.0 5.3 scatter_fusion
  454.1 4.3 gather_fusion.1
  460.9 5.3 scatter_fusion
  473.9 5.4 scatter_fusion
  480.0 4.3 gather_fusion.1
  486.8 5.4 scatter_fusion
  499.7 5.3 scatter_fusion
  512.6 5.3 scatter_fusion
  518.7 4.3 gather_fusion.1
  525.5 5.3 scatter_fusion
  534.8 98.4 %while.90 = (s32[]{:T(128)}, f32[14,16,64,64]{3,2,1,0:T(8,128)}, s32[2,12]{0,1:T(8,128)S(1)}, s32[14,16]{1,0:T(8,128)S(1)}, f32[2,33,64,64]{3,2,1,0:T(8,128)}, /*index=5*/f32[2,12,64,64]{3,2,1,0:T(8,128)S(1)}, s32[]{:T(128)}) while((s32[]{:T(128)}, f32[14,16,64,64]{3,2,1,0:T(8,128)}, s32[2,12]{0,1:T(8,128)S(1)}, ...), condition=%wide.region_9.10_spmd.clone.clone, body=%wide.region_7.9_spmd.clone.clone.sunk | while | flops 100795632 | bytes 5313693 | solution.py:120
  633.1 6.6 slice.13
  641.1 174.2 %while.88 = (s32[]{:T(128)}, f32[2,16,64,64]{3,2,1,0:T(8,128)S(1)}, f32[6,2,16,64,64]{4,3,2,1,0:T(8,128)}, s32[]{:T(128)}, s32[]{:T(128)}, /*index=5*/s32[]{:T(128)}, s32[]{:T(128)}) while((s32[]{:T(128)}, f32[2,16,64,64]{3,2,1,0:T(8,128)S(1)}, f32[6,2,16,64,64]{4,3,2,1,0:T(8,128)}, s32[]{:T(128)}, s32[]{:T(128)}, /*index=5*/s32[]{:T(128)}, ...), condition=%wide.region_11.12_spmd, body=%wide.region_10.11_spmd.sunk | while | flops 262150 | bytes 3670179 | solution.py:48
  643.1 25.3 %collective-permute-done.5 = f32[2,16,64,64]{3,2,1,0:T(8,128)S(1)} collective-permute-done((f32[2,16,64,64]{3,2,1,0:T(8,128)S(1)}, f32[2,16,64,64]{3,2,1,0:T(8,128)S(1)}, u32[]{:S(2)}, u32[]{:S(2)}) %collective-permute-start.5) | collective-permute-done | bytes 524320 | tf_op jit(solution)/shard_map/while/body/eval_jaxpr/ppermute | solution.py:18
  671.8 26.1 %collective-permute-done.5 = f32[2,16,64,64]{3,2,1,0:T(8,128)S(1)} collective-permute-done((f32[2,16,64,64]{3,2,1,0:T(8,128)S(1)}, f32[2,16,64,64]{3,2,1,0:T(8,128)S(1)}, u32[]{:S(2)}, u32[]{:S(2)}) %collective-permute-start.5) | collective-permute-done | bytes 524320 | tf_op jit(solution)/shard_map/while/body/eval_jaxpr/ppermute | solution.py:18
  701.2 25.3 %collective-permute-done.5 = f32[2,16,64,64]{3,2,1,0:T(8,128)S(1)} collective-permute-done((f32[2,16,64,64]{3,2,1,0:T(8,128)S(1)}, f32[2,16,64,64]{3,2,1,0:T(8,128)S(1)}, u32[]{:S(2)}, u32[]{:S(2)}) %collective-permute-start.5) | collective-permute-done | bytes 524320 | tf_op jit(solution)/shard_map/while/body/eval_jaxpr/ppermute | solution.py:18
  729.8 25.9 %collective-permute-done.5 = f32[2,16,64,64]{3,2,1,0:T(8,128)S(1)} collective-permute-done((f32[2,16,64,64]{3,2,1,0:T(8,128)S(1)}, f32[2,16,64,64]{3,2,1,0:T(8,128)S(1)}, u32[]{:S(2)}, u32[]{:S(2)}) %collective-permute-start.5) | collective-permute-done | bytes 524320 | tf_op jit(solution)/shard_map/while/body/eval_jaxpr/ppermute | solution.py:18
  759.1 25.5 %collective-permute-done.5 = f32[2,16,64,64]{3,2,1,0:T(8,128)S(1)} collective-permute-done((f32[2,16,64,64]{3,2,1,0:T(8,128)S(1)}, f32[2,16,64,64]{3,2,1,0:T(8,128)S(1)}, u32[]{:S(2)}, u32[]{:S(2)}) %collective-permute-start.5) | collective-permute-done | bytes 524320 | tf_op jit(solution)/shard_map/while/body/eval_jaxpr/ppermute | solution.py:18
  787.9 25.9 %collective-permute-done.5 = f32[2,16,64,64]{3,2,1,0:T(8,128)S(1)} collective-permute-done((f32[2,16,64,64]{3,2,1,0:T(8,128)S(1)}, f32[2,16,64,64]{3,2,1,0:T(8,128)S(1)}, u32[]{:S(2)}, u32[]{:S(2)}) %collective-permute-start.5) | collective-permute-done | bytes 524320 | tf_op jit(solution)/shard_map/while/body/eval_jaxpr/ppermute | solution.py:18
  (446 shorter events, 285.4 us)
Async XLA Ops:
  2.8 139.0 %copy-start.1 = (f32[2,12,64,64]{3,2,1,0:T(8,128)S(1)}, f32[2,12,64,64]{3,2,1,0:T(8,128)}, u32[]{:S(2)}) copy-start(f32[2,12,64,64]{3,2,1,0:T(8,128)} %param.17) | copy-start | bytes 1179652
  2.8 35.1 %collective-permute-start = (f32[2,12,64,64]{3,2,1,0:T(8,128)S(1)}, f32[2,12,64,64]{3,2,1,0:T(8,128)S(1)}, u32[]{:S(2)}, u32[]{:S(2)}) collective-permute-start(f32[2,12,64,64]{3,2,1,0:T(8,128)S(1)} %get-tuple-element.964), channel_id=1, source_target_pairs={{0,1023},{1,0},{2,1},{3,2},{4,3},{5,4},{6,5},{7,6},{8,7},{9,8},{10... | collective-permute-start | bytes 1179656 | tf_op jit(solution)/shard_map/while/body/eval_jaxpr/ppermute | solution.py:18
  20.5 17.4 %collective-permute-start.1 = (f32[2,12]{1,0:T(2,128)S(1)}, f32[2,12]{1,0:T(2,128)S(1)}, u32[]{:S(2)}, u32[]{:S(2)}) collective-permute-start(f32[2,12]{1,0:T(2,128)S(1)} %get-tuple-element.965), channel_id=1, source_target_pairs={{0,1023},{1,0},{2,1},{3,2},{4,3},{5,4},{6,5},{7,6},{8,7},{9,8},{10... | collective-permute-start | bytes 296 | tf_op jit(solution)/shard_map/while/body/eval_jaxpr/ppermute | solution.py:18
  22.4 15.5 %collective-permute-start.2 = (f32[2,16]{1,0:T(2,128)S(1)}, f32[2,16]{1,0:T(2,128)S(1)}, u32[]{:S(2)}, u32[]{:S(2)}) collective-permute-start(f32[2,16]{1,0:T(2,128)S(1)} %get-tuple-element.966), channel_id=1, source_target_pairs={{0,1023},{1,0},{2,1},{3,2},{4,3},{5,4},{6,5},{7,6},{8,7},{9,8},{10... | collective-permute-start | bytes 392 | tf_op jit(solution)/shard_map/while/body/eval_jaxpr/ppermute | solution.py:18
  39.0 19.4 %collective-permute-start = (f32[2,12,64,64]{3,2,1,0:T(8,128)S(1)}, f32[2,12,64,64]{3,2,1,0:T(8,128)S(1)}, u32[]{:S(2)}, u32[]{:S(2)}) collective-permute-start(f32[2,12,64,64]{3,2,1,0:T(8,128)S(1)} %get-tuple-element.964), channel_id=1, source_target_pairs={{0,1023},{1,0},{2,1},{3,2},{4,3},{5,4},{6,5},{7,6},{8,7},{9,8},{10... | collective-permute-start | bytes 1179656 | tf_op jit(solution)/shard_map/while/body/eval_jaxpr/ppermute | solution.py:18
  44.6 13.7 %collective-permute-start.1 = (f32[2,12]{1,0:T(2,128)S(1)}, f32[2,12]{1,0:T(2,128)S(1)}, u32[]{:S(2)}, u32[]{:S(2)}) collective-permute-start(f32[2,12]{1,0:T(2,128)S(1)} %get-tuple-element.965), channel_id=1, source_target_pairs={{0,1023},{1,0},{2,1},{3,2},{4,3},{5,4},{6,5},{7,6},{8,7},{9,8},{10... | collective-permute-start | bytes 296 | tf_op jit(solution)/shard_map/while/body/eval_jaxpr/ppermute | solution.py:18
  46.5 11.8 %collective-permute-start.2 = (f32[2,16]{1,0:T(2,128)S(1)}, f32[2,16]{1,0:T(2,128)S(1)}, u32[]{:S(2)}, u32[]{:S(2)}) collective-permute-start(f32[2,16]{1,0:T(2,128)S(1)} %get-tuple-element.966), channel_id=1, source_target_pairs={{0,1023},{1,0},{2,1},{3,2},{4,3},{5,4},{6,5},{7,6},{8,7},{9,8},{10... | collective-permute-start | bytes 392 | tf_op jit(solution)/shard_map/while/body/eval_jaxpr/ppermute | solution.py:18
  59.4 18.2 %collective-permute-start = (f32[2,12,64,64]{3,2,1,0:T(8,128)S(1)}, f32[2,12,64,64]{3,2,1,0:T(8,128)S(1)}, u32[]{:S(2)}, u32[]{:S(2)}) collective-permute-start(f32[2,12,64,64]{3,2,1,0:T(8,128)S(1)} %get-tuple-element.964), channel_id=1, source_target_pairs={{0,1023},{1,0},{2,1},{3,2},{4,3},{5,4},{6,5},{7,6},{8,7},{9,8},{10... | collective-permute-start | bytes 1179656 | tf_op jit(solution)/shard_map/while/body/eval_jaxpr/ppermute | solution.py:18
  65.0 12.5 %collective-permute-start.1 = (f32[2,12]{1,0:T(2,128)S(1)}, f32[2,12]{1,0:T(2,128)S(1)}, u32[]{:S(2)}, u32[]{:S(2)}) collective-permute-start(f32[2,12]{1,0:T(2,128)S(1)} %get-tuple-element.965), channel_id=1, source_target_pairs={{0,1023},{1,0},{2,1},{3,2},{4,3},{5,4},{6,5},{7,6},{8,7},{9,8},{10... | collective-permute-start | bytes 296 | tf_op jit(solution)/shard_map/while/body/eval_jaxpr/ppermute | solution.py:18
  66.9 10.6 %collective-permute-start.2 = (f32[2,16]{1,0:T(2,128)S(1)}, f32[2,16]{1,0:T(2,128)S(1)}, u32[]{:S(2)}, u32[]{:S(2)}) collective-permute-start(f32[2,16]{1,0:T(2,128)S(1)} %get-tuple-element.966), channel_id=1, source_target_pairs={{0,1023},{1,0},{2,1},{3,2},{4,3},{5,4},{6,5},{7,6},{8,7},{9,8},{10... | collective-permute-start | bytes 392 | tf_op jit(solution)/shard_map/while/body/eval_jaxpr/ppermute | solution.py:18
  78.6 18.8 %collective-permute-start = (f32[2,12,64,64]{3,2,1,0:T(8,128)S(1)}, f32[2,12,64,64]{3,2,1,0:T(8,128)S(1)}, u32[]{:S(2)}, u32[]{:S(2)}) collective-permute-start(f32[2,12,64,64]{3,2,1,0:T(8,128)S(1)} %get-tuple-element.964), channel_id=1, source_target_pairs={{0,1023},{1,0},{2,1},{3,2},{4,3},{5,4},{6,5},{7,6},{8,7},{9,8},{10... | collective-permute-start | bytes 1179656 | tf_op jit(solution)/shard_map/while/body/eval_jaxpr/ppermute | solution.py:18
  84.2 13.2 %collective-permute-start.1 = (f32[2,12]{1,0:T(2,128)S(1)}, f32[2,12]{1,0:T(2,128)S(1)}, u32[]{:S(2)}, u32[]{:S(2)}) collective-permute-start(f32[2,12]{1,0:T(2,128)S(1)} %get-tuple-element.965), channel_id=1, source_target_pairs={{0,1023},{1,0},{2,1},{3,2},{4,3},{5,4},{6,5},{7,6},{8,7},{9,8},{10... | collective-permute-start | bytes 296 | tf_op jit(solution)/shard_map/while/body/eval_jaxpr/ppermute | solution.py:18
  86.1 11.3 %collective-permute-start.2 = (f32[2,16]{1,0:T(2,128)S(1)}, f32[2,16]{1,0:T(2,128)S(1)}, u32[]{:S(2)}, u32[]{:S(2)}) collective-permute-start(f32[2,16]{1,0:T(2,128)S(1)} %get-tuple-element.966), channel_id=1, source_target_pairs={{0,1023},{1,0},{2,1},{3,2},{4,3},{5,4},{6,5},{7,6},{8,7},{9,8},{10... | collective-permute-start | bytes 392 | tf_op jit(solution)/shard_map/while/body/eval_jaxpr/ppermute | solution.py:18
  98.5 19.9 %collective-permute-start = (f32[2,12,64,64]{3,2,1,0:T(8,128)S(1)}, f32[2,12,64,64]{3,2,1,0:T(8,128)S(1)}, u32[]{:S(2)}, u32[]{:S(2)}) collective-permute-start(f32[2,12,64,64]{3,2,1,0:T(8,128)S(1)} %get-tuple-element.964), channel_id=1, source_target_pairs={{0,1023},{1,0},{2,1},{3,2},{4,3},{5,4},{6,5},{7,6},{8,7},{9,8},{10... | collective-permute-start | bytes 1179656 | tf_op jit(solution)/shard_map/while/body/eval_jaxpr/ppermute | solution.py:18
  102.3 16.1 %collective-permute-start.1 = (f32[2,12]{1,0:T(2,128)S(1)}, f32[2,12]{1,0:T(2,128)S(1)}, u32[]{:S(2)}, u32[]{:S(2)}) collective-permute-start(f32[2,12]{1,0:T(2,128)S(1)} %get-tuple-element.965), channel_id=1, source_target_pairs={{0,1023},{1,0},{2,1},{3,2},{4,3},{5,4},{6,5},{7,6},{8,7},{9,8},{10... | collective-permute-start | bytes 296 | tf_op jit(solution)/shard_map/while/body/eval_jaxpr/ppermute | solution.py:18
  105.5 12.8 %collective-permute-start.2 = (f32[2,16]{1,0:T(2,128)S(1)}, f32[2,16]{1,0:T(2,128)S(1)}, u32[]{:S(2)}, u32[]{:S(2)}) collective-permute-start(f32[2,16]{1,0:T(2,128)S(1)} %get-tuple-element.966), channel_id=1, source_target_pairs={{0,1023},{1,0},{2,1},{3,2},{4,3},{5,4},{6,5},{7,6},{8,7},{9,8},{10... | collective-permute-start | bytes 392 | tf_op jit(solution)/shard_map/while/body/eval_jaxpr/ppermute | solution.py:18
  119.5 21.2 %collective-permute-start = (f32[2,12,64,64]{3,2,1,0:T(8,128)S(1)}, f32[2,12,64,64]{3,2,1,0:T(8,128)S(1)}, u32[]{:S(2)}, u32[]{:S(2)}) collective-permute-start(f32[2,12,64,64]{3,2,1,0:T(8,128)S(1)} %get-tuple-element.964), channel_id=1, source_target_pairs={{0,1023},{1,0},{2,1},{3,2},{4,3},{5,4},{6,5},{7,6},{8,7},{9,8},{10... | collective-permute-start | bytes 1179656 | tf_op jit(solution)/shard_map/while/body/eval_jaxpr/ppermute | solution.py:18
  123.1 17.5 %collective-permute-start.1 = (f32[2,12]{1,0:T(2,128)S(1)}, f32[2,12]{1,0:T(2,128)S(1)}, u32[]{:S(2)}, u32[]{:S(2)}) collective-permute-start(f32[2,12]{1,0:T(2,128)S(1)} %get-tuple-element.965), channel_id=1, source_target_pairs={{0,1023},{1,0},{2,1},{3,2},{4,3},{5,4},{6,5},{7,6},{8,7},{9,8},{10... | collective-permute-start | bytes 296 | tf_op jit(solution)/shard_map/while/body/eval_jaxpr/ppermute | solution.py:18
  125.0 15.6 %collective-permute-start.2 = (f32[2,16]{1,0:T(2,128)S(1)}, f32[2,16]{1,0:T(2,128)S(1)}, u32[]{:S(2)}, u32[]{:S(2)}) collective-permute-start(f32[2,16]{1,0:T(2,128)S(1)} %get-tuple-element.966), channel_id=1, source_target_pairs={{0,1023},{1,0},{2,1},{3,2},{4,3},{5,4},{6,5},{7,6},{8,7},{9,8},{10... | collective-permute-start | bytes 392 | tf_op jit(solution)/shard_map/while/body/eval_jaxpr/ppermute | solution.py:18
  141.8 23.0 %collective-permute-start.3 = (f32[2,12,64,64]{3,2,1,0:T(8,128)S(1)}, f32[2,12,64,64]{3,2,1,0:T(8,128)S(1)}, u32[]{:S(2)}, u32[]{:S(2)}) collective-permute-start(f32[2,12,64,64]{3,2,1,0:T(8,128)S(1)} %get-tuple-element.986), channel_id=1, source_target_pairs={{0,1},{1,2},{2,3},{3,4},{4,5},{5,6},{6,7},{7,8},{8,9},{9,10},{10,1... | collective-permute-start | bytes 1179656 | tf_op jit(solution)/shard_map/while/body/eval_jaxpr/ppermute | solution.py:18
  143.7 21.1 %collective-permute-start.4 = (f32[2,12]{1,0:T(2,128)S(1)}, f32[2,12]{1,0:T(2,128)S(1)}, u32[]{:S(2)}, u32[]{:S(2)}) collective-permute-start(f32[2,12]{1,0:T(2,128)S(1)} %get-tuple-element.987), channel_id=1, source_target_pairs={{0,1},{1,2},{2,3},{3,4},{4,5},{5,6},{6,7},{7,8},{8,9},{9,10},{10,1... | collective-permute-start | bytes 296 | tf_op jit(solution)/shard_map/while/body/eval_jaxpr/ppermute | solution.py:18
  165.8 21.1 %collective-permute-start.3 = (f32[2,12,64,64]{3,2,1,0:T(8,128)S(1)}, f32[2,12,64,64]{3,2,1,0:T(8,128)S(1)}, u32[]{:S(2)}, u32[]{:S(2)}) collective-permute-start(f32[2,12,64,64]{3,2,1,0:T(8,128)S(1)} %get-tuple-element.986), channel_id=1, source_target_pairs={{0,1},{1,2},{2,3},{3,4},{4,5},{5,6},{6,7},{7,8},{8,9},{9,10},{10,1... | collective-permute-start | bytes 1179656 | tf_op jit(solution)/shard_map/while/body/eval_jaxpr/ppermute | solution.py:18
  167.7 19.2 %collective-permute-start.4 = (f32[2,12]{1,0:T(2,128)S(1)}, f32[2,12]{1,0:T(2,128)S(1)}, u32[]{:S(2)}, u32[]{:S(2)}) collective-permute-start(f32[2,12]{1,0:T(2,128)S(1)} %get-tuple-element.987), channel_id=1, source_target_pairs={{0,1},{1,2},{2,3},{3,4},{4,5},{5,6},{6,7},{7,8},{8,9},{9,10},{10,1... | collective-permute-start | bytes 296 | tf_op jit(solution)/shard_map/while/body/eval_jaxpr/ppermute | solution.py:18
  188.0 21.8 %collective-permute-start.3 = (f32[2,12,64,64]{3,2,1,0:T(8,128)S(1)}, f32[2,12,64,64]{3,2,1,0:T(8,128)S(1)}, u32[]{:S(2)}, u32[]{:S(2)}) collective-permute-start(f32[2,12,64,64]{3,2,1,0:T(8,128)S(1)} %get-tuple-element.986), channel_id=1, source_target_pairs={{0,1},{1,2},{2,3},{3,4},{4,5},{5,6},{6,7},{7,8},{8,9},{9,10},{10,1... | collective-permute-start | bytes 1179656 | tf_op jit(solution)/shard_map/while/body/eval_jaxpr/ppermute | solution.py:18
  189.9 19.8 %collective-permute-start.4 = (f32[2,12]{1,0:T(2,128)S(1)}, f32[2,12]{1,0:T(2,128)S(1)}, u32[]{:S(2)}, u32[]{:S(2)}) collective-permute-start(f32[2,12]{1,0:T(2,128)S(1)} %get-tuple-element.987), channel_id=1, source_target_pairs={{0,1},{1,2},{2,3},{3,4},{4,5},{5,6},{6,7},{7,8},{8,9},{9,10},{10,1... | collective-permute-start | bytes 296 | tf_op jit(solution)/shard_map/while/body/eval_jaxpr/ppermute | solution.py:18
  210.7 22.4 %collective-permute-start.3 = (f32[2,12,64,64]{3,2,1,0:T(8,128)S(1)}, f32[2,12,64,64]{3,2,1,0:T(8,128)S(1)}, u32[]{:S(2)}, u32[]{:S(2)}) collective-permute-start(f32[2,12,64,64]{3,2,1,0:T(8,128)S(1)} %get-tuple-element.986), channel_id=1, source_target_pairs={{0,1},{1,2},{2,3},{3,4},{4,5},{5,6},{6,7},{7,8},{8,9},{9,10},{10,1... | collective-permute-start | bytes 1179656 | tf_op jit(solution)/shard_map/while/body/eval_jaxpr/ppermute | solution.py:18
  212.7 20.4 %collective-permute-start.4 = (f32[2,12]{1,0:T(2,128)S(1)}, f32[2,12]{1,0:T(2,128)S(1)}, u32[]{:S(2)}, u32[]{:S(2)}) collective-permute-start(f32[2,12]{1,0:T(2,128)S(1)} %get-tuple-element.987), channel_id=1, source_target_pairs={{0,1},{1,2},{2,3},{3,4},{4,5},{5,6},{6,7},{7,8},{8,9},{9,10},{10,1... | collective-permute-start | bytes 296 | tf_op jit(solution)/shard_map/while/body/eval_jaxpr/ppermute | solution.py:18
  234.1 21.8 %collective-permute-start.3 = (f32[2,12,64,64]{3,2,1,0:T(8,128)S(1)}, f32[2,12,64,64]{3,2,1,0:T(8,128)S(1)}, u32[]{:S(2)}, u32[]{:S(2)}) collective-permute-start(f32[2,12,64,64]{3,2,1,0:T(8,128)S(1)} %get-tuple-element.986), channel_id=1, source_target_pairs={{0,1},{1,2},{2,3},{3,4},{4,5},{5,6},{6,7},{7,8},{8,9},{9,10},{10,1... | collective-permute-start | bytes 1179656 | tf_op jit(solution)/shard_map/while/body/eval_jaxpr/ppermute | solution.py:18
  236.0 19.8 %collective-permute-start.4 = (f32[2,12]{1,0:T(2,128)S(1)}, f32[2,12]{1,0:T(2,128)S(1)}, u32[]{:S(2)}, u32[]{:S(2)}) collective-permute-start(f32[2,12]{1,0:T(2,128)S(1)} %get-tuple-element.987), channel_id=1, source_target_pairs={{0,1},{1,2},{2,3},{3,4},{4,5},{5,6},{6,7},{7,8},{8,9},{9,10},{10,1... | collective-permute-start | bytes 296 | tf_op jit(solution)/shard_map/while/body/eval_jaxpr/ppermute | solution.py:18
  256.9 4.6 copy-start
  261.6 9.3 %copy-start.2 = (s32[2,20]{1,0:T(2,128)S(1)}, s32[2,20]{1,0:T(2,128)}, u32[]{:S(2)}) copy-start(s32[2,20]{1,0:T(2,128)} %param.16) | copy-start | bytes 484
  641.1 27.4 %collective-permute-start.5 = (f32[2,16,64,64]{3,2,1,0:T(8,128)S(1)}, f32[2,16,64,64]{3,2,1,0:T(8,128)S(1)}, u32[]{:S(2)}, u32[]{:S(2)}) collective-permute-start(f32[2,16,64,64]{3,2,1,0:T(8,128)S(1)} %get-tuple-element.1047), channel_id=1, source_target_pairs={{0,1},{1,2},{2,3},{3,4},{4,5},{5,6},{6,7},{7,8},{8,9},{9,10},{10,1... | collective-permute-start | bytes 1572872 | tf_op jit(solution)/shard_map/while/body/eval_jaxpr/ppermute | solution.py:18
  669.8 28.0 %collective-permute-start.5 = (f32[2,16,64,64]{3,2,1,0:T(8,128)S(1)}, f32[2,16,64,64]{3,2,1,0:T(8,128)S(1)}, u32[]{:S(2)}, u32[]{:S(2)}) collective-permute-start(f32[2,16,64,64]{3,2,1,0:T(8,128)S(1)} %get-tuple-element.1047), channel_id=1, source_target_pairs={{0,1},{1,2},{2,3},{3,4},{4,5},{5,6},{6,7},{7,8},{8,9},{9,10},{10,1... | collective-permute-start | bytes 1572872 | tf_op jit(solution)/shard_map/while/body/eval_jaxpr/ppermute | solution.py:18
  699.2 27.3 %collective-permute-start.5 = (f32[2,16,64,64]{3,2,1,0:T(8,128)S(1)}, f32[2,16,64,64]{3,2,1,0:T(8,128)S(1)}, u32[]{:S(2)}, u32[]{:S(2)}) collective-permute-start(f32[2,16,64,64]{3,2,1,0:T(8,128)S(1)} %get-tuple-element.1047), channel_id=1, source_target_pairs={{0,1},{1,2},{2,3},{3,4},{4,5},{5,6},{6,7},{7,8},{8,9},{9,10},{10,1... | collective-permute-start | bytes 1572872 | tf_op jit(solution)/shard_map/while/body/eval_jaxpr/ppermute | solution.py:18
  727.9 27.9 %collective-permute-start.5 = (f32[2,16,64,64]{3,2,1,0:T(8,128)S(1)}, f32[2,16,64,64]{3,2,1,0:T(8,128)S(1)}, u32[]{:S(2)}, u32[]{:S(2)}) collective-permute-start(f32[2,16,64,64]{3,2,1,0:T(8,128)S(1)} %get-tuple-element.1047), channel_id=1, source_target_pairs={{0,1},{1,2},{2,3},{3,4},{4,5},{5,6},{6,7},{7,8},{8,9},{9,10},{10,1... | collective-permute-start | bytes 1572872 | tf_op jit(solution)/shard_map/while/body/eval_jaxpr/ppermute | solution.py:18
  757.2 27.4 %collective-permute-start.5 = (f32[2,16,64,64]{3,2,1,0:T(8,128)S(1)}, f32[2,16,64,64]{3,2,1,0:T(8,128)S(1)}, u32[]{:S(2)}, u32[]{:S(2)}) collective-permute-start(f32[2,16,64,64]{3,2,1,0:T(8,128)S(1)} %get-tuple-element.1047), channel_id=1, source_target_pairs={{0,1},{1,2},{2,3},{3,4},{4,5},{5,6},{6,7},{7,8},{8,9},{9,10},{10,1... | collective-permute-start | bytes 1572872 | tf_op jit(solution)/shard_map/while/body/eval_jaxpr/ppermute | solution.py:18
  786.0 27.9 %collective-permute-start.5 = (f32[2,16,64,64]{3,2,1,0:T(8,128)S(1)}, f32[2,16,64,64]{3,2,1,0:T(8,128)S(1)}, u32[]{:S(2)}, u32[]{:S(2)}) collective-permute-start(f32[2,16,64,64]{3,2,1,0:T(8,128)S(1)} %get-tuple-element.1047), channel_id=1, source_target_pairs={{0,1},{1,2},{2,3},{3,4},{4,5},{5,6},{6,7},{7,8},{8,9},{9,10},{10,1... | collective-permute-start | bytes 1572872 | tf_op jit(solution)/shard_map/while/body/eval_jaxpr/ppermute | solution.py:18
where the time goes:
time: 825 us; the launch traced here: 818 us
  waiting for transfers between devices  304 us (37%)
  local copies, waits for them, and re-layouts  174 us (21%)
  other arithmetic  168 us (20%)
  starting transfers between devices  104 us (13%)
  matrix products  66.5 us (8%)
    ppermute x34, waiting for transfers between devices, from_behind(): lax.ppermute(shard, axis, [(i, (i + by) % size) for i in range(size)])  304 us
    scatter-add x20, other arithmetic, add_pair(): return w_band.at[row_ids[:, None], slots].add(products)  107 us
    ppermute x34, starting transfers between devices, from_behind(): lax.ppermute(shard, axis, [(i, (i + by) % size) for i in range(size)])  104 us
    gather x20, local copies, waits for them, and re-layouts, add_pair(): z_rows = ext_blocks[picks]  85.5 us
    dot_general x20, matrix products, add_pair(): products = jnp.einsum('rpk,rmkq->rmpq', h_piece, z_rows, precision=EXACT)  44.9 us
    scatter-add x12, other arithmetic, add_slot(): return pending.at[targets].add(terms)  36.8 us
    gather x12, local copies, waits for them, and re-layouts, add_slot(): selected = w_band[row_ids[:, None], columns]  26.8 us
    dot_general x12, matrix products, add_slot(): terms = jnp.einsum('rkp,rokq->ropq', z_piece, selected, precision=EXACT)  21.6 us
  transfers between devices with their start and end apart: 34, of which 17 were waited for; matrix products, arithmetic and copies ran while one was open for 0% of the time, Pallas kernels for 0%

commit v1 on v0

v1 whole, which is shorter than its diff:
```python
import functools

import jax
import jax.numpy as jnp
from jax import lax
from jax.experimental import pallas as pl
from jax.experimental.pallas import tpu as pltpu
from jax.sharding import PartitionSpec as P

NH = 20
NZ = 12
NO = 16
HS = 10
ZS = 13
B = 64
AXES = ("row", "col", "layer")
REACH = 5
LAST = 6
NJ = 2 * (2 * REACH + 1)
NC = NJ + ZS - 1
NA = 2 * (LAST + 1)
HALF = NZ // 2 * B
ZROWS = 2 * HALF
SPLIT = False
F32 = jnp.float32
BF16 = jnp.bfloat16

PARAMS = pltpu.CompilerParams(vmem_limit_bytes=48 * 1024 * 1024)


def split(x):
    hi = x.astype(BF16)
    return hi, (x - hi.astype(F32)).astype(BF16)


def shift(x, by):
    size = lax.axis_size(AXES)
    return lax.ppermute(x, AXES, [(i, (i + by) % size) for i in range(size)])


def vmem(count):
    return [pl.BlockSpec(memory_space=pltpu.VMEM)] * count


def smem(count):
    return [pl.BlockSpec(memory_space=pltpu.SMEM)] * count


def pack_kernel(here_ref, cols, z_ref, out_ref, h_off, meta_ref):
    total = here_ref[1]

    def offsets(at, count, low):
        rows = lax.broadcasted_iota(jnp.int32, (2, count), 0) + here_ref[0]
        away = cols[:, at : at + count] - rows
        away = jnp.where(away < low, away + total, away)
        return jnp.where(away >= low + total, away - total, away)

    h_off[...] = offsets(0, NH, -HS)
    meta_ref[...] = jnp.zeros_like(meta_ref)
    meta_ref[0:2, 0:NZ] = offsets(NH, NZ, 0)
    meta_ref[2:4, 0:NO] = offsets(NH + NZ, NO, -HS) + HS
    out_ref[ZROWS:, :] = meta_ref[...].astype(F32)
    for t in range(NZ):
        out_ref[t * B : (t + 1) * B, :] = z_ref[t].T


def pack(here, cols, z_pairs):
    return pl.pallas_call(
        pack_kernel,
        out_shape=(
            jax.ShapeDtypeStruct((ZROWS + 8, 2 * B), F32),
            jax.ShapeDtypeStruct((2, NH), jnp.int32),
            jax.ShapeDtypeStruct((8, 2 * B), jnp.int32),
        ),
        in_specs=smem(1) + vmem(2),
        out_specs=tuple(vmem(3)),
        compiler_params=PARAMS,
        name="pack",
    )(here, cols, z_pairs)


def prep_kernel(h_off, meta, h_ref, z_ref, hh_ref, hl_ref, zz_ref, stack):
    stack[...] = jnp.zeros_like(stack)
    for r in range(2):
        for k in range(NH):
            stack[h_off[r, k] + (HS + r), r * B : (r + 1) * B, :] = h_ref[r, k]
    for e in range(NJ):
        hi, lo = split(stack[e].T)
        hh_ref[e] = hi
        hl_ref[e] = lo
    stack[0:NA] = jnp.zeros((NA,) + stack.shape[1:], F32)
    for r in range(2):
        for m in range(NZ):
            stack[meta[r, m] + r, r * B : (r + 1) * B, :] = z_ref[r, m]
    for a in range(NA):
        hi, lo = split(stack[a].T)
        zz_ref[a, 0:B, 0 : 2 * B] = hi
        zz_ref[a, 0:B, 2 * B :] = hi
        zz_ref[a, B:, 0 : 2 * B] = lo
        zz_ref[a, B:, 2 * B :] = jnp.zeros_like(lo)


def prep(h_off, meta, h_blocks, z_blocks):
    return pl.pallas_call(
        prep_kernel,
        out_shape=(
            jax.ShapeDtypeStruct((NJ, B, 2 * B), BF16),
            jax.ShapeDtypeStruct((NJ, B, 2 * B), BF16),
            jax.ShapeDtypeStruct((NA, 2 * B, 4 * B), BF16),
        ),
        in_specs=smem(2) + vmem(2),
        out_specs=tuple(vmem(3)),
        scratch_shapes=[pltpu.VMEM((NJ, 2 * B, B), F32)],
        compiler_params=PARAMS,
        name="prep",
    )(h_off, meta, h_blocks, z_blocks)


def add_rows(d, meta, x_ref, hh_ref, hl_ref, w_ref):
    for r in range(2):
        e = 2 * (d + REACH) + r
        hi, lo = split(x_ref[r * HALF : (r + 1) * HALF, :])
        hh, hl = hh_ref[e], hl_ref[e]
        none = jnp.zeros_like(hh)
        top = jnp.concatenate([hh, none], axis=1)
        low = jnp.concatenate([none, hh], axis=1)
        main = jnp.concatenate([top, low, top, low], axis=0)
        rest = jnp.concatenate(
            [jnp.concatenate([hl, none], axis=1), jnp.concatenate([none, hl], axis=1)], axis=0
        )
        products = jnp.dot(
            jnp.concatenate([hi, lo], axis=1), main, preferred_element_type=F32
        ) + jnp.dot(hi, rest, preferred_element_type=F32)
        for m in range(NZ):
            at = meta[r, m] + e
            part = products[m // 2 * B : (m // 2 + 1) * B, m % 2 * 2 * B : (m % 2 + 1) * 2 * B]
            w_ref[at] = w_ref[at] + part


def gather_kernel(ds, first, last, *refs):
    n = len(ds)
    metas, xs = refs[:n], refs[n : 2 * n]
    hh_ref, hl_ref = refs[2 * n : 2 * n + 2]
    rest = list(refs[2 * n + 2 :])
    if last:
        w_in, ww_ref, w_ref = rest
        w_ref[...] = w_in[...]
    elif first:
        (w_ref,) = rest
        w_ref[...] = jnp.zeros_like(w_ref)
    else:
        w_in, w_ref = rest
        w_ref[...] = w_in[...]
    for d, meta, x_ref in zip(ds, metas, xs):
        add_rows(d, meta, x_ref, hh_ref, hl_ref, w_ref)
    if last:
        for f in range(NC):
            hi, lo = split(w_ref[f])
            ww_ref[f, :, 0 : 2 * B] = hi
            ww_ref[f, :, 2 * B :] = lo


def gather(ds, metas, xs, hh, hl, w, last):
    first = w is None
    acc = (NC, B, 2 * B)
    return pl.pallas_call(
        functools.partial(gather_kernel, ds, first, last),
        out_shape=jax.ShapeDtypeStruct((NC, B, 4 * B), BF16)
        if last
        else jax.ShapeDtypeStruct(acc, F32),
        in_specs=smem(len(ds)) + vmem(len(ds) + 2 + (not first)),
        out_specs=pl.BlockSpec(memory_space=pltpu.VMEM),
        scratch_shapes=[pltpu.VMEM(acc, F32)] if last else [],
        compiler_params=PARAMS,
        name="gather_last" if last else "gather",
    )(*metas, *xs, hh, hl, *([] if first else [w]))


def spread_kernel(jobs, *refs):
    ks = sorted({k for k, _ in jobs})
    metas = dict(zip(ks, refs))
    zz_ref, ww_ref = refs[len(ks) : len(ks) + 2]
    outs, picked = refs[len(ks) + 2 : -1], refs[-1]
    for slot, ((k, ra), out) in enumerate(zip(jobs, outs)):
        a = 2 * k + ra
        for o in range(NO):
            picked[slot % 2, o * B : (o + 1) * B, :] = ww_ref[metas[k][2 + ra, o] + a]
        both = lax.dot_general(
            zz_ref[a],
            picked[slot % 2],
            (((1,), (1,)), ((), ())),
            preferred_element_type=F32,
        )
        out[...] = both[0:B] + both[B:]


def spread(jobs, metas, zz, ww):
    ks = sorted({k for k, _ in jobs})
    half = jax.ShapeDtypeStruct((B, NO * B), F32)
    return pl.pallas_call(
        functools.partial(spread_kernel, jobs),
        out_shape=(half,) * len(jobs),
        in_specs=smem(len(ks)) + vmem(2),
        out_specs=tuple(vmem(len(jobs))),
        scratch_shapes=[pltpu.VMEM((2, NO * B, 4 * B), BF16)],
        compiler_params=PARAMS,
        name="spread",
    )(*(metas[k] for k in ks), zz, ww)


def unpack_kernel(*refs):
    out_ref = refs[-1]
    for ra in range(2):
        total = refs[3 * ra][...] + refs[3 * ra + 1][...] + refs[3 * ra + 2][...]
        for o in range(NO):
            out_ref[ra, o] = total[:, o * B : (o + 1) * B]


def unpack(*parts):
    return pl.pallas_call(
        unpack_kernel,
        out_shape=jax.ShapeDtypeStruct((2, NO, B, B), F32),
        in_specs=vmem(6),
        out_specs=pl.BlockSpec(memory_space=pltpu.VMEM),
        compiler_params=PARAMS,
        name="unpack",
    )(*parts)


def local(h_blocks, h_cols, z_blocks, z_cols, out_cols):
    here = jnp.stack([lax.axis_index(AXES) * 2, jnp.int32(2 * lax.axis_size(AXES))])
    cols = jnp.concatenate([h_cols, z_cols, out_cols], axis=1)
    own, h_off, meta = pack(here, cols, z_blocks.reshape(NZ, 2 * B, B))
    up = {0: own}
    down = {0: own}
    for d in range(1, REACH):
        up[d] = shift(up[d - 1], -1)
        down[d] = shift(down[d - 1], 1)
    metas = {0: meta}

    def note(d):
        metas[d] = up[d][ZROWS:].astype(jnp.int32)
        metas[-d] = down[d][ZROWS:].astype(jnp.int32)

    for d in range(1, REACH):
        note(d)
    hh, hl, zz = prep(h_off, meta, h_blocks, z_blocks)

    def step(ds, w, last=False):
        xs = [up[d] if d >= 0 else down[-d] for d in ds]
        return gather(ds, [metas[d] for d in ds], xs, hh, hl, w, last)

    w = step((0,), None)
    w = step((1, -1), w)
    w = step((2, -2), w)
    w = step((3, -3), w)
    far_up, far_down, w = lax.optimization_barrier((up[8 - REACH], down[8 - REACH], w))
    up[REACH] = shift(far_down, -8)
    down[REACH] = shift(far_up, 8)
    note(REACH)
    w = step((4, -4), w)
    ww = step((5, -5), w, last=True)

    p40, p41, p51, p50 = spread(((4, 0), (4, 1), (5, 1), (5, 0)), metas, zz, ww)
    head = jnp.pad(up[REACH][ZROWS:], ((0, 0), (0, (NO - 2) * B)))
    back0 = shift(jnp.concatenate([p40, head], axis=0), -1)
    metas[LAST] = back0[B:, 0 : 2 * B].astype(jnp.int32)
    p31, p30, p20, p21, p11, p10, p00, p01 = spread(
        ((3, 1), (3, 0), (2, 0), (2, 1), (1, 1), (1, 0), (0, 0), (0, 1)), metas, zz, ww
    )
    p61, p60 = spread(((6, 1), (6, 0)), metas, zz, ww)
    if SPLIT:
        ahead1 = shift(p41, 1)
        back1 = shift(p51, -1)
        ahead0 = shift(p30, 1)
        ahead1 = shift(ahead1 + p31, 1)
        back0 = shift(back0[0:B] + p50, -1)
        back1 = shift(back1 + p61, LAST)
        ahead0 = shift(ahead0 + p20, 1)
        ahead1 = shift(ahead1 + p21, 1)
        back0 = shift(back0 + p60, LAST)
        ahead0 = shift(ahead0 + p10, 1)
        ahead1 = shift(ahead1 + p11, 1)
    else:
        ahead1 = shift(p41, 1)
        ahead = shift(jnp.concatenate([p30, p31 + ahead1]), 1)
        back = shift(jnp.concatenate([p50 + back0[0:B], p51]), -1)
        ahead = shift(ahead + jnp.concatenate([p20, p21]), 1)
        back = shift(back + jnp.concatenate([p60, p61]), LAST)
        ahead = shift(ahead + jnp.concatenate([p10, p11]), 1)
        ahead0, ahead1 = ahead[0:B], ahead[B:]
        back0, back1 = back[0:B], back[B:]
    return unpack(p00, ahead0, back0, p01, ahead1, back1)


def solution(mesh):
    rows = P(AXES, None)
    blocks = P(AXES, None, None, None)
    return jax.shard_map(
        local,
        mesh=mesh,
        in_specs=(blocks, rows, blocks, rows, rows),
        out_specs=blocks,
        check_vma=False,
    )
```

time: 825 us -> 162 us (0.20)
  the two profiles are of different devices: /device:TPU:69 before, /device:TPU:1 now
where the time goes in v1:
time: 162 us; the launch traced here: 161 us
  starting transfers between devices  87.7 us (54%)
  waiting for transfers between devices  53.4 us (33%)
  Pallas kernels  15.9 us (10%)
  local copies, waits for them, and re-layouts  2.53 us (2%)
    ppermute x17, starting transfers between devices, shift(): return lax.ppermute(x, AXES, [(i, (i + by) % size) for i in range(size)])  87.7 us
    ppermute x17, waiting for transfers between devices, shift(): return lax.ppermute(x, AXES, [(i, (i + by) % size) for i in range(size)])  53.4 us
    pallas_call x6, Pallas kernels, gather(): pl.pallas_call(functools.partial(gather_kernel, ds, first, last), out_sha...  7.63 us
    pallas_call x3, Pallas kernels, spread(): pl.pallas_call(functools.partial(spread_kernel, jobs), out_shape=(half,)...  4.82 us
  transfers between devices with their start and end apart: 17, of which 10 were waited for; matrix products, arithmetic and copies ran while one was open for 0% of the time, Pallas kernels for 6%

profile of v1, /device:TPU:1, one launch (start us, length us, event | category | flops | bytes accessed | tf_op | source)
XLA Modules:
  0.0 161.2 jit_solution(12281881341608345690)
XLA Ops:
  0.0 0.1 pad_add_fusion.1.here_ref
  0.1 0.8 pad_add_fusion.cols
  0.9 0.0 copy-start
  0.9 1.1 copy-done
  2.0 0.0 copy-start.1
  2.0 0.8 pack.1
  2.8 18.4 %collective-permute-start = (f32[776,128]{1,0:T(8,128)S(1)}, f32[776,128]{1,0:T(8,128)S(1)}, u32[]{:S(2)}, u32[]{:S(2)}) collective-permute-start(f32[776,128]{1,0:T(8,128)S(1)} %get-tuple-element.29.refs_1_), channel_id=1, source_target_pairs={{0,1023},{1,0},{2,1},{3,2},{4,3},{5,4},{6,5},{7,6},{8,7},{9,8},{10... | collective-permute-start | bytes 1191944 | tf_op jit(solution)/shard_map/ppermute | solution.py:38
  21.2 1.9 %collective-permute-start.3 = (f32[776,128]{1,0:T(8,128)S(1)}, f32[776,128]{1,0:T(8,128)S(1)}, u32[]{:S(2)}, u32[]{:S(2)}) collective-permute-start(f32[776,128]{1,0:T(8,128)S(1)} %get-tuple-element.29.refs_1_), channel_id=1, source_target_pairs={{0,1},{1,2},{2,3},{3,4},{4,5},{5,6},{6,7},{7,8},{8,9},{9,10},{10,1... | collective-permute-start | bytes 1191944 | tf_op jit(solution)/shard_map/ppermute | solution.py:38
  23.2 0.0 copy-done.1
  23.2 0.0 copy-start.2
  23.2 1.3 copy-done.2
  24.5 1.5 prep.1
  26.0 1.0 gather.5.refs_6_
  27.0 3.2 %collective-permute-done.refs_2_ = f32[776,128]{1,0:T(8,128)S(1)} collective-permute-done((f32[776,128]{1,0:T(8,128)S(1)}, f32[776,128]{1,0:T(8,128)S(1)}, u32[]{:S(2)}, u32[]{:S(2)}) %collective-permute-start) | collective-permute-done | bytes 397344 | tf_op jit(solution)/shard_map/ppermute | solution.py:38
  30.2 5.6 %collective-permute-start.1 = (f32[776,128]{1,0:T(8,128)S(1)}, f32[776,128]{1,0:T(8,128)S(1)}, u32[]{:S(2)}, u32[]{:S(2)}) collective-permute-start(f32[776,128]{1,0:T(8,128)S(1)} %collective-permute-done.refs_2_), channel_id=1, source_target_pairs={{0,1023},{1,0},{2,1},{3,2},{4,3},{5,4},{6,5},{7,6},{8,7},{9,8},{10... | collective-permute-start | bytes 1191944 | tf_op jit(solution)/shard_map/ppermute | solution.py:38
  35.8 0.0 collective-permute-done.3.refs_3_
  35.8 1.9 %collective-permute-start.4 = (f32[776,128]{1,0:T(8,128)S(1)}, f32[776,128]{1,0:T(8,128)S(1)}, u32[]{:S(2)}, u32[]{:S(2)}) collective-permute-start(f32[776,128]{1,0:T(8,128)S(1)} %collective-permute-done.3.refs_3_), channel_id=1, source_target_pairs={{0,1},{1,2},{2,3},{3,4},{4,5},{5,6},{6,7},{7,8},{8,9},{9,10},{10,1... | collective-permute-start | bytes 1191944 | tf_op jit(solution)/shard_map/ppermute | solution.py:38
  37.8 1.3 gather.6.refs_6_
  39.1 3.6 %collective-permute-done.1.refs_2_ = f32[776,128]{1,0:T(8,128)S(1)} collective-permute-done((f32[776,128]{1,0:T(8,128)S(1)}, f32[776,128]{1,0:T(8,128)S(1)}, u32[]{:S(2)}, u32[]{:S(2)}) %collective-permute-start.1) | collective-permute-done | bytes 397344 | tf_op jit(solution)/shard_map/ppermute | solution.py:38
  42.7 5.6 %collective-permute-start.2 = (f32[776,128]{1,0:T(8,128)S(1)}, f32[776,128]{1,0:T(8,128)S(1)}, u32[]{:S(2)}, u32[]{:S(2)}) collective-permute-start(f32[776,128]{1,0:T(8,128)S(1)} %collective-permute-done.1.refs_2_), channel_id=1, source_target_pairs={{0,1023},{1,0},{2,1},{3,2},{4,3},{5,4},{6,5},{7,6},{8,7},{9,8},{10... | collective-permute-start | bytes 1191944 | tf_op jit(solution)/shard_map/ppermute | solution.py:38
  48.3 0.0 collective-permute-done.4.refs_3_
  48.3 1.9 %collective-permute-start.5 = (f32[776,128]{1,0:T(8,128)S(1)}, f32[776,128]{1,0:T(8,128)S(1)}, u32[]{:S(2)}, u32[]{:S(2)}) collective-permute-start(f32[776,128]{1,0:T(8,128)S(1)} %collective-permute-done.4.refs_3_), channel_id=1, source_target_pairs={{0,1},{1,2},{2,3},{3,4},{4,5},{5,6},{6,7},{7,8},{8,9},{9,10},{10,1... | collective-permute-start | bytes 1191944 | tf_op jit(solution)/shard_map/ppermute | solution.py:38
  50.2 1.3 gather.7.refs_6_
  51.5 2.5 %collective-permute-done.2.refs_2_ = f32[776,128]{1,0:T(8,128)S(1)} collective-permute-done((f32[776,128]{1,0:T(8,128)S(1)}, f32[776,128]{1,0:T(8,128)S(1)}, u32[]{:S(2)}, u32[]{:S(2)}) %collective-permute-start.2) | collective-permute-done | bytes 397344 | tf_op jit(solution)/shard_map/ppermute | solution.py:38
  54.0 5.6 %collective-permute-start.8 = (f32[776,128]{1,0:T(8,128)S(1)}, f32[776,128]{1,0:T(8,128)S(1)}, u32[]{:S(2)}, u32[]{:S(2)}) collective-permute-start(f32[776,128]{1,0:T(8,128)S(1)} %collective-permute-done.2.refs_2_), channel_id=1, source_target_pairs={{0,1023},{1,0},{2,1},{3,2},{4,3},{5,4},{6,5},{7,6},{8,7},{9,8},{10... | collective-permute-start | bytes 1191944 | tf_op jit(solution)/shard_map/ppermute | solution.py:38
  59.6 0.5 collective-permute-done.5.refs_3_
  60.1 1.9 %collective-permute-start.9 = (f32[776,128]{1,0:T(8,128)S(1)}, f32[776,128]{1,0:T(8,128)S(1)}, u32[]{:S(2)}, u32[]{:S(2)}) collective-permute-start(f32[776,128]{1,0:T(8,128)S(1)} %collective-permute-done.5.refs_3_), channel_id=1, source_target_pairs={{0,1},{1,2},{2,3},{3,4},{4,5},{5,6},{6,7},{7,8},{8,9},{9,10},{10,1... | collective-permute-start | bytes 1191944 | tf_op jit(solution)/shard_map/ppermute | solution.py:38
  62.0 1.3 gather.8.refs_6_
  63.3 13.1 %collective-permute-start.6 = (f32[776,128]{1,0:T(8,128)S(1)}, f32[776,128]{1,0:T(8,128)S(1)}, u32[]{:S(2)}, u32[]{:S(2)}) collective-permute-start(f32[776,128]{1,0:T(8,128)S(1)} %collective-permute-done.5.refs_3_), channel_id=1, source_target_pairs={{0,1016},{1,1017},{2,1018},{3,1019},{4,1020},{5,1021},{6,1022},{7,... | collective-permute-start | bytes 1191944 | tf_op jit(solution)/shard_map/ppermute | solution.py:38
  76.4 1.9 %collective-permute-start.7 = (f32[776,128]{1,0:T(8,128)S(1)}, f32[776,128]{1,0:T(8,128)S(1)}, u32[]{:S(2)}, u32[]{:S(2)}) collective-permute-start(f32[776,128]{1,0:T(8,128)S(1)} %collective-permute-done.2.refs_2_), channel_id=1, source_target_pairs={{0,8},{1,9},{2,10},{3,11},{4,12},{5,13},{6,14},{7,15},{8,16},{9,17... | collective-permute-start | bytes 1191944 | tf_op jit(solution)/shard_map/ppermute | solution.py:38
  78.4 0.0 collective-permute-done.8.refs_2_
  78.4 0.0 collective-permute-done.9.refs_3_
  78.4 0.0 collective-permute-done.6.refs_2_
  78.4 4.7 %collective-permute-done.7.refs_3_ = f32[776,128]{1,0:T(8,128)S(1)} collective-permute-done((f32[776,128]{1,0:T(8,128)S(1)}, f32[776,128]{1,0:T(8,128)S(1)}, u32[]{:S(2)}, u32[]{:S(2)}) %collective-permute-start.7) | collective-permute-done | bytes 397344 | tf_op jit(solution)/shard_map/ppermute | solution.py:38
  83.1 1.3 gather.9.refs_6_
  84.4 1.5 gather_last.1.refs_5_.refs_3_.refs_2_
  85.9 1.5 spread.4
  87.3 1.9 %collective-permute-start.10 = (f32[64,1024]{1,0:T(8,128)S(1)}, f32[64,1024]{1,0:T(8,128)S(1)}, u32[]{:S(2)}, u32[]{:S(2)}) collective-permute-start(f32[64,1024]{1,0:T(8,128)S(1)} %get-tuple-element.40), channel_id=1, source_target_pairs={{0,1},{1,2},{2,3},{3,4},{4,5},{5,6},{6,7},{7,8},{8,9},{9,10},{10,1... | collective-permute-start | bytes 786440 | tf_op jit(solution)/shard_map/ppermute | solution.py:38
  89.3 15.0 %collective-permute-start.14 = (f32[72,1024]{1,0:T(8,128)S(1)}, f32[72,1024]{1,0:T(8,128)S(1)}, u32[]{:S(2)}, u32[]{:S(2)}) collective-permute-start(f32[72,1024]{1,0:T(8,128)S(1)} %select_maximum_fusion), channel_id=1, source_target_pairs={{0,1023},{1,0},{2,1},{3,2},{4,3},{5,4},{6,5},{7,6},{8,7},{9,8},{10... | collective-permute-start | bytes 884744 | tf_op jit(solution)/shard_map/ppermute | solution.py:38
  104.3 2.3 %spread.3 = (f32[64,1024]{1,0:T(8,128)S(1)}, f32[64,1024]{1,0:T(8,128)S(1)}, f32[64,1024]{1,0:T(8,128)S(1)}, f32[64,1024]{1,0:T(8,128)S(1)}, f32[64,1024]{1,0:T(...) custom-call(s32[8,128]{1,0:T(8,128)S(1)} %get-tuple-element.28.meta.refs_0_, ...), custom_call_target="tpu_custom_call" | custom-call | tf_op jit(solution)/shard_map/spread/pallas_call | solution.py:200
  106.6 1.8 %collective-permute-done.10 = f32[64,1024]{1,0:T(8,128)S(1)} collective-permute-done((f32[64,1024]{1,0:T(8,128)S(1)}, f32[64,1024]{1,0:T(8,128)S(1)}, u32[]{:S(2)}, u32[]{:S(2)}) %collective-permute-start.10) | collective-permute-done | bytes 262176 | tf_op jit(solution)/shard_map/ppermute | solution.py:38
  108.5 1.9 %collective-permute-start.11 = (f32[128,1024]{1,0:T(8,128)S(1)}, f32[128,1024]{1,0:T(8,128)S(1)}, u32[]{:S(2)}, u32[]{:S(2)}) collective-permute-start(f32[128,1024]{1,0:T(8,128)S(1)} %pad_maximum_fusion), channel_id=1, source_target_pairs={{0,1},{1,2},{2,3},{3,4},{4,5},{5,6},{6,7},{7,8},{8,9},{9,10},{10,1... | collective-permute-start | bytes 1572872 | tf_op jit(solution)/shard_map/ppermute | solution.py:38
  110.4 0.0 collective-permute-done.14
  110.5 5.2 %collective-permute-start.15 = (f32[128,1024]{1,0:T(8,128)S(1)}, f32[128,1024]{1,0:T(8,128)S(1)}, u32[]{:S(2)}, u32[]{:S(2)}) collective-permute-start(f32[128,1024]{1,0:T(8,128)S(1)} %pad_maximum_fusion.1), channel_id=1, source_target_pairs={{0,1023},{1,0},{2,1},{3,2},{4,3},{5,4},{6,5},{7,6},{8,7},{9,8},{10... | collective-permute-start | bytes 1572872 | tf_op jit(solution)/shard_map/ppermute | solution.py:38
  115.7 10.3 %collective-permute-done.11 = f32[128,1024]{1,0:T(8,128)S(1)} collective-permute-done((f32[128,1024]{1,0:T(8,128)S(1)}, f32[128,1024]{1,0:T(8,128)S(1)}, u32[]{:S(2)}, u32[]{:S(2)}) %collective-permute-start.11) | collective-permute-done | bytes 524320 | tf_op jit(solution)/shard_map/ppermute | solution.py:38
  126.1 0.1 maximum_add_fusion
  126.1 1.9 %collective-permute-start.12 = (f32[128,1024]{1,0:T(8,128)S(1)}, f32[128,1024]{1,0:T(8,128)S(1)}, u32[]{:S(2)}, u32[]{:S(2)}) collective-permute-start(f32[128,1024]{1,0:T(8,128)S(1)} %maximum_add_fusion), channel_id=1, source_target_pairs={{0,1},{1,2},{2,3},{3,4},{4,5},{5,6},{6,7},{7,8},{8,9},{9,10},{10,1... | collective-permute-start | bytes 1572872 | tf_op jit(solution)/shard_map/ppermute | solution.py:38
  128.1 1.1 spread.5
  129.2 0.0 collective-permute-done.15
  129.2 0.1 maximum_add_fusion.2
  129.2 1.9 %collective-permute-start.16 = (f32[128,1024]{1,0:T(8,128)S(1)}, f32[128,1024]{1,0:T(8,128)S(1)}, u32[]{:S(2)}, u32[]{:S(2)}) collective-permute-start(f32[128,1024]{1,0:T(8,128)S(1)} %maximum_add_fusion.2), channel_id=1, source_target_pairs={{0,6},{1,7},{2,8},{3,9},{4,10},{5,11},{6,12},{7,13},{8,14},{9,15},... | collective-permute-start | bytes 1572872 | tf_op jit(solution)/shard_map/ppermute | solution.py:38
  131.2 12.3 %collective-permute-done.12 = f32[128,1024]{1,0:T(8,128)S(1)} collective-permute-done((f32[128,1024]{1,0:T(8,128)S(1)}, f32[128,1024]{1,0:T(8,128)S(1)}, u32[]{:S(2)}, u32[]{:S(2)}) %collective-permute-start.12) | collective-permute-done | bytes 524320 | tf_op jit(solution)/shard_map/ppermute | solution.py:38
  143.5 0.1 maximum_add_fusion.1
  143.5 1.9 %collective-permute-start.13 = (f32[128,1024]{1,0:T(8,128)S(1)}, f32[128,1024]{1,0:T(8,128)S(1)}, u32[]{:S(2)}, u32[]{:S(2)}) collective-permute-start(f32[128,1024]{1,0:T(8,128)S(1)} %maximum_add_fusion.1), channel_id=1, source_target_pairs={{0,1},{1,2},{2,3},{3,4},{4,5},{5,6},{6,7},{7,8},{8,9},{9,10},{10,1... | collective-permute-start | bytes 1572872 | tf_op jit(solution)/shard_map/ppermute | solution.py:38
  145.5 10.2 %collective-permute-done.16 = f32[128,1024]{1,0:T(8,128)S(1)} collective-permute-done((f32[128,1024]{1,0:T(8,128)S(1)}, f32[128,1024]{1,0:T(8,128)S(1)}, u32[]{:S(2)}, u32[]{:S(2)}) %collective-permute-start.16) | collective-permute-done | bytes 524320 | tf_op jit(solution)/shard_map/ppermute | solution.py:38
  155.8 4.2 %collective-permute-done.13 = f32[128,1024]{1,0:T(8,128)S(1)} collective-permute-done((f32[128,1024]{1,0:T(8,128)S(1)}, f32[128,1024]{1,0:T(8,128)S(1)}, u32[]{:S(2)}, u32[]{:S(2)}) %collective-permute-start.13) | collective-permute-done | bytes 524320 | tf_op jit(solution)/shard_map/ppermute | solution.py:38
  160.0 1.2 unpack.1
  (18 shorter events, 0.3 us)
Async XLA Ops:
  0.9 1.1 copy-start
  2.0 21.2 %copy-start.1 = (f32[2,12,64,64]{3,2,1,0:T(8,128)S(1)}, f32[2,12,64,64]{3,2,1,0:T(8,128)}, u32[]{:S(2)}) copy-start(f32[2,12,64,64]{3,2,1,0:T(8,128)} %z_ref.1) | copy-start | bytes 1179652
  2.8 27.4 %collective-permute-start = (f32[776,128]{1,0:T(8,128)S(1)}, f32[776,128]{1,0:T(8,128)S(1)}, u32[]{:S(2)}, u32[]{:S(2)}) collective-permute-start(f32[776,128]{1,0:T(8,128)S(1)} %get-tuple-element.29.refs_1_), channel_id=1, source_target_pairs={{0,1023},{1,0},{2,1},{3,2},{4,3},{5,4},{6,5},{7,6},{8,7},{9,8},{10... | collective-permute-start | bytes 1191944 | tf_op jit(solution)/shard_map/ppermute | solution.py:38
  21.2 14.6 %collective-permute-start.3 = (f32[776,128]{1,0:T(8,128)S(1)}, f32[776,128]{1,0:T(8,128)S(1)}, u32[]{:S(2)}, u32[]{:S(2)}) collective-permute-start(f32[776,128]{1,0:T(8,128)S(1)} %get-tuple-element.29.refs_1_), channel_id=1, source_target_pairs={{0,1},{1,2},{2,3},{3,4},{4,5},{5,6},{6,7},{7,8},{8,9},{9,10},{10,1... | collective-permute-start | bytes 1191944 | tf_op jit(solution)/shard_map/ppermute | solution.py:38
  23.2 1.3 copy-start.2
  30.2 12.4 %collective-permute-start.1 = (f32[776,128]{1,0:T(8,128)S(1)}, f32[776,128]{1,0:T(8,128)S(1)}, u32[]{:S(2)}, u32[]{:S(2)}) collective-permute-start(f32[776,128]{1,0:T(8,128)S(1)} %collective-permute-done.refs_2_), channel_id=1, source_target_pairs={{0,1023},{1,0},{2,1},{3,2},{4,3},{5,4},{6,5},{7,6},{8,7},{9,8},{10... | collective-permute-start | bytes 1191944 | tf_op jit(solution)/shard_map/ppermute | solution.py:38
  35.8 12.4 %collective-permute-start.4 = (f32[776,128]{1,0:T(8,128)S(1)}, f32[776,128]{1,0:T(8,128)S(1)}, u32[]{:S(2)}, u32[]{:S(2)}) collective-permute-start(f32[776,128]{1,0:T(8,128)S(1)} %collective-permute-done.3.refs_3_), channel_id=1, source_target_pairs={{0,1},{1,2},{2,3},{3,4},{4,5},{5,6},{6,7},{7,8},{8,9},{9,10},{10,1... | collective-permute-start | bytes 1191944 | tf_op jit(solution)/shard_map/ppermute | solution.py:38
  42.7 11.3 %collective-permute-start.2 = (f32[776,128]{1,0:T(8,128)S(1)}, f32[776,128]{1,0:T(8,128)S(1)}, u32[]{:S(2)}, u32[]{:S(2)}) collective-permute-start(f32[776,128]{1,0:T(8,128)S(1)} %collective-permute-done.1.refs_2_), channel_id=1, source_target_pairs={{0,1023},{1,0},{2,1},{3,2},{4,3},{5,4},{6,5},{7,6},{8,7},{9,8},{10... | collective-permute-start | bytes 1191944 | tf_op jit(solution)/shard_map/ppermute | solution.py:38
  48.3 11.8 %collective-permute-start.5 = (f32[776,128]{1,0:T(8,128)S(1)}, f32[776,128]{1,0:T(8,128)S(1)}, u32[]{:S(2)}, u32[]{:S(2)}) collective-permute-start(f32[776,128]{1,0:T(8,128)S(1)} %collective-permute-done.4.refs_3_), channel_id=1, source_target_pairs={{0,1},{1,2},{2,3},{3,4},{4,5},{5,6},{6,7},{7,8},{8,9},{9,10},{10,1... | collective-permute-start | bytes 1191944 | tf_op jit(solution)/shard_map/ppermute | solution.py:38
  54.0 24.3 %collective-permute-start.8 = (f32[776,128]{1,0:T(8,128)S(1)}, f32[776,128]{1,0:T(8,128)S(1)}, u32[]{:S(2)}, u32[]{:S(2)}) collective-permute-start(f32[776,128]{1,0:T(8,128)S(1)} %collective-permute-done.2.refs_2_), channel_id=1, source_target_pairs={{0,1023},{1,0},{2,1},{3,2},{4,3},{5,4},{6,5},{7,6},{8,7},{9,8},{10... | collective-permute-start | bytes 1191944 | tf_op jit(solution)/shard_map/ppermute | solution.py:38
  60.1 18.3 %collective-permute-start.9 = (f32[776,128]{1,0:T(8,128)S(1)}, f32[776,128]{1,0:T(8,128)S(1)}, u32[]{:S(2)}, u32[]{:S(2)}) collective-permute-start(f32[776,128]{1,0:T(8,128)S(1)} %collective-permute-done.5.refs_3_), channel_id=1, source_target_pairs={{0,1},{1,2},{2,3},{3,4},{4,5},{5,6},{6,7},{7,8},{8,9},{9,10},{10,1... | collective-permute-start | bytes 1191944 | tf_op jit(solution)/shard_map/ppermute | solution.py:38
  63.3 15.1 %collective-permute-start.6 = (f32[776,128]{1,0:T(8,128)S(1)}, f32[776,128]{1,0:T(8,128)S(1)}, u32[]{:S(2)}, u32[]{:S(2)}) collective-permute-start(f32[776,128]{1,0:T(8,128)S(1)} %collective-permute-done.5.refs_3_), channel_id=1, source_target_pairs={{0,1016},{1,1017},{2,1018},{3,1019},{4,1020},{5,1021},{6,1022},{7,... | collective-permute-start | bytes 1191944 | tf_op jit(solution)/shard_map/ppermute | solution.py:38
  76.4 6.7 %collective-permute-start.7 = (f32[776,128]{1,0:T(8,128)S(1)}, f32[776,128]{1,0:T(8,128)S(1)}, u32[]{:S(2)}, u32[]{:S(2)}) collective-permute-start(f32[776,128]{1,0:T(8,128)S(1)} %collective-permute-done.2.refs_2_), channel_id=1, source_target_pairs={{0,8},{1,9},{2,10},{3,11},{4,12},{5,13},{6,14},{7,15},{8,16},{9,17... | collective-permute-start | bytes 1191944 | tf_op jit(solution)/shard_map/ppermute | solution.py:38
  87.3 21.0 %collective-permute-start.10 = (f32[64,1024]{1,0:T(8,128)S(1)}, f32[64,1024]{1,0:T(8,128)S(1)}, u32[]{:S(2)}, u32[]{:S(2)}) collective-permute-start(f32[64,1024]{1,0:T(8,128)S(1)} %get-tuple-element.40), channel_id=1, source_target_pairs={{0,1},{1,2},{2,3},{3,4},{4,5},{5,6},{6,7},{7,8},{8,9},{9,10},{10,1... | collective-permute-start | bytes 786440 | tf_op jit(solution)/shard_map/ppermute | solution.py:38
  89.3 21.1 %collective-permute-start.14 = (f32[72,1024]{1,0:T(8,128)S(1)}, f32[72,1024]{1,0:T(8,128)S(1)}, u32[]{:S(2)}, u32[]{:S(2)}) collective-permute-start(f32[72,1024]{1,0:T(8,128)S(1)} %select_maximum_fusion), channel_id=1, source_target_pairs={{0,1023},{1,0},{2,1},{3,2},{4,3},{5,4},{6,5},{7,6},{8,7},{9,8},{10... | collective-permute-start | bytes 884744 | tf_op jit(solution)/shard_map/ppermute | solution.py:38
  108.5 17.6 %collective-permute-start.11 = (f32[128,1024]{1,0:T(8,128)S(1)}, f32[128,1024]{1,0:T(8,128)S(1)}, u32[]{:S(2)}, u32[]{:S(2)}) collective-permute-start(f32[128,1024]{1,0:T(8,128)S(1)} %pad_maximum_fusion), channel_id=1, source_target_pairs={{0,1},{1,2},{2,3},{3,4},{4,5},{5,6},{6,7},{7,8},{8,9},{9,10},{10,1... | collective-permute-start | bytes 1572872 | tf_op jit(solution)/shard_map/ppermute | solution.py:38
  110.5 18.7 %collective-permute-start.15 = (f32[128,1024]{1,0:T(8,128)S(1)}, f32[128,1024]{1,0:T(8,128)S(1)}, u32[]{:S(2)}, u32[]{:S(2)}) collective-permute-start(f32[128,1024]{1,0:T(8,128)S(1)} %pad_maximum_fusion.1), channel_id=1, source_target_pairs={{0,1023},{1,0},{2,1},{3,2},{4,3},{5,4},{6,5},{7,6},{8,7},{9,8},{10... | collective-permute-start | bytes 1572872 | tf_op jit(solution)/shard_map/ppermute | solution.py:38
  126.1 17.3 %collective-permute-start.12 = (f32[128,1024]{1,0:T(8,128)S(1)}, f32[128,1024]{1,0:T(8,128)S(1)}, u32[]{:S(2)}, u32[]{:S(2)}) collective-permute-start(f32[128,1024]{1,0:T(8,128)S(1)} %maximum_add_fusion), channel_id=1, source_target_pairs={{0,1},{1,2},{2,3},{3,4},{4,5},{5,6},{6,7},{7,8},{8,9},{9,10},{10,1... | collective-permute-start | bytes 1572872 | tf_op jit(solution)/shard_map/ppermute | solution.py:38
  129.2 26.5 %collective-permute-start.16 = (f32[128,1024]{1,0:T(8,128)S(1)}, f32[128,1024]{1,0:T(8,128)S(1)}, u32[]{:S(2)}, u32[]{:S(2)}) collective-permute-start(f32[128,1024]{1,0:T(8,128)S(1)} %maximum_add_fusion.2), channel_id=1, source_target_pairs={{0,6},{1,7},{2,8},{3,9},{4,10},{5,11},{6,12},{7,13},{8,14},{9,15},... | collective-permute-start | bytes 1572872 | tf_op jit(solution)/shard_map/ppermute | solution.py:38
  143.5 16.5 %collective-permute-start.13 = (f32[128,1024]{1,0:T(8,128)S(1)}, f32[128,1024]{1,0:T(8,128)S(1)}, u32[]{:S(2)}, u32[]{:S(2)}) collective-permute-start(f32[128,1024]{1,0:T(8,128)S(1)} %maximum_add_fusion.1), channel_id=1, source_target_pairs={{0,1},{1,2},{2,3},{3,4},{4,5},{5,6},{6,7},{7,8},{8,9},{9,10},{10,1... | collective-permute-start | bytes 1572872 | tf_op jit(solution)/shard_map/ppermute | solution.py:38

commit v2 on v1

--- a/solution.py
+++ b/solution.py
@@ -21,7 +21,6 @@
 NA = 2 * (LAST + 1)
 HALF = NZ // 2 * B
 ZROWS = 2 * HALF
-SPLIT = False
 F32 = jnp.float32
 BF16 = jnp.bfloat16
 
@@ -237,13 +236,20 @@
         up[d] = shift(up[d - 1], -1)
         down[d] = shift(down[d - 1], 1)
     metas = {0: meta}
+    down[REACH] = shift(up[8 - REACH], 8)
+    far = jnp.concatenate(
+        [down[8 - REACH][0 : ZROWS + 4], down[8 - LAST][ZROWS : ZROWS + 4]], axis=0
+    )
+    up[REACH] = shift(far, -8)
+    down[REACH], up[REACH] = lax.optimization_barrier((down[REACH], up[REACH]))
 
     def note(d):
         metas[d] = up[d][ZROWS:].astype(jnp.int32)
         metas[-d] = down[d][ZROWS:].astype(jnp.int32)
 
-    for d in range(1, REACH):
+    for d in range(1, REACH + 1):
         note(d)
+    metas[LAST] = up[REACH][ZROWS + 4 :].astype(jnp.int32)
     hh, hl, zz = prep(h_off, meta, h_blocks, z_blocks)
 
     def step(ds, w, last=False):
@@ -254,42 +260,28 @@
     w = step((1, -1), w)
     w = step((2, -2), w)
     w = step((3, -3), w)
-    far_up, far_down, w = lax.optimization_barrier((up[8 - REACH], down[8 - REACH], w))
-    up[REACH] = shift(far_down, -8)
-    down[REACH] = shift(far_up, 8)
-    note(REACH)
     w = step((4, -4), w)
     ww = step((5, -5), w, last=True)
 
-    p40, p41, p51, p50 = spread(((4, 0), (4, 1), (5, 1), (5, 0)), metas, zz, ww)
-    head = jnp.pad(up[REACH][ZROWS:], ((0, 0), (0, (NO - 2) * B)))
-    back0 = shift(jnp.concatenate([p40, head], axis=0), -1)
-    metas[LAST] = back0[B:, 0 : 2 * B].astype(jnp.int32)
-    p31, p30, p20, p21, p11, p10, p00, p01 = spread(
-        ((3, 1), (3, 0), (2, 0), (2, 1), (1, 1), (1, 0), (0, 0), (0, 1)), metas, zz, ww
+    def parts(*jobs):
+        return spread(jobs, metas, zz, ww)
+
+    p50, p51 = parts((5, 0), (5, 1))
+    back = shift(jnp.concatenate([p50, p51], axis=0), -1)
+    p41, p40 = parts((4, 1), (4, 0))
+    ahead1 = shift(p41, 1)
+    ahead0 = shift(p40, 1)
+    p31, p30, p60, p61, p21, p20, p11, p10, p00, p01 = parts(
+        (3, 1), (3, 0), (6, 0), (6, 1), (2, 1), (2, 0), (1, 1), (1, 0), (0, 0), (0, 1)
     )
-    p61, p60 = spread(((6, 1), (6, 0)), metas, zz, ww)
-    if SPLIT:
-        ahead1 = shift(p41, 1)
-        back1 = shift(p51, -1)
-        ahead0 = shift(p30, 1)
-        ahead1 = shift(ahead1 + p31, 1)
-        back0 = shift(back0[0:B] + p50, -1)
-        back1 = shift(back1 + p61, LAST)
-        ahead0 = shift(ahead0 + p20, 1)
-        ahead1 = shift(ahead1 + p21, 1)
-        back0 = shift(back0 + p60, LAST)
-        ahead0 = shift(ahead0 + p10, 1)
-        ahead1 = shift(ahead1 + p11, 1)
-    else:
-        ahead1 = shift(p41, 1)
-        ahead = shift(jnp.concatenate([p30, p31 + ahead1]), 1)
-        back = shift(jnp.concatenate([p50 + back0[0:B], p51]), -1)
-        ahead = shift(ahead + jnp.concatenate([p20, p21]), 1)
-        back = shift(back + jnp.concatenate([p60, p61]), LAST)
-        ahead = shift(ahead + jnp.concatenate([p10, p11]), 1)
-        ahead0, ahead1 = ahead[0:B], ahead[B:]
-        back0, back1 = back[0:B], back[B:]
+    ahead1 = shift(ahead1 + p31, 1)
+    ahead0 = shift(ahead0 + p30, 1)
+    back = shift(back + jnp.concatenate([p60, p61], axis=0), LAST)
+    ahead1 = shift(ahead1 + p21, 1)
+    ahead0 = shift(ahead0 + p20, 1)
+    ahead1 = shift(ahead1 + p11, 1)
+    ahead0 = shift(ahead0 + p10, 1)
+    back0, back1 = back[0:B], back[B:]
     return unpack(p00, ahead0, back0, p01, ahead1, back1)
 
 

time: 162 us -> 151 us (0.932)
  the two profiles are of different devices: /device:TPU:1 before, /device:TPU:8 now
where the time goes in v2:
time: 151 us; the launch traced here: 150 us
  starting transfers between devices  80.3 us (53%)
  waiting for transfers between devices  49.5 us (33%)
  Pallas kernels  15.9 us (11%)
  local copies, waits for them, and re-layouts  2.49 us (2%)
    ppermute x20, starting transfers between devices, shift(): return lax.ppermute(x, AXES, [(i, (i + by) % size) for i in range(size)])  80.3 us
    ppermute x20, waiting for transfers between devices, shift(): return lax.ppermute(x, AXES, [(i, (i + by) % size) for i in range(size)])  49.5 us
    pallas_call x6, Pallas kernels, gather(): pl.pallas_call(functools.partial(gather_kernel, ds, first, last), out_sha...  7.65 us
    pallas_call x3, Pallas kernels, spread(): pl.pallas_call(functools.partial(spread_kernel, jobs), out_shape=(half,)...  4.81 us
  transfers between devices with their start and end apart: 20, of which 11 were waited for; matrix products, arithmetic and copies ran while one was open for 0% of the time, Pallas kernels for 7%

profile of v2, /device:TPU:8, one launch (start us, length us, event | category | flops | bytes accessed | tf_op | source)
XLA Modules:
  0.0 150.0 jit_solution(8398094937507873878)
XLA Ops:
  0.0 0.1 pad_add_fusion.1.here_ref
  0.1 0.8 pad_add_fusion.cols
  0.9 0.0 copy-start
  0.9 1.1 copy-done
  2.0 0.0 copy-start.1
  2.0 0.8 pack.1
  2.8 5.2 %collective-permute-start.4 = (f32[776,128]{1,0:T(8,128)S(1)}, f32[776,128]{1,0:T(8,128)S(1)}, u32[]{:S(2)}, u32[]{:S(2)}) collective-permute-start(f32[776,128]{1,0:T(8,128)S(1)} %get-tuple-element.28.refs_1_), channel_id=1, source_target_pairs={{0,1},{1,2},{2,3},{3,4},{4,5},{5,6},{6,7},{7,8},{8,9},{9,10},{10,1... | collective-permute-start | bytes 1191944 | tf_op jit(solution)/shard_map/ppermute | solution.py:37
  8.0 17.2 %collective-permute-start = (f32[776,128]{1,0:T(8,128)S(1)}, f32[776,128]{1,0:T(8,128)S(1)}, u32[]{:S(2)}, u32[]{:S(2)}) collective-permute-start(f32[776,128]{1,0:T(8,128)S(1)} %get-tuple-element.28.refs_1_), channel_id=1, source_target_pairs={{0,1023},{1,0},{2,1},{3,2},{4,3},{5,4},{6,5},{7,6},{8,7},{9,8},{10... | collective-permute-start | bytes 1191944 | tf_op jit(solution)/shard_map/ppermute | solution.py:37
  25.2 0.0 copy-done.1
  25.2 0.0 copy-start.2
  25.2 1.3 copy-done.2
  26.5 1.5 prep.1
  28.0 1.0 gather.5.refs_6_
  29.0 0.0 collective-permute-done.4.refs_3_
  29.0 1.9 %collective-permute-start.5 = (f32[776,128]{1,0:T(8,128)S(1)}, f32[776,128]{1,0:T(8,128)S(1)}, u32[]{:S(2)}, u32[]{:S(2)}) collective-permute-start(f32[776,128]{1,0:T(8,128)S(1)} %collective-permute-done.4.refs_3_), channel_id=1, source_target_pairs={{0,1},{1,2},{2,3},{3,4},{4,5},{5,6},{6,7},{7,8},{8,9},{9,10},{10,1... | collective-permute-start | bytes 1191944 | tf_op jit(solution)/shard_map/ppermute | solution.py:37
  30.9 0.0 collective-permute-done.refs_2_
  31.0 9.1 %collective-permute-start.1 = (f32[776,128]{1,0:T(8,128)S(1)}, f32[776,128]{1,0:T(8,128)S(1)}, u32[]{:S(2)}, u32[]{:S(2)}) collective-permute-start(f32[776,128]{1,0:T(8,128)S(1)} %collective-permute-done.refs_2_), channel_id=1, source_target_pairs={{0,1023},{1,0},{2,1},{3,2},{4,3},{5,4},{6,5},{7,6},{8,7},{9,8},{10... | collective-permute-start | bytes 1191944 | tf_op jit(solution)/shard_map/ppermute | solution.py:37
  40.1 1.3 gather.6.refs_6_
  41.4 2.3 %collective-permute-done.5.refs_3_ = f32[776,128]{1,0:T(8,128)S(1)} collective-permute-done((f32[776,128]{1,0:T(8,128)S(1)}, f32[776,128]{1,0:T(8,128)S(1)}, u32[]{:S(2)}, u32[]{:S(2)}) %collective-permute-start.5) | collective-permute-done | bytes 397344 | tf_op jit(solution)/shard_map/ppermute | solution.py:37
  43.7 1.9 %collective-permute-start.6 = (f32[776,128]{1,0:T(8,128)S(1)}, f32[776,128]{1,0:T(8,128)S(1)}, u32[]{:S(2)}, u32[]{:S(2)}) collective-permute-start(f32[776,128]{1,0:T(8,128)S(1)} %collective-permute-done.5.refs_3_), channel_id=1, source_target_pairs={{0,1},{1,2},{2,3},{3,4},{4,5},{5,6},{6,7},{7,8},{8,9},{9,10},{10,1... | collective-permute-start | bytes 1191944 | tf_op jit(solution)/shard_map/ppermute | solution.py:37
  45.6 0.0 collective-permute-done.1.refs_2_
  45.6 9.1 %collective-permute-start.2 = (f32[776,128]{1,0:T(8,128)S(1)}, f32[776,128]{1,0:T(8,128)S(1)}, u32[]{:S(2)}, u32[]{:S(2)}) collective-permute-start(f32[776,128]{1,0:T(8,128)S(1)} %collective-permute-done.1.refs_2_), channel_id=1, source_target_pairs={{0,1023},{1,0},{2,1},{3,2},{4,3},{5,4},{6,5},{7,6},{8,7},{9,8},{10... | collective-permute-start | bytes 1191944 | tf_op jit(solution)/shard_map/ppermute | solution.py:37
  54.7 1.3 gather.7.refs_6_
  56.0 2.3 %collective-permute-done.6.refs_3_ = f32[776,128]{1,0:T(8,128)S(1)} collective-permute-done((f32[776,128]{1,0:T(8,128)S(1)}, f32[776,128]{1,0:T(8,128)S(1)}, u32[]{:S(2)}, u32[]{:S(2)}) %collective-permute-start.6) | collective-permute-done | bytes 397344 | tf_op jit(solution)/shard_map/ppermute | solution.py:37
  58.4 1.9 %collective-permute-start.7 = (f32[776,128]{1,0:T(8,128)S(1)}, f32[776,128]{1,0:T(8,128)S(1)}, u32[]{:S(2)}, u32[]{:S(2)}) collective-permute-start(f32[776,128]{1,0:T(8,128)S(1)} %pad_maximum_fusion.1), channel_id=1, source_target_pairs={{0,1016},{1,1017},{2,1018},{3,1019},{4,1020},{5,1021},{6,1022},{7,... | collective-permute-start | bytes 1191944 | tf_op jit(solution)/shard_map/ppermute | solution.py:37
  60.3 1.9 %collective-permute-start.9 = (f32[776,128]{1,0:T(8,128)S(1)}, f32[776,128]{1,0:T(8,128)S(1)}, u32[]{:S(2)}, u32[]{:S(2)}) collective-permute-start(f32[776,128]{1,0:T(8,128)S(1)} %collective-permute-done.6.refs_3_), channel_id=1, source_target_pairs={{0,1},{1,2},{2,3},{3,4},{4,5},{5,6},{6,7},{7,8},{8,9},{9,10},{10,1... | collective-permute-start | bytes 1191944 | tf_op jit(solution)/shard_map/ppermute | solution.py:37
  62.2 0.0 collective-permute-done.2.refs_2_
  62.3 9.1 %collective-permute-start.8 = (f32[776,128]{1,0:T(8,128)S(1)}, f32[776,128]{1,0:T(8,128)S(1)}, u32[]{:S(2)}, u32[]{:S(2)}) collective-permute-start(f32[776,128]{1,0:T(8,128)S(1)} %collective-permute-done.2.refs_2_), channel_id=1, source_target_pairs={{0,1023},{1,0},{2,1},{3,2},{4,3},{5,4},{6,5},{7,6},{8,7},{9,8},{10... | collective-permute-start | bytes 1191944 | tf_op jit(solution)/shard_map/ppermute | solution.py:37
  71.3 1.9 %collective-permute-start.3 = (f32[776,128]{1,0:T(8,128)S(1)}, f32[776,128]{1,0:T(8,128)S(1)}, u32[]{:S(2)}, u32[]{:S(2)}) collective-permute-start(f32[776,128]{1,0:T(8,128)S(1)} %collective-permute-done.2.refs_2_), channel_id=1, source_target_pairs={{0,8},{1,9},{2,10},{3,11},{4,12},{5,13},{6,14},{7,15},{8,16},{9,17... | collective-permute-start | bytes 1191944 | tf_op jit(solution)/shard_map/ppermute | solution.py:37
  73.3 1.3 gather.8.refs_6_
  74.6 0.0 collective-permute-done.7.refs_2_
  74.6 9.2 %collective-permute-done.3.refs_3_ = f32[776,128]{1,0:T(8,128)S(1)} collective-permute-done((f32[776,128]{1,0:T(8,128)S(1)}, f32[776,128]{1,0:T(8,128)S(1)}, u32[]{:S(2)}, u32[]{:S(2)}) %collective-permute-start.3) | collective-permute-done | bytes 397344 | tf_op jit(solution)/shard_map/ppermute | solution.py:37
  83.8 0.0 collective-permute-done.9.refs_3_
  83.8 0.0 collective-permute-done.8.refs_2_
  83.8 1.3 gather.9.refs_6_
  85.1 1.5 gather_last.1.refs_6_.refs_2_
  86.6 1.1 spread.5
  87.7 2.1 %collective-permute-start.14 = (f32[128,1024]{1,0:T(8,128)S(1)}, f32[128,1024]{1,0:T(8,128)S(1)}, u32[]{:S(2)}, u32[]{:S(2)}) collective-permute-start(f32[128,1024]{1,0:T(8,128)S(1)} %pad_maximum_fusion), channel_id=1, source_target_pairs={{0,1023},{1,0},{2,1},{3,2},{4,3},{5,4},{6,5},{7,6},{8,7},{9,8},{10... | collective-permute-start | bytes 1572872 | tf_op jit(solution)/shard_map/ppermute | solution.py:37
  89.8 1.1 spread.4
  90.9 3.8 %collective-permute-start.16 = (f32[64,1024]{1,0:T(8,128)S(1)}, f32[64,1024]{1,0:T(8,128)S(1)}, u32[]{:S(2)}, u32[]{:S(2)}) collective-permute-start(f32[64,1024]{1,0:T(8,128)S(1)} %get-tuple-element.45), channel_id=1, source_target_pairs={{0,1},{1,2},{2,3},{3,4},{4,5},{5,6},{6,7},{7,8},{8,9},{9,10},{10,1... | collective-permute-start | bytes 786440 | tf_op jit(solution)/shard_map/ppermute | solution.py:37
  94.7 1.9 %collective-permute-start.10 = (f32[64,1024]{1,0:T(8,128)S(1)}, f32[64,1024]{1,0:T(8,128)S(1)}, u32[]{:S(2)}, u32[]{:S(2)}) collective-permute-start(f32[64,1024]{1,0:T(8,128)S(1)} %get-tuple-element.36), channel_id=1, source_target_pairs={{0,1},{1,2},{2,3},{3,4},{4,5},{5,6},{6,7},{7,8},{8,9},{9,10},{10,1... | collective-permute-start | bytes 786440 | tf_op jit(solution)/shard_map/ppermute | solution.py:37
  96.6 2.7 %spread.3 = (f32[64,1024]{1,0:T(8,128)S(1)}, f32[64,1024]{1,0:T(8,128)S(1)}, f32[64,1024]{1,0:T(8,128)S(1)}, f32[64,1024]{1,0:T(8,128)S(1)}, f32[64,1024]{1,0:T(...) custom-call(s32[8,128]{1,0:T(8,128)S(1)} %get-tuple-element.27.meta., ...), custom_call_target="tpu_custom_call" | custom-call | tf_op jit(solution)/shard_map/spread/pallas_call | solution.py:199
  99.3 4.8 %collective-permute-done.16 = f32[64,1024]{1,0:T(8,128)S(1)} collective-permute-done((f32[64,1024]{1,0:T(8,128)S(1)}, f32[64,1024]{1,0:T(8,128)S(1)}, u32[]{:S(2)}, u32[]{:S(2)}) %collective-permute-start.16) | collective-permute-done | bytes 262176 | tf_op jit(solution)/shard_map/ppermute | solution.py:37
  104.2 1.9 %collective-permute-start.17 = (f32[64,1024]{1,0:T(8,128)S(1)}, f32[64,1024]{1,0:T(8,128)S(1)}, u32[]{:S(2)}, u32[]{:S(2)}) collective-permute-start(f32[64,1024]{1,0:T(8,128)S(1)} %add.33), channel_id=1, source_target_pairs={{0,1},{1,2},{2,3},{3,4},{4,5},{5,6},{6,7},{7,8},{8,9},{9,10},{10,1... | collective-permute-start | bytes 786440 | tf_op jit(solution)/shard_map/ppermute | solution.py:37
  106.1 1.8 %collective-permute-done.10 = f32[64,1024]{1,0:T(8,128)S(1)} collective-permute-done((f32[64,1024]{1,0:T(8,128)S(1)}, f32[64,1024]{1,0:T(8,128)S(1)}, u32[]{:S(2)}, u32[]{:S(2)}) %collective-permute-start.10) | collective-permute-done | bytes 262176 | tf_op jit(solution)/shard_map/ppermute | solution.py:37
  107.9 1.9 %collective-permute-start.11 = (f32[64,1024]{1,0:T(8,128)S(1)}, f32[64,1024]{1,0:T(8,128)S(1)}, u32[]{:S(2)}, u32[]{:S(2)}) collective-permute-start(f32[64,1024]{1,0:T(8,128)S(1)} %add.29), channel_id=1, source_target_pairs={{0,1},{1,2},{2,3},{3,4},{4,5},{5,6},{6,7},{7,8},{8,9},{9,10},{10,1... | collective-permute-start | bytes 786440 | tf_op jit(solution)/shard_map/ppermute | solution.py:37
  109.8 0.0 collective-permute-done.14
  109.8 0.1 maximum_add_fusion
  109.9 1.9 %collective-permute-start.15 = (f32[128,1024]{1,0:T(8,128)S(1)}, f32[128,1024]{1,0:T(8,128)S(1)}, u32[]{:S(2)}, u32[]{:S(2)}) collective-permute-start(f32[128,1024]{1,0:T(8,128)S(1)} %maximum_add_fusion), channel_id=1, source_target_pairs={{0,6},{1,7},{2,8},{3,9},{4,10},{5,11},{6,12},{7,13},{8,14},{9,15},... | collective-permute-start | bytes 1572872 | tf_op jit(solution)/shard_map/ppermute | solution.py:37
  111.8 5.5 %collective-permute-done.17 = f32[64,1024]{1,0:T(8,128)S(1)} collective-permute-done((f32[64,1024]{1,0:T(8,128)S(1)}, f32[64,1024]{1,0:T(8,128)S(1)}, u32[]{:S(2)}, u32[]{:S(2)}) %collective-permute-start.17) | collective-permute-done | bytes 262176 | tf_op jit(solution)/shard_map/ppermute | solution.py:37
  117.4 1.9 %collective-permute-start.18 = (f32[64,1024]{1,0:T(8,128)S(1)}, f32[64,1024]{1,0:T(8,128)S(1)}, u32[]{:S(2)}, u32[]{:S(2)}) collective-permute-start(f32[64,1024]{1,0:T(8,128)S(1)} %add.34), channel_id=1, source_target_pairs={{0,1},{1,2},{2,3},{3,4},{4,5},{5,6},{6,7},{7,8},{8,9},{9,10},{10,1... | collective-permute-start | bytes 786440 | tf_op jit(solution)/shard_map/ppermute | solution.py:37
  119.4 1.7 %collective-permute-done.11 = f32[64,1024]{1,0:T(8,128)S(1)} collective-permute-done((f32[64,1024]{1,0:T(8,128)S(1)}, f32[64,1024]{1,0:T(8,128)S(1)}, u32[]{:S(2)}, u32[]{:S(2)}) %collective-permute-start.11) | collective-permute-done | bytes 262176 | tf_op jit(solution)/shard_map/ppermute | solution.py:37
  121.1 1.9 %collective-permute-start.12 = (f32[64,1024]{1,0:T(8,128)S(1)}, f32[64,1024]{1,0:T(8,128)S(1)}, u32[]{:S(2)}, u32[]{:S(2)}) collective-permute-start(f32[64,1024]{1,0:T(8,128)S(1)} %add.30), channel_id=1, source_target_pairs={{0,1},{1,2},{2,3},{3,4},{4,5},{5,6},{6,7},{7,8},{8,9},{9,10},{10,1... | collective-permute-start | bytes 786440 | tf_op jit(solution)/shard_map/ppermute | solution.py:37
  123.1 9.7 %collective-permute-done.18 = f32[64,1024]{1,0:T(8,128)S(1)} collective-permute-done((f32[64,1024]{1,0:T(8,128)S(1)}, f32[64,1024]{1,0:T(8,128)S(1)}, u32[]{:S(2)}, u32[]{:S(2)}) %collective-permute-start.18) | collective-permute-done | bytes 262176 | tf_op jit(solution)/shard_map/ppermute | solution.py:37
  132.8 1.9 %collective-permute-start.19 = (f32[64,1024]{1,0:T(8,128)S(1)}, f32[64,1024]{1,0:T(8,128)S(1)}, u32[]{:S(2)}, u32[]{:S(2)}) collective-permute-start(f32[64,1024]{1,0:T(8,128)S(1)} %add.35), channel_id=1, source_target_pairs={{0,1},{1,2},{2,3},{3,4},{4,5},{5,6},{6,7},{7,8},{8,9},{9,10},{10,1... | collective-permute-start | bytes 786440 | tf_op jit(solution)/shard_map/ppermute | solution.py:37
  134.8 0.8 collective-permute-done.12
  135.6 1.9 %collective-permute-start.13 = (f32[64,1024]{1,0:T(8,128)S(1)}, f32[64,1024]{1,0:T(8,128)S(1)}, u32[]{:S(2)}, u32[]{:S(2)}) collective-permute-start(f32[64,1024]{1,0:T(8,128)S(1)} %add.31), channel_id=1, source_target_pairs={{0,1},{1,2},{2,3},{3,4},{4,5},{5,6},{6,7},{7,8},{8,9},{9,10},{10,1... | collective-permute-start | bytes 786440 | tf_op jit(solution)/shard_map/ppermute | solution.py:37
  137.6 0.0 collective-permute-done.15
  137.6 8.3 %collective-permute-done.19.refs_4_ = f32[64,1024]{1,0:T(8,128)S(1)} collective-permute-done((f32[64,1024]{1,0:T(8,128)S(1)}, f32[64,1024]{1,0:T(8,128)S(1)}, u32[]{:S(2)}, u32[]{:S(2)}) %collective-permute-start.19) | collective-permute-done | bytes 262176 | tf_op jit(solution)/shard_map/ppermute | solution.py:37
  145.9 2.8 %collective-permute-done.13.refs_1_ = f32[64,1024]{1,0:T(8,128)S(1)} collective-permute-done((f32[64,1024]{1,0:T(8,128)S(1)}, f32[64,1024]{1,0:T(8,128)S(1)}, u32[]{:S(2)}, u32[]{:S(2)}) %collective-permute-start.13) | collective-permute-done | bytes 262176 | tf_op jit(solution)/shard_map/ppermute | solution.py:37
  148.8 1.2 unpack.1
  (20 shorter events, 0.4 us)
Async XLA Ops:
  0.9 1.1 copy-start
  2.0 23.2 %copy-start.1 = (f32[2,12,64,64]{3,2,1,0:T(8,128)S(1)}, f32[2,12,64,64]{3,2,1,0:T(8,128)}, u32[]{:S(2)}) copy-start(f32[2,12,64,64]{3,2,1,0:T(8,128)} %z_ref.1) | copy-start | bytes 1179652
  2.8 26.2 %collective-permute-start.4 = (f32[776,128]{1,0:T(8,128)S(1)}, f32[776,128]{1,0:T(8,128)S(1)}, u32[]{:S(2)}, u32[]{:S(2)}) collective-permute-start(f32[776,128]{1,0:T(8,128)S(1)} %get-tuple-element.28.refs_1_), channel_id=1, source_target_pairs={{0,1},{1,2},{2,3},{3,4},{4,5},{5,6},{6,7},{7,8},{8,9},{9,10},{10,1... | collective-permute-start | bytes 1191944 | tf_op jit(solution)/shard_map/ppermute | solution.py:37
  8.0 22.9 %collective-permute-start = (f32[776,128]{1,0:T(8,128)S(1)}, f32[776,128]{1,0:T(8,128)S(1)}, u32[]{:S(2)}, u32[]{:S(2)}) collective-permute-start(f32[776,128]{1,0:T(8,128)S(1)} %get-tuple-element.28.refs_1_), channel_id=1, source_target_pairs={{0,1023},{1,0},{2,1},{3,2},{4,3},{5,4},{6,5},{7,6},{8,7},{9,8},{10... | collective-permute-start | bytes 1191944 | tf_op jit(solution)/shard_map/ppermute | solution.py:37
  25.2 1.3 copy-start.2
  29.0 14.7 %collective-permute-start.5 = (f32[776,128]{1,0:T(8,128)S(1)}, f32[776,128]{1,0:T(8,128)S(1)}, u32[]{:S(2)}, u32[]{:S(2)}) collective-permute-start(f32[776,128]{1,0:T(8,128)S(1)} %collective-permute-done.4.refs_3_), channel_id=1, source_target_pairs={{0,1},{1,2},{2,3},{3,4},{4,5},{5,6},{6,7},{7,8},{8,9},{9,10},{10,1... | collective-permute-start | bytes 1191944 | tf_op jit(solution)/shard_map/ppermute | solution.py:37
  31.0 14.7 %collective-permute-start.1 = (f32[776,128]{1,0:T(8,128)S(1)}, f32[776,128]{1,0:T(8,128)S(1)}, u32[]{:S(2)}, u32[]{:S(2)}) collective-permute-start(f32[776,128]{1,0:T(8,128)S(1)} %collective-permute-done.refs_2_), channel_id=1, source_target_pairs={{0,1023},{1,0},{2,1},{3,2},{4,3},{5,4},{6,5},{7,6},{8,7},{9,8},{10... | collective-permute-start | bytes 1191944 | tf_op jit(solution)/shard_map/ppermute | solution.py:37
  43.7 14.7 %collective-permute-start.6 = (f32[776,128]{1,0:T(8,128)S(1)}, f32[776,128]{1,0:T(8,128)S(1)}, u32[]{:S(2)}, u32[]{:S(2)}) collective-permute-start(f32[776,128]{1,0:T(8,128)S(1)} %collective-permute-done.5.refs_3_), channel_id=1, source_target_pairs={{0,1},{1,2},{2,3},{3,4},{4,5},{5,6},{6,7},{7,8},{8,9},{9,10},{10,1... | collective-permute-start | bytes 1191944 | tf_op jit(solution)/shard_map/ppermute | solution.py:37
  45.6 16.6 %collective-permute-start.2 = (f32[776,128]{1,0:T(8,128)S(1)}, f32[776,128]{1,0:T(8,128)S(1)}, u32[]{:S(2)}, u32[]{:S(2)}) collective-permute-start(f32[776,128]{1,0:T(8,128)S(1)} %collective-permute-done.1.refs_2_), channel_id=1, source_target_pairs={{0,1023},{1,0},{2,1},{3,2},{4,3},{5,4},{6,5},{7,6},{8,7},{9,8},{10... | collective-permute-start | bytes 1191944 | tf_op jit(solution)/shard_map/ppermute | solution.py:37
  58.4 16.2 %collective-permute-start.7 = (f32[776,128]{1,0:T(8,128)S(1)}, f32[776,128]{1,0:T(8,128)S(1)}, u32[]{:S(2)}, u32[]{:S(2)}) collective-permute-start(f32[776,128]{1,0:T(8,128)S(1)} %pad_maximum_fusion.1), channel_id=1, source_target_pairs={{0,1016},{1,1017},{2,1018},{3,1019},{4,1020},{5,1021},{6,1022},{7,... | collective-permute-start | bytes 1191944 | tf_op jit(solution)/shard_map/ppermute | solution.py:37
  60.3 23.5 %collective-permute-start.9 = (f32[776,128]{1,0:T(8,128)S(1)}, f32[776,128]{1,0:T(8,128)S(1)}, u32[]{:S(2)}, u32[]{:S(2)}) collective-permute-start(f32[776,128]{1,0:T(8,128)S(1)} %collective-permute-done.6.refs_3_), channel_id=1, source_target_pairs={{0,1},{1,2},{2,3},{3,4},{4,5},{5,6},{6,7},{7,8},{8,9},{9,10},{10,1... | collective-permute-start | bytes 1191944 | tf_op jit(solution)/shard_map/ppermute | solution.py:37
  62.3 21.6 %collective-permute-start.8 = (f32[776,128]{1,0:T(8,128)S(1)}, f32[776,128]{1,0:T(8,128)S(1)}, u32[]{:S(2)}, u32[]{:S(2)}) collective-permute-start(f32[776,128]{1,0:T(8,128)S(1)} %collective-permute-done.2.refs_2_), channel_id=1, source_target_pairs={{0,1023},{1,0},{2,1},{3,2},{4,3},{5,4},{6,5},{7,6},{8,7},{9,8},{10... | collective-permute-start | bytes 1191944 | tf_op jit(solution)/shard_map/ppermute | solution.py:37
  71.3 12.5 %collective-permute-start.3 = (f32[776,128]{1,0:T(8,128)S(1)}, f32[776,128]{1,0:T(8,128)S(1)}, u32[]{:S(2)}, u32[]{:S(2)}) collective-permute-start(f32[776,128]{1,0:T(8,128)S(1)} %collective-permute-done.2.refs_2_), channel_id=1, source_target_pairs={{0,8},{1,9},{2,10},{3,11},{4,12},{5,13},{6,14},{7,15},{8,16},{9,17... | collective-permute-start | bytes 1191944 | tf_op jit(solution)/shard_map/ppermute | solution.py:37
  87.7 22.1 %collective-permute-start.14 = (f32[128,1024]{1,0:T(8,128)S(1)}, f32[128,1024]{1,0:T(8,128)S(1)}, u32[]{:S(2)}, u32[]{:S(2)}) collective-permute-start(f32[128,1024]{1,0:T(8,128)S(1)} %pad_maximum_fusion), channel_id=1, source_target_pairs={{0,1023},{1,0},{2,1},{3,2},{4,3},{5,4},{6,5},{7,6},{8,7},{9,8},{10... | collective-permute-start | bytes 1572872 | tf_op jit(solution)/shard_map/ppermute | solution.py:37
  90.9 13.2 %collective-permute-start.16 = (f32[64,1024]{1,0:T(8,128)S(1)}, f32[64,1024]{1,0:T(8,128)S(1)}, u32[]{:S(2)}, u32[]{:S(2)}) collective-permute-start(f32[64,1024]{1,0:T(8,128)S(1)} %get-tuple-element.45), channel_id=1, source_target_pairs={{0,1},{1,2},{2,3},{3,4},{4,5},{5,6},{6,7},{7,8},{8,9},{9,10},{10,1... | collective-permute-start | bytes 786440 | tf_op jit(solution)/shard_map/ppermute | solution.py:37
  94.7 13.2 %collective-permute-start.10 = (f32[64,1024]{1,0:T(8,128)S(1)}, f32[64,1024]{1,0:T(8,128)S(1)}, u32[]{:S(2)}, u32[]{:S(2)}) collective-permute-start(f32[64,1024]{1,0:T(8,128)S(1)} %get-tuple-element.36), channel_id=1, source_target_pairs={{0,1},{1,2},{2,3},{3,4},{4,5},{5,6},{6,7},{7,8},{8,9},{9,10},{10,1... | collective-permute-start | bytes 786440 | tf_op jit(solution)/shard_map/ppermute | solution.py:37
  104.2 13.2 %collective-permute-start.17 = (f32[64,1024]{1,0:T(8,128)S(1)}, f32[64,1024]{1,0:T(8,128)S(1)}, u32[]{:S(2)}, u32[]{:S(2)}) collective-permute-start(f32[64,1024]{1,0:T(8,128)S(1)} %add.33), channel_id=1, source_target_pairs={{0,1},{1,2},{2,3},{3,4},{4,5},{5,6},{6,7},{7,8},{8,9},{9,10},{10,1... | collective-permute-start | bytes 786440 | tf_op jit(solution)/shard_map/ppermute | solution.py:37
  107.9 13.2 %collective-permute-start.11 = (f32[64,1024]{1,0:T(8,128)S(1)}, f32[64,1024]{1,0:T(8,128)S(1)}, u32[]{:S(2)}, u32[]{:S(2)}) collective-permute-start(f32[64,1024]{1,0:T(8,128)S(1)} %add.29), channel_id=1, source_target_pairs={{0,1},{1,2},{2,3},{3,4},{4,5},{5,6},{6,7},{7,8},{8,9},{9,10},{10,1... | collective-permute-start | bytes 786440 | tf_op jit(solution)/shard_map/ppermute | solution.py:37
  109.9 27.7 %collective-permute-start.15 = (f32[128,1024]{1,0:T(8,128)S(1)}, f32[128,1024]{1,0:T(8,128)S(1)}, u32[]{:S(2)}, u32[]{:S(2)}) collective-permute-start(f32[128,1024]{1,0:T(8,128)S(1)} %maximum_add_fusion), channel_id=1, source_target_pairs={{0,6},{1,7},{2,8},{3,9},{4,10},{5,11},{6,12},{7,13},{8,14},{9,15},... | collective-permute-start | bytes 1572872 | tf_op jit(solution)/shard_map/ppermute | solution.py:37
  117.4 15.4 %collective-permute-start.18 = (f32[64,1024]{1,0:T(8,128)S(1)}, f32[64,1024]{1,0:T(8,128)S(1)}, u32[]{:S(2)}, u32[]{:S(2)}) collective-permute-start(f32[64,1024]{1,0:T(8,128)S(1)} %add.34), channel_id=1, source_target_pairs={{0,1},{1,2},{2,3},{3,4},{4,5},{5,6},{6,7},{7,8},{8,9},{9,10},{10,1... | collective-permute-start | bytes 786440 | tf_op jit(solution)/shard_map/ppermute | solution.py:37
  121.1 14.5 %collective-permute-start.12 = (f32[64,1024]{1,0:T(8,128)S(1)}, f32[64,1024]{1,0:T(8,128)S(1)}, u32[]{:S(2)}, u32[]{:S(2)}) collective-permute-start(f32[64,1024]{1,0:T(8,128)S(1)} %add.30), channel_id=1, source_target_pairs={{0,1},{1,2},{2,3},{3,4},{4,5},{5,6},{6,7},{7,8},{8,9},{9,10},{10,1... | collective-permute-start | bytes 786440 | tf_op jit(solution)/shard_map/ppermute | solution.py:37
  132.8 13.1 %collective-permute-start.19 = (f32[64,1024]{1,0:T(8,128)S(1)}, f32[64,1024]{1,0:T(8,128)S(1)}, u32[]{:S(2)}, u32[]{:S(2)}) collective-permute-start(f32[64,1024]{1,0:T(8,128)S(1)} %add.35), channel_id=1, source_target_pairs={{0,1},{1,2},{2,3},{3,4},{4,5},{5,6},{6,7},{7,8},{8,9},{9,10},{10,1... | collective-permute-start | bytes 786440 | tf_op jit(solution)/shard_map/ppermute | solution.py:37
  135.6 13.1 %collective-permute-start.13 = (f32[64,1024]{1,0:T(8,128)S(1)}, f32[64,1024]{1,0:T(8,128)S(1)}, u32[]{:S(2)}, u32[]{:S(2)}) collective-permute-start(f32[64,1024]{1,0:T(8,128)S(1)} %add.31), channel_id=1, source_target_pairs={{0,1},{1,2},{2,3},{3,4},{4,5},{5,6},{6,7},{7,8},{8,9},{9,10},{10,1... | collective-permute-start | bytes 786440 | tf_op jit(solution)/shard_map/ppermute | solution.py:37

commit v3 on v2

--- a/solution.py
+++ b/solution.py
@@ -136,43 +136,36 @@
             w_ref[at] = w_ref[at] + part
 
 
-def gather_kernel(ds, first, last, *refs):
+def gather_kernel(ds, first, *refs):
     n = len(ds)
     metas, xs = refs[:n], refs[n : 2 * n]
-    hh_ref, hl_ref = refs[2 * n : 2 * n + 2]
-    rest = list(refs[2 * n + 2 :])
-    if last:
-        w_in, ww_ref, w_ref = rest
-        w_ref[...] = w_in[...]
-    elif first:
-        (w_ref,) = rest
-        w_ref[...] = jnp.zeros_like(w_ref)
-    else:
-        w_in, w_ref = rest
-        w_ref[...] = w_in[...]
+    hh_ref, hl_ref, w_ref = refs[2 * n], refs[2 * n + 1], refs[-1]
+    w_ref[...] = jnp.zeros_like(w_ref) if first else refs[-2][...]
     for d, meta, x_ref in zip(ds, metas, xs):
         add_rows(d, meta, x_ref, hh_ref, hl_ref, w_ref)
-    if last:
-        for f in range(NC):
-            hi, lo = split(w_ref[f])
-            ww_ref[f, :, 0 : 2 * B] = hi
-            ww_ref[f, :, 2 * B :] = lo
-
-
-def gather(ds, metas, xs, hh, hl, w, last):
+
+
+def gather(ds, metas, xs, hh, hl, w):
+    n = len(ds)
     first = w is None
-    acc = (NC, B, 2 * B)
-    return pl.pallas_call(
-        functools.partial(gather_kernel, ds, first, last),
-        out_shape=jax.ShapeDtypeStruct((NC, B, 4 * B), BF16)
-        if last
-        else jax.ShapeDtypeStruct(acc, F32),
-        in_specs=smem(len(ds)) + vmem(len(ds) + 2 + (not first)),
+    return pl.pallas_call(
+        functools.partial(gather_kernel, ds, first),
+        out_shape=jax.ShapeDtypeStruct((NC, B, 2 * B), F32),
+        in_specs=smem(n) + vmem(n + 2 + (not first)),
         out_specs=pl.BlockSpec(memory_space=pltpu.VMEM),
-        scratch_shapes=[pltpu.VMEM(acc, F32)] if last else [],
-        compiler_params=PARAMS,
-        name="gather_last" if last else "gather",
+        compiler_params=PARAMS,
+        name="gather",
     )(*metas, *xs, hh, hl, *([] if first else [w]))
+
+
+def spread_half(k, ra, meta, zz_ref, ww_ref, picked, out):
+    a = 2 * k + ra
+    for o in range(NO):
+        picked[o * B : (o + 1) * B, :] = ww_ref[meta[2 + ra, o] + a]
+    both = lax.dot_general(
+        zz_ref[a], picked[...], (((1,), (1,)), ((), ())), preferred_element_type=F32
+    )
+    out[...] = both[0:B] + both[B:]
 
 
 def spread_kernel(jobs, *refs):
@@ -181,16 +174,7 @@
     zz_ref, ww_ref = refs[len(ks) : len(ks) + 2]
     outs, picked = refs[len(ks) + 2 : -1], refs[-1]
     for slot, ((k, ra), out) in enumerate(zip(jobs, outs)):
-        a = 2 * k + ra
-        for o in range(NO):
-            picked[slot % 2, o * B : (o + 1) * B, :] = ww_ref[metas[k][2 + ra, o] + a]
-        both = lax.dot_general(
-            zz_ref[a],
-            picked[slot % 2],
-            (((1,), (1,)), ((), ())),
-            preferred_element_type=F32,
-        )
-        out[...] = both[0:B] + both[B:]
+        spread_half(k, ra, metas[k], zz_ref, ww_ref, picked.at[slot % 2], out)
 
 
 def spread(jobs, metas, zz, ww):
@@ -205,6 +189,42 @@
         compiler_params=PARAMS,
         name="spread",
     )(*(metas[k] for k in ks), zz, ww)
+
+
+def finish_kernel(ds, m0, m1, m4, x0, x1, hh_ref, hl_ref, zz_ref, w_in, *refs):
+    ww_ref, p5, p41, p40, w_ref, picked = refs
+    w_ref[...] = w_in[...]
+    for d, meta, x_ref in zip(ds, (m0, m1), (x0, x1)):
+        add_rows(d, meta, x_ref, hh_ref, hl_ref, w_ref)
+    for f in range(NC):
+        hi, lo = split(w_ref[f])
+        ww_ref[f, :, 0 : 2 * B] = hi
+        ww_ref[f, :, 2 * B :] = lo
+    spread_half(5, 0, m0, zz_ref, ww_ref, picked.at[0], p5.at[0:B])
+    spread_half(5, 1, m0, zz_ref, ww_ref, picked.at[1], p5.at[B : 2 * B])
+    spread_half(4, 1, m4, zz_ref, ww_ref, picked.at[0], p41)
+    spread_half(4, 0, m4, zz_ref, ww_ref, picked.at[1], p40)
+
+
+def finish(ds, metas, xs, hh, hl, zz, w):
+    half = jax.ShapeDtypeStruct((B, NO * B), F32)
+    return pl.pallas_call(
+        functools.partial(finish_kernel, ds),
+        out_shape=(
+            jax.ShapeDtypeStruct((NC, B, 4 * B), BF16),
+            jax.ShapeDtypeStruct((2 * B, NO * B), F32),
+            half,
+            half,
+        ),
+        in_specs=smem(3) + vmem(6),
+        out_specs=tuple(vmem(4)),
+        scratch_shapes=[
+            pltpu.VMEM((NC, B, 2 * B), F32),
+            pltpu.VMEM((2, NO * B, 4 * B), BF16),
+        ],
+        compiler_params=PARAMS,
+        name="finish",
+    )(*metas, *xs, hh, hl, zz, w)
 
 
 def unpack_kernel(*refs):
@@ -252,23 +272,29 @@
     metas[LAST] = up[REACH][ZROWS + 4 :].astype(jnp.int32)
     hh, hl, zz = prep(h_off, meta, h_blocks, z_blocks)
 
-    def step(ds, w, last=False):
+    def step(ds, w):
         xs = [up[d] if d >= 0 else down[-d] for d in ds]
-        return gather(ds, [metas[d] for d in ds], xs, hh, hl, w, last)
+        return gather(ds, [metas[d] for d in ds], xs, hh, hl, w)
 
     w = step((0,), None)
     w = step((1, -1), w)
     w = step((2, -2), w)
     w = step((3, -3), w)
     w = step((4, -4), w)
-    ww = step((5, -5), w, last=True)
+    ww, p5, p41, p40 = finish(
+        (REACH, -REACH),
+        (metas[REACH], metas[-REACH], metas[4]),
+        (up[REACH], down[REACH]),
+        hh,
+        hl,
+        zz,
+        w,
+    )
 
     def parts(*jobs):
         return spread(jobs, metas, zz, ww)
 
-    p50, p51 = parts((5, 0), (5, 1))
-    back = shift(jnp.concatenate([p50, p51], axis=0), -1)
-    p41, p40 = parts((4, 1), (4, 0))
+    back = shift(p5, -1)
     ahead1 = shift(p41, 1)
     ahead0 = shift(p40, 1)
     p31, p30, p60, p61, p21, p20, p11, p10, p00, p01 = parts(

time: 151 us -> 149 us (0.987)
    pallas_call x3 -> x1, Pallas kernels: 4.81 us -> 2.66 us  [spread(): pl.pallas_call(functools.partial(spread_kernel, jobs), out_shape=(half,)...]
  transfers between devices with their start and end apart: 20 -> 20, of which waited for: 11 -> 11; matrix products, arithmetic and copies ran while one was open for 0% -> 0% of each run, Pallas kernels for 7% -> 6%
where the time goes in v3:
time: 149 us
  starting transfers between devices  80.3 us (54%)
  waiting for transfers between devices  49.5 us (33%)
  Pallas kernels  14.7 us (10%)
  local copies, waits for them, and re-layouts  2.49 us (2%)
    ppermute x20, starting transfers between devices, shift(): return lax.ppermute(x, AXES, [(i, (i + by) % size) for i in range(size)])  80.3 us
    ppermute x20, waiting for transfers between devices, shift(): return lax.ppermute(x, AXES, [(i, (i + by) % size) for i in range(size)])  49.5 us
    pallas_call x5, Pallas kernels, gather(): pl.pallas_call(functools.partial(gather_kernel, ds, first), out_shape=jax...  6.17 us
  transfers between devices with their start and end apart: 20, of which 11 were waited for; matrix products, arithmetic and copies ran while one was open for 0% of the time, Pallas kernels for 6%

profile of v3, /device:TPU:8, one launch (start us, length us, event | category | flops | bytes accessed | tf_op | source)
XLA Modules:
  0.0 148.7 jit_solution(17180976057546160921)
XLA Ops:
  0.0 0.1 pad_add_fusion.1.here_ref
  0.1 0.8 pad_add_fusion.cols
  0.9 0.0 copy-start
  0.9 1.1 copy-done
  2.0 0.0 copy-start.1
  2.0 0.8 pack.1
  2.8 5.2 %collective-permute-start.4 = (f32[776,128]{1,0:T(8,128)S(1)}, f32[776,128]{1,0:T(8,128)S(1)}, u32[]{:S(2)}, u32[]{:S(2)}) collective-permute-start(f32[776,128]{1,0:T(8,128)S(1)} %get-tuple-element.28.refs_1_), channel_id=1, source_target_pairs={{0,1},{1,2},{2,3},{3,4},{4,5},{5,6},{6,7},{7,8},{8,9},{9,10},{10,1... | collective-permute-start | bytes 1191944 | tf_op jit(solution)/shard_map/ppermute | solution.py:37
  8.0 17.2 %collective-permute-start = (f32[776,128]{1,0:T(8,128)S(1)}, f32[776,128]{1,0:T(8,128)S(1)}, u32[]{:S(2)}, u32[]{:S(2)}) collective-permute-start(f32[776,128]{1,0:T(8,128)S(1)} %get-tuple-element.28.refs_1_), channel_id=1, source_target_pairs={{0,1023},{1,0},{2,1},{3,2},{4,3},{5,4},{6,5},{7,6},{8,7},{9,8},{10... | collective-permute-start | bytes 1191944 | tf_op jit(solution)/shard_map/ppermute | solution.py:37
  25.2 0.0 copy-done.1
  25.2 0.0 copy-start.2
  25.2 1.3 copy-done.2
  26.5 1.5 prep.1
  28.0 1.0 gather.5.refs_6_
  29.0 0.0 collective-permute-done.4.refs_3_
  29.0 1.9 %collective-permute-start.5 = (f32[776,128]{1,0:T(8,128)S(1)}, f32[776,128]{1,0:T(8,128)S(1)}, u32[]{:S(2)}, u32[]{:S(2)}) collective-permute-start(f32[776,128]{1,0:T(8,128)S(1)} %collective-permute-done.4.refs_3_), channel_id=1, source_target_pairs={{0,1},{1,2},{2,3},{3,4},{4,5},{5,6},{6,7},{7,8},{8,9},{9,10},{10,1... | collective-permute-start | bytes 1191944 | tf_op jit(solution)/shard_map/ppermute | solution.py:37
  30.9 0.0 collective-permute-done.refs_2_
  31.0 9.1 %collective-permute-start.1 = (f32[776,128]{1,0:T(8,128)S(1)}, f32[776,128]{1,0:T(8,128)S(1)}, u32[]{:S(2)}, u32[]{:S(2)}) collective-permute-start(f32[776,128]{1,0:T(8,128)S(1)} %collective-permute-done.refs_2_), channel_id=1, source_target_pairs={{0,1023},{1,0},{2,1},{3,2},{4,3},{5,4},{6,5},{7,6},{8,7},{9,8},{10... | collective-permute-start | bytes 1191944 | tf_op jit(solution)/shard_map/ppermute | solution.py:37
  40.1 1.3 gather.6.refs_6_
  41.4 2.3 %collective-permute-done.5.refs_3_ = f32[776,128]{1,0:T(8,128)S(1)} collective-permute-done((f32[776,128]{1,0:T(8,128)S(1)}, f32[776,128]{1,0:T(8,128)S(1)}, u32[]{:S(2)}, u32[]{:S(2)}) %collective-permute-start.5) | collective-permute-done | bytes 397344 | tf_op jit(solution)/shard_map/ppermute | solution.py:37
  43.7 1.9 %collective-permute-start.6 = (f32[776,128]{1,0:T(8,128)S(1)}, f32[776,128]{1,0:T(8,128)S(1)}, u32[]{:S(2)}, u32[]{:S(2)}) collective-permute-start(f32[776,128]{1,0:T(8,128)S(1)} %collective-permute-done.5.refs_3_), channel_id=1, source_target_pairs={{0,1},{1,2},{2,3},{3,4},{4,5},{5,6},{6,7},{7,8},{8,9},{9,10},{10,1... | collective-permute-start | bytes 1191944 | tf_op jit(solution)/shard_map/ppermute | solution.py:37
  45.6 0.0 collective-permute-done.1.refs_2_
  45.6 9.1 %collective-permute-start.2 = (f32[776,128]{1,0:T(8,128)S(1)}, f32[776,128]{1,0:T(8,128)S(1)}, u32[]{:S(2)}, u32[]{:S(2)}) collective-permute-start(f32[776,128]{1,0:T(8,128)S(1)} %collective-permute-done.1.refs_2_), channel_id=1, source_target_pairs={{0,1023},{1,0},{2,1},{3,2},{4,3},{5,4},{6,5},{7,6},{8,7},{9,8},{10... | collective-permute-start | bytes 1191944 | tf_op jit(solution)/shard_map/ppermute | solution.py:37
  54.7 1.3 gather.7.refs_6_
  56.0 2.3 %collective-permute-done.6.refs_3_ = f32[776,128]{1,0:T(8,128)S(1)} collective-permute-done((f32[776,128]{1,0:T(8,128)S(1)}, f32[776,128]{1,0:T(8,128)S(1)}, u32[]{:S(2)}, u32[]{:S(2)}) %collective-permute-start.6) | collective-permute-done | bytes 397344 | tf_op jit(solution)/shard_map/ppermute | solution.py:37
  58.4 1.9 %collective-permute-start.7 = (f32[776,128]{1,0:T(8,128)S(1)}, f32[776,128]{1,0:T(8,128)S(1)}, u32[]{:S(2)}, u32[]{:S(2)}) collective-permute-start(f32[776,128]{1,0:T(8,128)S(1)} %pad_maximum_fusion), channel_id=1, source_target_pairs={{0,1016},{1,1017},{2,1018},{3,1019},{4,1020},{5,1021},{6,1022},{7,... | collective-permute-start | bytes 1191944 | tf_op jit(solution)/shard_map/ppermute | solution.py:37
  60.3 1.9 %collective-permute-start.9 = (f32[776,128]{1,0:T(8,128)S(1)}, f32[776,128]{1,0:T(8,128)S(1)}, u32[]{:S(2)}, u32[]{:S(2)}) collective-permute-start(f32[776,128]{1,0:T(8,128)S(1)} %collective-permute-done.6.refs_3_), channel_id=1, source_target_pairs={{0,1},{1,2},{2,3},{3,4},{4,5},{5,6},{6,7},{7,8},{8,9},{9,10},{10,1... | collective-permute-start | bytes 1191944 | tf_op jit(solution)/shard_map/ppermute | solution.py:37
  62.2 0.0 collective-permute-done.2.refs_2_
  62.3 9.1 %collective-permute-start.8 = (f32[776,128]{1,0:T(8,128)S(1)}, f32[776,128]{1,0:T(8,128)S(1)}, u32[]{:S(2)}, u32[]{:S(2)}) collective-permute-start(f32[776,128]{1,0:T(8,128)S(1)} %collective-permute-done.2.refs_2_), channel_id=1, source_target_pairs={{0,1023},{1,0},{2,1},{3,2},{4,3},{5,4},{6,5},{7,6},{8,7},{9,8},{10... | collective-permute-start | bytes 1191944 | tf_op jit(solution)/shard_map/ppermute | solution.py:37
  71.3 1.9 %collective-permute-start.3 = (f32[776,128]{1,0:T(8,128)S(1)}, f32[776,128]{1,0:T(8,128)S(1)}, u32[]{:S(2)}, u32[]{:S(2)}) collective-permute-start(f32[776,128]{1,0:T(8,128)S(1)} %collective-permute-done.2.refs_2_), channel_id=1, source_target_pairs={{0,8},{1,9},{2,10},{3,11},{4,12},{5,13},{6,14},{7,15},{8,16},{9,17... | collective-permute-start | bytes 1191944 | tf_op jit(solution)/shard_map/ppermute | solution.py:37
  73.3 1.3 gather.8.refs_6_
  74.6 0.0 collective-permute-done.7.x0
  74.6 9.2 %collective-permute-done.3.x1 = f32[776,128]{1,0:T(8,128)S(1)} collective-permute-done((f32[776,128]{1,0:T(8,128)S(1)}, f32[776,128]{1,0:T(8,128)S(1)}, u32[]{:S(2)}, u32[]{:S(2)}) %collective-permute-start.3) | collective-permute-done | bytes 397344 | tf_op jit(solution)/shard_map/ppermute | solution.py:37
  83.8 0.0 collective-permute-done.9.refs_3_
  83.8 0.0 collective-permute-done.8.refs_2_
  83.8 1.3 gather.9.w_in
  85.1 2.4 %finish.1 = (bf16[34,64,256]{2,1,0:T(8,128)(2,1)S(1)}, f32[128,1024]{1,0:T(8,128)S(1)}, f32[64,1024]{1,0:T(8,128)S(1)}, f32[64,1024]{1,0:T(8,128)S(1)}) custom-call(s32[8,128]{1,0:T(8,128)S(1)} %get-tuple-element.52.m0, s32[8,128]{1,0:T(8,128)S(1)} %get-tuple-element.51.m1, s32[8,128]{1,0:T(8,128)S(1)} %slice_convert_fusion.4.refs_0_.m4, ...), custom_call_target="tpu_custom_call" | custom-call | tf_op jit(solution)/shard_map/finish/pallas_call | solution.py:211
  87.5 2.1 %collective-permute-start.14 = (f32[128,1024]{1,0:T(8,128)S(1)}, f32[128,1024]{1,0:T(8,128)S(1)}, u32[]{:S(2)}, u32[]{:S(2)}) collective-permute-start(f32[128,1024]{1,0:T(8,128)S(1)} %get-tuple-element.41), channel_id=1, source_target_pairs={{0,1023},{1,0},{2,1},{3,2},{4,3},{5,4},{6,5},{7,6},{8,7},{9,8},{10... | collective-permute-start | bytes 1572872 | tf_op jit(solution)/shard_map/ppermute | solution.py:37
  89.6 3.8 %collective-permute-start.16 = (f32[64,1024]{1,0:T(8,128)S(1)}, f32[64,1024]{1,0:T(8,128)S(1)}, u32[]{:S(2)}, u32[]{:S(2)}) collective-permute-start(f32[64,1024]{1,0:T(8,128)S(1)} %get-tuple-element.45), channel_id=1, source_target_pairs={{0,1},{1,2},{2,3},{3,4},{4,5},{5,6},{6,7},{7,8},{8,9},{9,10},{10,1... | collective-permute-start | bytes 786440 | tf_op jit(solution)/shard_map/ppermute | solution.py:37
  93.4 1.9 %collective-permute-start.10 = (f32[64,1024]{1,0:T(8,128)S(1)}, f32[64,1024]{1,0:T(8,128)S(1)}, u32[]{:S(2)}, u32[]{:S(2)}) collective-permute-start(f32[64,1024]{1,0:T(8,128)S(1)} %get-tuple-element.37), channel_id=1, source_target_pairs={{0,1},{1,2},{2,3},{3,4},{4,5},{5,6},{6,7},{7,8},{8,9},{9,10},{10,1... | collective-permute-start | bytes 786440 | tf_op jit(solution)/shard_map/ppermute | solution.py:37
  95.3 2.7 %spread.1 = (f32[64,1024]{1,0:T(8,128)S(1)}, f32[64,1024]{1,0:T(8,128)S(1)}, f32[64,1024]{1,0:T(8,128)S(1)}, f32[64,1024]{1,0:T(8,128)S(1)}, f32[64,1024]{1,0:T(...) custom-call(s32[8,128]{1,0:T(8,128)S(1)} %get-tuple-element.27.meta., ...), custom_call_target="tpu_custom_call" | custom-call | tf_op jit(solution)/shard_map/spread/pallas_call | solution.py:183
  98.0 4.8 %collective-permute-done.16 = f32[64,1024]{1,0:T(8,128)S(1)} collective-permute-done((f32[64,1024]{1,0:T(8,128)S(1)}, f32[64,1024]{1,0:T(8,128)S(1)}, u32[]{:S(2)}, u32[]{:S(2)}) %collective-permute-start.16) | collective-permute-done | bytes 262176 | tf_op jit(solution)/shard_map/ppermute | solution.py:37
  102.9 1.9 %collective-permute-start.17 = (f32[64,1024]{1,0:T(8,128)S(1)}, f32[64,1024]{1,0:T(8,128)S(1)}, u32[]{:S(2)}, u32[]{:S(2)}) collective-permute-start(f32[64,1024]{1,0:T(8,128)S(1)} %add.33), channel_id=1, source_target_pairs={{0,1},{1,2},{2,3},{3,4},{4,5},{5,6},{6,7},{7,8},{8,9},{9,10},{10,1... | collective-permute-start | bytes 786440 | tf_op jit(solution)/shard_map/ppermute | solution.py:37
  104.8 1.8 %collective-permute-done.10 = f32[64,1024]{1,0:T(8,128)S(1)} collective-permute-done((f32[64,1024]{1,0:T(8,128)S(1)}, f32[64,1024]{1,0:T(8,128)S(1)}, u32[]{:S(2)}, u32[]{:S(2)}) %collective-permute-start.10) | collective-permute-done | bytes 262176 | tf_op jit(solution)/shard_map/ppermute | solution.py:37
  106.6 1.9 %collective-permute-start.11 = (f32[64,1024]{1,0:T(8,128)S(1)}, f32[64,1024]{1,0:T(8,128)S(1)}, u32[]{:S(2)}, u32[]{:S(2)}) collective-permute-start(f32[64,1024]{1,0:T(8,128)S(1)} %add.29), channel_id=1, source_target_pairs={{0,1},{1,2},{2,3},{3,4},{4,5},{5,6},{6,7},{7,8},{8,9},{9,10},{10,1... | collective-permute-start | bytes 786440 | tf_op jit(solution)/shard_map/ppermute | solution.py:37
  108.5 0.0 collective-permute-done.14
  108.5 0.1 maximum_add_fusion
  108.6 1.9 %collective-permute-start.15 = (f32[128,1024]{1,0:T(8,128)S(1)}, f32[128,1024]{1,0:T(8,128)S(1)}, u32[]{:S(2)}, u32[]{:S(2)}) collective-permute-start(f32[128,1024]{1,0:T(8,128)S(1)} %maximum_add_fusion), channel_id=1, source_target_pairs={{0,6},{1,7},{2,8},{3,9},{4,10},{5,11},{6,12},{7,13},{8,14},{9,15},... | collective-permute-start | bytes 1572872 | tf_op jit(solution)/shard_map/ppermute | solution.py:37
  110.5 5.5 %collective-permute-done.17 = f32[64,1024]{1,0:T(8,128)S(1)} collective-permute-done((f32[64,1024]{1,0:T(8,128)S(1)}, f32[64,1024]{1,0:T(8,128)S(1)}, u32[]{:S(2)}, u32[]{:S(2)}) %collective-permute-start.17) | collective-permute-done | bytes 262176 | tf_op jit(solution)/shard_map/ppermute | solution.py:37
  116.1 1.9 %collective-permute-start.18 = (f32[64,1024]{1,0:T(8,128)S(1)}, f32[64,1024]{1,0:T(8,128)S(1)}, u32[]{:S(2)}, u32[]{:S(2)}) collective-permute-start(f32[64,1024]{1,0:T(8,128)S(1)} %add.34), channel_id=1, source_target_pairs={{0,1},{1,2},{2,3},{3,4},{4,5},{5,6},{6,7},{7,8},{8,9},{9,10},{10,1... | collective-permute-start | bytes 786440 | tf_op jit(solution)/shard_map/ppermute | solution.py:37
  118.1 1.7 %collective-permute-done.11 = f32[64,1024]{1,0:T(8,128)S(1)} collective-permute-done((f32[64,1024]{1,0:T(8,128)S(1)}, f32[64,1024]{1,0:T(8,128)S(1)}, u32[]{:S(2)}, u32[]{:S(2)}) %collective-permute-start.11) | collective-permute-done | bytes 262176 | tf_op jit(solution)/shard_map/ppermute | solution.py:37
  119.8 1.9 %collective-permute-start.12 = (f32[64,1024]{1,0:T(8,128)S(1)}, f32[64,1024]{1,0:T(8,128)S(1)}, u32[]{:S(2)}, u32[]{:S(2)}) collective-permute-start(f32[64,1024]{1,0:T(8,128)S(1)} %add.30), channel_id=1, source_target_pairs={{0,1},{1,2},{2,3},{3,4},{4,5},{5,6},{6,7},{7,8},{8,9},{9,10},{10,1... | collective-permute-start | bytes 786440 | tf_op jit(solution)/shard_map/ppermute | solution.py:37
  121.8 9.7 %collective-permute-done.18 = f32[64,1024]{1,0:T(8,128)S(1)} collective-permute-done((f32[64,1024]{1,0:T(8,128)S(1)}, f32[64,1024]{1,0:T(8,128)S(1)}, u32[]{:S(2)}, u32[]{:S(2)}) %collective-permute-start.18) | collective-permute-done | bytes 262176 | tf_op jit(solution)/shard_map/ppermute | solution.py:37
  131.5 1.9 %collective-permute-start.19 = (f32[64,1024]{1,0:T(8,128)S(1)}, f32[64,1024]{1,0:T(8,128)S(1)}, u32[]{:S(2)}, u32[]{:S(2)}) collective-permute-start(f32[64,1024]{1,0:T(8,128)S(1)} %add.35), channel_id=1, source_target_pairs={{0,1},{1,2},{2,3},{3,4},{4,5},{5,6},{6,7},{7,8},{8,9},{9,10},{10,1... | collective-permute-start | bytes 786440 | tf_op jit(solution)/shard_map/ppermute | solution.py:37
  133.4 0.8 collective-permute-done.12
  134.3 1.9 %collective-permute-start.13 = (f32[64,1024]{1,0:T(8,128)S(1)}, f32[64,1024]{1,0:T(8,128)S(1)}, u32[]{:S(2)}, u32[]{:S(2)}) collective-permute-start(f32[64,1024]{1,0:T(8,128)S(1)} %add.31), channel_id=1, source_target_pairs={{0,1},{1,2},{2,3},{3,4},{4,5},{5,6},{6,7},{7,8},{8,9},{9,10},{10,1... | collective-permute-start | bytes 786440 | tf_op jit(solution)/shard_map/ppermute | solution.py:37
  136.3 0.0 collective-permute-done.15
  136.3 8.3 %collective-permute-done.19.refs_4_ = f32[64,1024]{1,0:T(8,128)S(1)} collective-permute-done((f32[64,1024]{1,0:T(8,128)S(1)}, f32[64,1024]{1,0:T(8,128)S(1)}, u32[]{:S(2)}, u32[]{:S(2)}) %collective-permute-start.19) | collective-permute-done | bytes 262176 | tf_op jit(solution)/shard_map/ppermute | solution.py:37
  144.6 2.8 %collective-permute-done.13.refs_1_ = f32[64,1024]{1,0:T(8,128)S(1)} collective-permute-done((f32[64,1024]{1,0:T(8,128)S(1)}, f32[64,1024]{1,0:T(8,128)S(1)}, u32[]{:S(2)}, u32[]{:S(2)}) %collective-permute-start.13) | collective-permute-done | bytes 262176 | tf_op jit(solution)/shard_map/ppermute | solution.py:37
  147.5 1.2 unpack.1
  (19 shorter events, 0.4 us)
Async XLA Ops:
  0.9 1.1 copy-start
  2.0 23.2 %copy-start.1 = (f32[2,12,64,64]{3,2,1,0:T(8,128)S(1)}, f32[2,12,64,64]{3,2,1,0:T(8,128)}, u32[]{:S(2)}) copy-start(f32[2,12,64,64]{3,2,1,0:T(8,128)} %z_ref.1) | copy-start | bytes 1179652
  2.8 26.2 %collective-permute-start.4 = (f32[776,128]{1,0:T(8,128)S(1)}, f32[776,128]{1,0:T(8,128)S(1)}, u32[]{:S(2)}, u32[]{:S(2)}) collective-permute-start(f32[776,128]{1,0:T(8,128)S(1)} %get-tuple-element.28.refs_1_), channel_id=1, source_target_pairs={{0,1},{1,2},{2,3},{3,4},{4,5},{5,6},{6,7},{7,8},{8,9},{9,10},{10,1... | collective-permute-start | bytes 1191944 | tf_op jit(solution)/shard_map/ppermute | solution.py:37
  8.0 22.9 %collective-permute-start = (f32[776,128]{1,0:T(8,128)S(1)}, f32[776,128]{1,0:T(8,128)S(1)}, u32[]{:S(2)}, u32[]{:S(2)}) collective-permute-start(f32[776,128]{1,0:T(8,128)S(1)} %get-tuple-element.28.refs_1_), channel_id=1, source_target_pairs={{0,1023},{1,0},{2,1},{3,2},{4,3},{5,4},{6,5},{7,6},{8,7},{9,8},{10... | collective-permute-start | bytes 1191944 | tf_op jit(solution)/shard_map/ppermute | solution.py:37
  25.2 1.3 copy-start.2
  29.0 14.7 %collective-permute-start.5 = (f32[776,128]{1,0:T(8,128)S(1)}, f32[776,128]{1,0:T(8,128)S(1)}, u32[]{:S(2)}, u32[]{:S(2)}) collective-permute-start(f32[776,128]{1,0:T(8,128)S(1)} %collective-permute-done.4.refs_3_), channel_id=1, source_target_pairs={{0,1},{1,2},{2,3},{3,4},{4,5},{5,6},{6,7},{7,8},{8,9},{9,10},{10,1... | collective-permute-start | bytes 1191944 | tf_op jit(solution)/shard_map/ppermute | solution.py:37
  31.0 14.7 %collective-permute-start.1 = (f32[776,128]{1,0:T(8,128)S(1)}, f32[776,128]{1,0:T(8,128)S(1)}, u32[]{:S(2)}, u32[]{:S(2)}) collective-permute-start(f32[776,128]{1,0:T(8,128)S(1)} %collective-permute-done.refs_2_), channel_id=1, source_target_pairs={{0,1023},{1,0},{2,1},{3,2},{4,3},{5,4},{6,5},{7,6},{8,7},{9,8},{10... | collective-permute-start | bytes 1191944 | tf_op jit(solution)/shard_map/ppermute | solution.py:37
  43.7 14.7 %collective-permute-start.6 = (f32[776,128]{1,0:T(8,128)S(1)}, f32[776,128]{1,0:T(8,128)S(1)}, u32[]{:S(2)}, u32[]{:S(2)}) collective-permute-start(f32[776,128]{1,0:T(8,128)S(1)} %collective-permute-done.5.refs_3_), channel_id=1, source_target_pairs={{0,1},{1,2},{2,3},{3,4},{4,5},{5,6},{6,7},{7,8},{8,9},{9,10},{10,1... | collective-permute-start | bytes 1191944 | tf_op jit(solution)/shard_map/ppermute | solution.py:37
  45.6 16.6 %collective-permute-start.2 = (f32[776,128]{1,0:T(8,128)S(1)}, f32[776,128]{1,0:T(8,128)S(1)}, u32[]{:S(2)}, u32[]{:S(2)}) collective-permute-start(f32[776,128]{1,0:T(8,128)S(1)} %collective-permute-done.1.refs_2_), channel_id=1, source_target_pairs={{0,1023},{1,0},{2,1},{3,2},{4,3},{5,4},{6,5},{7,6},{8,7},{9,8},{10... | collective-permute-start | bytes 1191944 | tf_op jit(solution)/shard_map/ppermute | solution.py:37
  58.4 16.2 %collective-permute-start.7 = (f32[776,128]{1,0:T(8,128)S(1)}, f32[776,128]{1,0:T(8,128)S(1)}, u32[]{:S(2)}, u32[]{:S(2)}) collective-permute-start(f32[776,128]{1,0:T(8,128)S(1)} %pad_maximum_fusion), channel_id=1, source_target_pairs={{0,1016},{1,1017},{2,1018},{3,1019},{4,1020},{5,1021},{6,1022},{7,... | collective-permute-start | bytes 1191944 | tf_op jit(solution)/shard_map/ppermute | solution.py:37
  60.3 23.5 %collective-permute-start.9 = (f32[776,128]{1,0:T(8,128)S(1)}, f32[776,128]{1,0:T(8,128)S(1)}, u32[]{:S(2)}, u32[]{:S(2)}) collective-permute-start(f32[776,128]{1,0:T(8,128)S(1)} %collective-permute-done.6.refs_3_), channel_id=1, source_target_pairs={{0,1},{1,2},{2,3},{3,4},{4,5},{5,6},{6,7},{7,8},{8,9},{9,10},{10,1... | collective-permute-start | bytes 1191944 | tf_op jit(solution)/shard_map/ppermute | solution.py:37
  62.3 21.6 %collective-permute-start.8 = (f32[776,128]{1,0:T(8,128)S(1)}, f32[776,128]{1,0:T(8,128)S(1)}, u32[]{:S(2)}, u32[]{:S(2)}) collective-permute-start(f32[776,128]{1,0:T(8,128)S(1)} %collective-permute-done.2.refs_2_), channel_id=1, source_target_pairs={{0,1023},{1,0},{2,1},{3,2},{4,3},{5,4},{6,5},{7,6},{8,7},{9,8},{10... | collective-permute-start | bytes 1191944 | tf_op jit(solution)/shard_map/ppermute | solution.py:37
  71.3 12.5 %collective-permute-start.3 = (f32[776,128]{1,0:T(8,128)S(1)}, f32[776,128]{1,0:T(8,128)S(1)}, u32[]{:S(2)}, u32[]{:S(2)}) collective-permute-start(f32[776,128]{1,0:T(8,128)S(1)} %collective-permute-done.2.refs_2_), channel_id=1, source_target_pairs={{0,8},{1,9},{2,10},{3,11},{4,12},{5,13},{6,14},{7,15},{8,16},{9,17... | collective-permute-start | bytes 1191944 | tf_op jit(solution)/shard_map/ppermute | solution.py:37
  87.5 21.0 %collective-permute-start.14 = (f32[128,1024]{1,0:T(8,128)S(1)}, f32[128,1024]{1,0:T(8,128)S(1)}, u32[]{:S(2)}, u32[]{:S(2)}) collective-permute-start(f32[128,1024]{1,0:T(8,128)S(1)} %get-tuple-element.41), channel_id=1, source_target_pairs={{0,1023},{1,0},{2,1},{3,2},{4,3},{5,4},{6,5},{7,6},{8,7},{9,8},{10... | collective-permute-start | bytes 1572872 | tf_op jit(solution)/shard_map/ppermute | solution.py:37
  89.6 13.2 %collective-permute-start.16 = (f32[64,1024]{1,0:T(8,128)S(1)}, f32[64,1024]{1,0:T(8,128)S(1)}, u32[]{:S(2)}, u32[]{:S(2)}) collective-permute-start(f32[64,1024]{1,0:T(8,128)S(1)} %get-tuple-element.45), channel_id=1, source_target_pairs={{0,1},{1,2},{2,3},{3,4},{4,5},{5,6},{6,7},{7,8},{8,9},{9,10},{10,1... | collective-permute-start | bytes 786440 | tf_op jit(solution)/shard_map/ppermute | solution.py:37
  93.4 13.2 %collective-permute-start.10 = (f32[64,1024]{1,0:T(8,128)S(1)}, f32[64,1024]{1,0:T(8,128)S(1)}, u32[]{:S(2)}, u32[]{:S(2)}) collective-permute-start(f32[64,1024]{1,0:T(8,128)S(1)} %get-tuple-element.37), channel_id=1, source_target_pairs={{0,1},{1,2},{2,3},{3,4},{4,5},{5,6},{6,7},{7,8},{8,9},{9,10},{10,1... | collective-permute-start | bytes 786440 | tf_op jit(solution)/shard_map/ppermute | solution.py:37
  102.9 13.2 %collective-permute-start.17 = (f32[64,1024]{1,0:T(8,128)S(1)}, f32[64,1024]{1,0:T(8,128)S(1)}, u32[]{:S(2)}, u32[]{:S(2)}) collective-permute-start(f32[64,1024]{1,0:T(8,128)S(1)} %add.33), channel_id=1, source_target_pairs={{0,1},{1,2},{2,3},{3,4},{4,5},{5,6},{6,7},{7,8},{8,9},{9,10},{10,1... | collective-permute-start | bytes 786440 | tf_op jit(solution)/shard_map/ppermute | solution.py:37
  106.6 13.2 %collective-permute-start.11 = (f32[64,1024]{1,0:T(8,128)S(1)}, f32[64,1024]{1,0:T(8,128)S(1)}, u32[]{:S(2)}, u32[]{:S(2)}) collective-permute-start(f32[64,1024]{1,0:T(8,128)S(1)} %add.29), channel_id=1, source_target_pairs={{0,1},{1,2},{2,3},{3,4},{4,5},{5,6},{6,7},{7,8},{8,9},{9,10},{10,1... | collective-permute-start | bytes 786440 | tf_op jit(solution)/shard_map/ppermute | solution.py:37
  108.6 27.7 %collective-permute-start.15 = (f32[128,1024]{1,0:T(8,128)S(1)}, f32[128,1024]{1,0:T(8,128)S(1)}, u32[]{:S(2)}, u32[]{:S(2)}) collective-permute-start(f32[128,1024]{1,0:T(8,128)S(1)} %maximum_add_fusion), channel_id=1, source_target_pairs={{0,6},{1,7},{2,8},{3,9},{4,10},{5,11},{6,12},{7,13},{8,14},{9,15},... | collective-permute-start | bytes 1572872 | tf_op jit(solution)/shard_map/ppermute | solution.py:37
  116.1 15.3 %collective-permute-start.18 = (f32[64,1024]{1,0:T(8,128)S(1)}, f32[64,1024]{1,0:T(8,128)S(1)}, u32[]{:S(2)}, u32[]{:S(2)}) collective-permute-start(f32[64,1024]{1,0:T(8,128)S(1)} %add.34), channel_id=1, source_target_pairs={{0,1},{1,2},{2,3},{3,4},{4,5},{5,6},{6,7},{7,8},{8,9},{9,10},{10,1... | collective-permute-start | bytes 786440 | tf_op jit(solution)/shard_map/ppermute | solution.py:37
  119.8 14.5 %collective-permute-start.12 = (f32[64,1024]{1,0:T(8,128)S(1)}, f32[64,1024]{1,0:T(8,128)S(1)}, u32[]{:S(2)}, u32[]{:S(2)}) collective-permute-start(f32[64,1024]{1,0:T(8,128)S(1)} %add.30), channel_id=1, source_target_pairs={{0,1},{1,2},{2,3},{3,4},{4,5},{5,6},{6,7},{7,8},{8,9},{9,10},{10,1... | collective-permute-start | bytes 786440 | tf_op jit(solution)/shard_map/ppermute | solution.py:37
  131.5 13.1 %collective-permute-start.19 = (f32[64,1024]{1,0:T(8,128)S(1)}, f32[64,1024]{1,0:T(8,128)S(1)}, u32[]{:S(2)}, u32[]{:S(2)}) collective-permute-start(f32[64,1024]{1,0:T(8,128)S(1)} %add.35), channel_id=1, source_target_pairs={{0,1},{1,2},{2,3},{3,4},{4,5},{5,6},{6,7},{7,8},{8,9},{9,10},{10,1... | collective-permute-start | bytes 786440 | tf_op jit(solution)/shard_map/ppermute | solution.py:37
  134.3 13.1 %collective-permute-start.13 = (f32[64,1024]{1,0:T(8,128)S(1)}, f32[64,1024]{1,0:T(8,128)S(1)}, u32[]{:S(2)}, u32[]{:S(2)}) collective-permute-start(f32[64,1024]{1,0:T(8,128)S(1)} %add.31), channel_id=1, source_target_pairs={{0,1},{1,2},{2,3},{3,4},{4,5},{5,6},{6,7},{7,8},{8,9},{9,10},{10,1... | collective-permute-start | bytes 786440 | tf_op jit(solution)/shard_map/ppermute | solution.py:37

commit v4 on v3

--- a/solution.py
+++ b/solution.py
@@ -191,19 +191,21 @@
     )(*(metas[k] for k in ks), zz, ww)
 
 
-def finish_kernel(ds, m0, m1, m4, x0, x1, hh_ref, hl_ref, zz_ref, w_in, *refs):
-    ww_ref, p5, p41, p40, w_ref, picked = refs
+def finish_kernel(ds, *refs):
+    n = len(ds)
+    metas, xs = dict(zip(ds, refs)), refs[n : 2 * n]
+    hh_ref, hl_ref, zz_ref, w_in, ww_ref, p5, p41, p40, w_ref, picked = refs[2 * n :]
     w_ref[...] = w_in[...]
-    for d, meta, x_ref in zip(ds, (m0, m1), (x0, x1)):
-        add_rows(d, meta, x_ref, hh_ref, hl_ref, w_ref)
+    for d, x_ref in zip(ds, xs):
+        add_rows(d, metas[d], x_ref, hh_ref, hl_ref, w_ref)
     for f in range(NC):
         hi, lo = split(w_ref[f])
         ww_ref[f, :, 0 : 2 * B] = hi
         ww_ref[f, :, 2 * B :] = lo
-    spread_half(5, 0, m0, zz_ref, ww_ref, picked.at[0], p5.at[0:B])
-    spread_half(5, 1, m0, zz_ref, ww_ref, picked.at[1], p5.at[B : 2 * B])
-    spread_half(4, 1, m4, zz_ref, ww_ref, picked.at[0], p41)
-    spread_half(4, 0, m4, zz_ref, ww_ref, picked.at[1], p40)
+    spread_half(5, 0, metas[5], zz_ref, ww_ref, picked.at[0], p5.at[0:B])
+    spread_half(5, 1, metas[5], zz_ref, ww_ref, picked.at[1], p5.at[B : 2 * B])
+    spread_half(4, 1, metas[4], zz_ref, ww_ref, picked.at[0], p41)
+    spread_half(4, 0, metas[4], zz_ref, ww_ref, picked.at[1], p40)
 
 
 def finish(ds, metas, xs, hh, hl, zz, w):
@@ -216,7 +218,7 @@
             half,
             half,
         ),
-        in_specs=smem(3) + vmem(6),
+        in_specs=smem(len(ds)) + vmem(len(ds) + 4),
         out_specs=tuple(vmem(4)),
         scratch_shapes=[
             pltpu.VMEM((NC, B, 2 * B), F32),
@@ -224,7 +226,7 @@
         ],
         compiler_params=PARAMS,
         name="finish",
-    )(*metas, *xs, hh, hl, zz, w)
+    )(*(metas[d] for d in ds), *xs, hh, hl, zz, w)
 
 
 def unpack_kernel(*refs):
@@ -261,7 +263,6 @@
         [down[8 - REACH][0 : ZROWS + 4], down[8 - LAST][ZROWS : ZROWS + 4]], axis=0
     )
     up[REACH] = shift(far, -8)
-    down[REACH], up[REACH] = lax.optimization_barrier((down[REACH], up[REACH]))
 
     def note(d):
         metas[d] = up[d][ZROWS:].astype(jnp.int32)
@@ -280,11 +281,10 @@
     w = step((1, -1), w)
     w = step((2, -2), w)
     w = step((3, -3), w)
-    w = step((4, -4), w)
     ww, p5, p41, p40 = finish(
-        (REACH, -REACH),
-        (metas[REACH], metas[-REACH], metas[4]),
-        (up[REACH], down[REACH]),
+        (-5, 5, -4, 4),
+        metas,
+        [up[d] if d >= 0 else down[-d] for d in (-5, 5, -4, 4)],
         hh,
         hl,
         zz,

time: 149 us -> 149 us (level)
    pallas_call x5 -> x4, Pallas kernels: 6.17 us -> 4.88 us  [gather(): pl.pallas_call(functools.partial(gather_kernel, ds, first), out_shape=jax...]
    unnamed x6 -> x8, local copies, waits for them, and re-layouts: 2.45 us -> 3.45 us
  transfers between devices with their start and end apart: 20 -> 20, of which waited for: 11 -> 12; matrix products, arithmetic and copies ran while one was open for 0% -> 0% of each run, Pallas kernels for 6% -> 6%
where the time goes in v4:
time: 149 us; the launch traced here: 148 us
  starting transfers between devices  80.3 us (54%)
  waiting for transfers between devices  48.6 us (33%)
  Pallas kernels  14.3 us (10%)
  local copies, waits for them, and re-layouts  3.5 us (2%)
    ppermute x20, starting transfers between devices, shift(): return lax.ppermute(x, AXES, [(i, (i + by) % size) for i in range(size)])  80.3 us
    ppermute x20, waiting for transfers between devices, shift(): return lax.ppermute(x, AXES, [(i, (i + by) % size) for i in range(size)])  48.6 us
    pallas_call x4, Pallas kernels, gather(): pl.pallas_call(functools.partial(gather_kernel, ds, first), out_shape=jax...  4.88 us
    unnamed x8, local copies, waits for them, and re-layouts  3.45 us
    pallas_call x1, Pallas kernels, finish(): pl.pallas_call(functools.partial(finish_kernel, ds), out_shape=(jax.Shape...  3.31 us
  transfers between devices with their start and end apart: 20, of which 12 were waited for; matrix products, arithmetic and copies ran while one was open for 0% of the time, Pallas kernels for 6%

profile of v4, /device:TPU:8, one launch (start us, length us, event | category | flops | bytes accessed | tf_op | source)
XLA Modules:
  0.0 148.3 jit_solution(14457988183227062431)
XLA Ops:
  0.0 0.1 pad_add_fusion.1.here_ref
  0.1 0.8 pad_add_fusion.cols
  0.9 0.0 copy-start.1
  0.9 1.1 copy-done.1
  2.0 0.0 copy-start.2
  2.0 0.8 pack.1
  2.8 5.2 %collective-permute-start.3 = (f32[776,128]{1,0:T(8,128)S(1)}, f32[776,128]{1,0:T(8,128)S(1)}, u32[]{:S(2)}, u32[]{:S(2)}) collective-permute-start(f32[776,128]{1,0:T(8,128)S(1)} %get-tuple-element.26.refs_1_), channel_id=1, source_target_pairs={{0,1},{1,2},{2,3},{3,4},{4,5},{5,6},{6,7},{7,8},{8,9},{9,10},{10,1... | collective-permute-start | bytes 1191944 | tf_op jit(solution)/shard_map/ppermute | solution.py:37
  8.0 17.2 %collective-permute-start = (f32[776,128]{1,0:T(8,128)S(1)}, f32[776,128]{1,0:T(8,128)S(1)}, u32[]{:S(2)}, u32[]{:S(2)}) collective-permute-start(f32[776,128]{1,0:T(8,128)S(1)} %get-tuple-element.26.refs_1_), channel_id=1, source_target_pairs={{0,1023},{1,0},{2,1},{3,2},{4,3},{5,4},{6,5},{7,6},{8,7},{9,8},{10... | collective-permute-start | bytes 1191944 | tf_op jit(solution)/shard_map/ppermute | solution.py:37
  25.2 0.0 copy-done.2
  25.2 0.0 copy-start.3
  25.2 1.3 copy-done.3
  26.5 1.5 prep.1
  28.0 1.0 gather.4.refs_6_
  29.0 0.0 collective-permute-done.3.refs_3_
  29.0 1.9 %collective-permute-start.4 = (f32[776,128]{1,0:T(8,128)S(1)}, f32[776,128]{1,0:T(8,128)S(1)}, u32[]{:S(2)}, u32[]{:S(2)}) collective-permute-start(f32[776,128]{1,0:T(8,128)S(1)} %collective-permute-done.3.refs_3_), channel_id=1, source_target_pairs={{0,1},{1,2},{2,3},{3,4},{4,5},{5,6},{6,7},{7,8},{8,9},{9,10},{10,1... | collective-permute-start | bytes 1191944 | tf_op jit(solution)/shard_map/ppermute | solution.py:37
  30.9 0.0 collective-permute-done.refs_2_
  31.0 9.1 %collective-permute-start.1 = (f32[776,128]{1,0:T(8,128)S(1)}, f32[776,128]{1,0:T(8,128)S(1)}, u32[]{:S(2)}, u32[]{:S(2)}) collective-permute-start(f32[776,128]{1,0:T(8,128)S(1)} %collective-permute-done.refs_2_), channel_id=1, source_target_pairs={{0,1023},{1,0},{2,1},{3,2},{4,3},{5,4},{6,5},{7,6},{8,7},{9,8},{10... | collective-permute-start | bytes 1191944 | tf_op jit(solution)/shard_map/ppermute | solution.py:37
  40.1 1.3 gather.5.refs_6_
  41.4 2.3 %collective-permute-done.4.refs_3_ = f32[776,128]{1,0:T(8,128)S(1)} collective-permute-done((f32[776,128]{1,0:T(8,128)S(1)}, f32[776,128]{1,0:T(8,128)S(1)}, u32[]{:S(2)}, u32[]{:S(2)}) %collective-permute-start.4) | collective-permute-done | bytes 397344 | tf_op jit(solution)/shard_map/ppermute | solution.py:37
  43.7 1.9 %collective-permute-start.5 = (f32[776,128]{1,0:T(8,128)S(1)}, f32[776,128]{1,0:T(8,128)S(1)}, u32[]{:S(2)}, u32[]{:S(2)}) collective-permute-start(f32[776,128]{1,0:T(8,128)S(1)} %collective-permute-done.4.refs_3_), channel_id=1, source_target_pairs={{0,1},{1,2},{2,3},{3,4},{4,5},{5,6},{6,7},{7,8},{8,9},{9,10},{10,1... | collective-permute-start | bytes 1191944 | tf_op jit(solution)/shard_map/ppermute | solution.py:37
  45.6 0.0 collective-permute-done.1.refs_2_
  45.6 9.1 %collective-permute-start.2 = (f32[776,128]{1,0:T(8,128)S(1)}, f32[776,128]{1,0:T(8,128)S(1)}, u32[]{:S(2)}, u32[]{:S(2)}) collective-permute-start(f32[776,128]{1,0:T(8,128)S(1)} %collective-permute-done.1.refs_2_), channel_id=1, source_target_pairs={{0,1023},{1,0},{2,1},{3,2},{4,3},{5,4},{6,5},{7,6},{8,7},{9,8},{10... | collective-permute-start | bytes 1191944 | tf_op jit(solution)/shard_map/ppermute | solution.py:37
  54.7 1.3 gather.6.refs_6_
  56.0 2.3 %collective-permute-done.5.refs_3_ = f32[776,128]{1,0:T(8,128)S(1)} collective-permute-done((f32[776,128]{1,0:T(8,128)S(1)}, f32[776,128]{1,0:T(8,128)S(1)}, u32[]{:S(2)}, u32[]{:S(2)}) %collective-permute-start.5) | collective-permute-done | bytes 397344 | tf_op jit(solution)/shard_map/ppermute | solution.py:37
  58.4 1.9 %collective-permute-start.6 = (f32[776,128]{1,0:T(8,128)S(1)}, f32[776,128]{1,0:T(8,128)S(1)}, u32[]{:S(2)}, u32[]{:S(2)}) collective-permute-start(f32[776,128]{1,0:T(8,128)S(1)} %pad_maximum_fusion), channel_id=1, source_target_pairs={{0,1016},{1,1017},{2,1018},{3,1019},{4,1020},{5,1021},{6,1022},{7,... | collective-permute-start | bytes 1191944 | tf_op jit(solution)/shard_map/ppermute | solution.py:37
  60.3 1.9 %collective-permute-start.8 = (f32[776,128]{1,0:T(8,128)S(1)}, f32[776,128]{1,0:T(8,128)S(1)}, u32[]{:S(2)}, u32[]{:S(2)}) collective-permute-start(f32[776,128]{1,0:T(8,128)S(1)} %collective-permute-done.5.refs_3_), channel_id=1, source_target_pairs={{0,1},{1,2},{2,3},{3,4},{4,5},{5,6},{6,7},{7,8},{8,9},{9,10},{10,1... | collective-permute-start | bytes 1191944 | tf_op jit(solution)/shard_map/ppermute | solution.py:37
  62.2 0.0 collective-permute-done.2.refs_2_
  62.3 9.1 %collective-permute-start.9 = (f32[776,128]{1,0:T(8,128)S(1)}, f32[776,128]{1,0:T(8,128)S(1)}, u32[]{:S(2)}, u32[]{:S(2)}) collective-permute-start(f32[776,128]{1,0:T(8,128)S(1)} %collective-permute-done.2.refs_2_), channel_id=1, source_target_pairs={{0,1023},{1,0},{2,1},{3,2},{4,3},{5,4},{6,5},{7,6},{8,7},{9,8},{10... | collective-permute-start | bytes 1191944 | tf_op jit(solution)/shard_map/ppermute | solution.py:37
  71.3 1.9 %collective-permute-start.7 = (f32[776,128]{1,0:T(8,128)S(1)}, f32[776,128]{1,0:T(8,128)S(1)}, u32[]{:S(2)}, u32[]{:S(2)}) collective-permute-start(f32[776,128]{1,0:T(8,128)S(1)} %collective-permute-done.2.refs_2_), channel_id=1, source_target_pairs={{0,8},{1,9},{2,10},{3,11},{4,12},{5,13},{6,14},{7,15},{8,16},{9,17... | collective-permute-start | bytes 1191944 | tf_op jit(solution)/shard_map/ppermute | solution.py:37
  73.3 1.3 gather.7.refs_11_
  74.6 0.0 copy-start
  74.6 1.0 copy-done
  75.6 0.0 collective-permute-done.6.refs_5_
  75.6 0.0 collective-permute-done.8.refs_6_
  75.6 1.0 collective-permute-done.9.refs_7_
  76.7 7.1 %collective-permute-done.7.refs_4_ = f32[776,128]{1,0:T(8,128)S(1)} collective-permute-done((f32[776,128]{1,0:T(8,128)S(1)}, f32[776,128]{1,0:T(8,128)S(1)}, u32[]{:S(2)}, u32[]{:S(2)}) %collective-permute-start.7) | collective-permute-done | bytes 397344 | tf_op jit(solution)/shard_map/ppermute | solution.py:37
  83.8 3.3 %finish.1 = (bf16[34,64,256]{2,1,0:T(8,128)(2,1)S(1)}, f32[128,1024]{1,0:T(8,128)S(1)}, f32[64,1024]{1,0:T(8,128)S(1)}, f32[64,1024]{1,0:T(8,128)S(1)}) custom-call(s32[8,128]{1,0:T(8,128)S(1)} %slice_convert_fusion.6.refs_0_, s32[8,128]{1,0:T(8,128)S(1)} %slice_convert_fusion.5.refs_1_, s32[8,128]{1,0:T(8,128)S(1)} %slice_convert_fusion.4.refs_2_, ...), custom_call_target="tpu_custom_call" | custom-call | tf_op jit(solution)/shard_map/finish/pallas_call | solution.py:213
  87.1 2.1 %collective-permute-start.14 = (f32[128,1024]{1,0:T(8,128)S(1)}, f32[128,1024]{1,0:T(8,128)S(1)}, u32[]{:S(2)}, u32[]{:S(2)}) collective-permute-start(f32[128,1024]{1,0:T(8,128)S(1)} %get-tuple-element.37), channel_id=1, source_target_pairs={{0,1023},{1,0},{2,1},{3,2},{4,3},{5,4},{6,5},{7,6},{8,7},{9,8},{10... | collective-permute-start | bytes 1572872 | tf_op jit(solution)/shard_map/ppermute | solution.py:37
  89.2 3.7 %collective-permute-start.16 = (f32[64,1024]{1,0:T(8,128)S(1)}, f32[64,1024]{1,0:T(8,128)S(1)}, u32[]{:S(2)}, u32[]{:S(2)}) collective-permute-start(f32[64,1024]{1,0:T(8,128)S(1)} %get-tuple-element.41), channel_id=1, source_target_pairs={{0,1},{1,2},{2,3},{3,4},{4,5},{5,6},{6,7},{7,8},{8,9},{9,10},{10,1... | collective-permute-start | bytes 786440 | tf_op jit(solution)/shard_map/ppermute | solution.py:37
  93.0 1.9 %collective-permute-start.10 = (f32[64,1024]{1,0:T(8,128)S(1)}, f32[64,1024]{1,0:T(8,128)S(1)}, u32[]{:S(2)}, u32[]{:S(2)}) collective-permute-start(f32[64,1024]{1,0:T(8,128)S(1)} %get-tuple-element.33), channel_id=1, source_target_pairs={{0,1},{1,2},{2,3},{3,4},{4,5},{5,6},{6,7},{7,8},{8,9},{9,10},{10,1... | collective-permute-start | bytes 786440 | tf_op jit(solution)/shard_map/ppermute | solution.py:37
  94.9 2.7 %spread.1 = (f32[64,1024]{1,0:T(8,128)S(1)}, f32[64,1024]{1,0:T(8,128)S(1)}, f32[64,1024]{1,0:T(8,128)S(1)}, f32[64,1024]{1,0:T(8,128)S(1)}, f32[64,1024]{1,0:T(...) custom-call(s32[8,128]{1,0:T(8,128)S(1)} %get-tuple-element.25.meta., ...), custom_call_target="tpu_custom_call" | custom-call | tf_op jit(solution)/shard_map/spread/pallas_call | solution.py:183
  97.6 4.9 %collective-permute-done.16 = f32[64,1024]{1,0:T(8,128)S(1)} collective-permute-done((f32[64,1024]{1,0:T(8,128)S(1)}, f32[64,1024]{1,0:T(8,128)S(1)}, u32[]{:S(2)}, u32[]{:S(2)}) %collective-permute-start.16) | collective-permute-done | bytes 262176 | tf_op jit(solution)/shard_map/ppermute | solution.py:37
  102.5 1.9 %collective-permute-start.17 = (f32[64,1024]{1,0:T(8,128)S(1)}, f32[64,1024]{1,0:T(8,128)S(1)}, u32[]{:S(2)}, u32[]{:S(2)}) collective-permute-start(f32[64,1024]{1,0:T(8,128)S(1)} %add.33), channel_id=1, source_target_pairs={{0,1},{1,2},{2,3},{3,4},{4,5},{5,6},{6,7},{7,8},{8,9},{9,10},{10,1... | collective-permute-start | bytes 786440 | tf_op jit(solution)/shard_map/ppermute | solution.py:37
  104.4 1.7 %collective-permute-done.10 = f32[64,1024]{1,0:T(8,128)S(1)} collective-permute-done((f32[64,1024]{1,0:T(8,128)S(1)}, f32[64,1024]{1,0:T(8,128)S(1)}, u32[]{:S(2)}, u32[]{:S(2)}) %collective-permute-start.10) | collective-permute-done | bytes 262176 | tf_op jit(solution)/shard_map/ppermute | solution.py:37
  106.2 1.9 %collective-permute-start.11 = (f32[64,1024]{1,0:T(8,128)S(1)}, f32[64,1024]{1,0:T(8,128)S(1)}, u32[]{:S(2)}, u32[]{:S(2)}) collective-permute-start(f32[64,1024]{1,0:T(8,128)S(1)} %add.29), channel_id=1, source_target_pairs={{0,1},{1,2},{2,3},{3,4},{4,5},{5,6},{6,7},{7,8},{8,9},{9,10},{10,1... | collective-permute-start | bytes 786440 | tf_op jit(solution)/shard_map/ppermute | solution.py:37
  108.1 0.0 collective-permute-done.14
  108.1 0.1 maximum_add_fusion
  108.2 1.9 %collective-permute-start.15 = (f32[128,1024]{1,0:T(8,128)S(1)}, f32[128,1024]{1,0:T(8,128)S(1)}, u32[]{:S(2)}, u32[]{:S(2)}) collective-permute-start(f32[128,1024]{1,0:T(8,128)S(1)} %maximum_add_fusion), channel_id=1, source_target_pairs={{0,6},{1,7},{2,8},{3,9},{4,10},{5,11},{6,12},{7,13},{8,14},{9,15},... | collective-permute-start | bytes 1572872 | tf_op jit(solution)/shard_map/ppermute | solution.py:37
  110.1 5.6 %collective-permute-done.17 = f32[64,1024]{1,0:T(8,128)S(1)} collective-permute-done((f32[64,1024]{1,0:T(8,128)S(1)}, f32[64,1024]{1,0:T(8,128)S(1)}, u32[]{:S(2)}, u32[]{:S(2)}) %collective-permute-start.17) | collective-permute-done | bytes 262176 | tf_op jit(solution)/shard_map/ppermute | solution.py:37
  115.8 1.9 %collective-permute-start.18 = (f32[64,1024]{1,0:T(8,128)S(1)}, f32[64,1024]{1,0:T(8,128)S(1)}, u32[]{:S(2)}, u32[]{:S(2)}) collective-permute-start(f32[64,1024]{1,0:T(8,128)S(1)} %add.34), channel_id=1, source_target_pairs={{0,1},{1,2},{2,3},{3,4},{4,5},{5,6},{6,7},{7,8},{8,9},{9,10},{10,1... | collective-permute-start | bytes 786440 | tf_op jit(solution)/shard_map/ppermute | solution.py:37
  117.7 1.7 %collective-permute-done.11 = f32[64,1024]{1,0:T(8,128)S(1)} collective-permute-done((f32[64,1024]{1,0:T(8,128)S(1)}, f32[64,1024]{1,0:T(8,128)S(1)}, u32[]{:S(2)}, u32[]{:S(2)}) %collective-permute-start.11) | collective-permute-done | bytes 262176 | tf_op jit(solution)/shard_map/ppermute | solution.py:37
  119.4 1.9 %collective-permute-start.12 = (f32[64,1024]{1,0:T(8,128)S(1)}, f32[64,1024]{1,0:T(8,128)S(1)}, u32[]{:S(2)}, u32[]{:S(2)}) collective-permute-start(f32[64,1024]{1,0:T(8,128)S(1)} %add.30), channel_id=1, source_target_pairs={{0,1},{1,2},{2,3},{3,4},{4,5},{5,6},{6,7},{7,8},{8,9},{9,10},{10,1... | collective-permute-start | bytes 786440 | tf_op jit(solution)/shard_map/ppermute | solution.py:37
  121.3 9.8 %collective-permute-done.18 = f32[64,1024]{1,0:T(8,128)S(1)} collective-permute-done((f32[64,1024]{1,0:T(8,128)S(1)}, f32[64,1024]{1,0:T(8,128)S(1)}, u32[]{:S(2)}, u32[]{:S(2)}) %collective-permute-start.18) | collective-permute-done | bytes 262176 | tf_op jit(solution)/shard_map/ppermute | solution.py:37
  131.2 1.9 %collective-permute-start.19 = (f32[64,1024]{1,0:T(8,128)S(1)}, f32[64,1024]{1,0:T(8,128)S(1)}, u32[]{:S(2)}, u32[]{:S(2)}) collective-permute-start(f32[64,1024]{1,0:T(8,128)S(1)} %add.35), channel_id=1, source_target_pairs={{0,1},{1,2},{2,3},{3,4},{4,5},{5,6},{6,7},{7,8},{8,9},{9,10},{10,1... | collective-permute-start | bytes 786440 | tf_op jit(solution)/shard_map/ppermute | solution.py:37
  133.1 0.8 collective-permute-done.12
  134.0 1.9 %collective-permute-start.13 = (f32[64,1024]{1,0:T(8,128)S(1)}, f32[64,1024]{1,0:T(8,128)S(1)}, u32[]{:S(2)}, u32[]{:S(2)}) collective-permute-start(f32[64,1024]{1,0:T(8,128)S(1)} %add.31), channel_id=1, source_target_pairs={{0,1},{1,2},{2,3},{3,4},{4,5},{5,6},{6,7},{7,8},{8,9},{9,10},{10,1... | collective-permute-start | bytes 786440 | tf_op jit(solution)/shard_map/ppermute | solution.py:37
  135.9 0.0 collective-permute-done.15
  136.0 8.3 %collective-permute-done.19.refs_4_ = f32[64,1024]{1,0:T(8,128)S(1)} collective-permute-done((f32[64,1024]{1,0:T(8,128)S(1)}, f32[64,1024]{1,0:T(8,128)S(1)}, u32[]{:S(2)}, u32[]{:S(2)}) %collective-permute-start.19) | collective-permute-done | bytes 262176 | tf_op jit(solution)/shard_map/ppermute | solution.py:37
  144.3 2.8 %collective-permute-done.13.refs_1_ = f32[64,1024]{1,0:T(8,128)S(1)} collective-permute-done((f32[64,1024]{1,0:T(8,128)S(1)}, f32[64,1024]{1,0:T(8,128)S(1)}, u32[]{:S(2)}, u32[]{:S(2)}) %collective-permute-start.13) | collective-permute-done | bytes 262176 | tf_op jit(solution)/shard_map/ppermute | solution.py:37
  147.1 1.2 unpack.1
  (20 shorter events, 0.3 us)
Async XLA Ops:
  0.9 1.1 copy-start.1
  2.0 23.2 %copy-start.2 = (f32[2,12,64,64]{3,2,1,0:T(8,128)S(1)}, f32[2,12,64,64]{3,2,1,0:T(8,128)}, u32[]{:S(2)}) copy-start(f32[2,12,64,64]{3,2,1,0:T(8,128)} %z_ref.1) | copy-start | bytes 1179652
  2.8 26.2 %collective-permute-start.3 = (f32[776,128]{1,0:T(8,128)S(1)}, f32[776,128]{1,0:T(8,128)S(1)}, u32[]{:S(2)}, u32[]{:S(2)}) collective-permute-start(f32[776,128]{1,0:T(8,128)S(1)} %get-tuple-element.26.refs_1_), channel_id=1, source_target_pairs={{0,1},{1,2},{2,3},{3,4},{4,5},{5,6},{6,7},{7,8},{8,9},{9,10},{10,1... | collective-permute-start | bytes 1191944 | tf_op jit(solution)/shard_map/ppermute | solution.py:37
  8.0 22.9 %collective-permute-start = (f32[776,128]{1,0:T(8,128)S(1)}, f32[776,128]{1,0:T(8,128)S(1)}, u32[]{:S(2)}, u32[]{:S(2)}) collective-permute-start(f32[776,128]{1,0:T(8,128)S(1)} %get-tuple-element.26.refs_1_), channel_id=1, source_target_pairs={{0,1023},{1,0},{2,1},{3,2},{4,3},{5,4},{6,5},{7,6},{8,7},{9,8},{10... | collective-permute-start | bytes 1191944 | tf_op jit(solution)/shard_map/ppermute | solution.py:37
  25.2 1.3 copy-start.3
  29.0 14.7 %collective-permute-start.4 = (f32[776,128]{1,0:T(8,128)S(1)}, f32[776,128]{1,0:T(8,128)S(1)}, u32[]{:S(2)}, u32[]{:S(2)}) collective-permute-start(f32[776,128]{1,0:T(8,128)S(1)} %collective-permute-done.3.refs_3_), channel_id=1, source_target_pairs={{0,1},{1,2},{2,3},{3,4},{4,5},{5,6},{6,7},{7,8},{8,9},{9,10},{10,1... | collective-permute-start | bytes 1191944 | tf_op jit(solution)/shard_map/ppermute | solution.py:37
  31.0 14.7 %collective-permute-start.1 = (f32[776,128]{1,0:T(8,128)S(1)}, f32[776,128]{1,0:T(8,128)S(1)}, u32[]{:S(2)}, u32[]{:S(2)}) collective-permute-start(f32[776,128]{1,0:T(8,128)S(1)} %collective-permute-done.refs_2_), channel_id=1, source_target_pairs={{0,1023},{1,0},{2,1},{3,2},{4,3},{5,4},{6,5},{7,6},{8,7},{9,8},{10... | collective-permute-start | bytes 1191944 | tf_op jit(solution)/shard_map/ppermute | solution.py:37
  43.7 14.7 %collective-permute-start.5 = (f32[776,128]{1,0:T(8,128)S(1)}, f32[776,128]{1,0:T(8,128)S(1)}, u32[]{:S(2)}, u32[]{:S(2)}) collective-permute-start(f32[776,128]{1,0:T(8,128)S(1)} %collective-permute-done.4.refs_3_), channel_id=1, source_target_pairs={{0,1},{1,2},{2,3},{3,4},{4,5},{5,6},{6,7},{7,8},{8,9},{9,10},{10,1... | collective-permute-start | bytes 1191944 | tf_op jit(solution)/shard_map/ppermute | solution.py:37
  45.6 16.6 %collective-permute-start.2 = (f32[776,128]{1,0:T(8,128)S(1)}, f32[776,128]{1,0:T(8,128)S(1)}, u32[]{:S(2)}, u32[]{:S(2)}) collective-permute-start(f32[776,128]{1,0:T(8,128)S(1)} %collective-permute-done.1.refs_2_), channel_id=1, source_target_pairs={{0,1023},{1,0},{2,1},{3,2},{4,3},{5,4},{6,5},{7,6},{8,7},{9,8},{10... | collective-permute-start | bytes 1191944 | tf_op jit(solution)/shard_map/ppermute | solution.py:37
  58.4 17.2 %collective-permute-start.6 = (f32[776,128]{1,0:T(8,128)S(1)}, f32[776,128]{1,0:T(8,128)S(1)}, u32[]{:S(2)}, u32[]{:S(2)}) collective-permute-start(f32[776,128]{1,0:T(8,128)S(1)} %pad_maximum_fusion), channel_id=1, source_target_pairs={{0,1016},{1,1017},{2,1018},{3,1019},{4,1020},{5,1021},{6,1022},{7,... | collective-permute-start | bytes 1191944 | tf_op jit(solution)/shard_map/ppermute | solution.py:37
  60.3 15.3 %collective-permute-start.8 = (f32[776,128]{1,0:T(8,128)S(1)}, f32[776,128]{1,0:T(8,128)S(1)}, u32[]{:S(2)}, u32[]{:S(2)}) collective-permute-start(f32[776,128]{1,0:T(8,128)S(1)} %collective-permute-done.5.refs_3_), channel_id=1, source_target_pairs={{0,1},{1,2},{2,3},{3,4},{4,5},{5,6},{6,7},{7,8},{8,9},{9,10},{10,1... | collective-permute-start | bytes 1191944 | tf_op jit(solution)/shard_map/ppermute | solution.py:37
  62.3 14.4 %collective-permute-start.9 = (f32[776,128]{1,0:T(8,128)S(1)}, f32[776,128]{1,0:T(8,128)S(1)}, u32[]{:S(2)}, u32[]{:S(2)}) collective-permute-start(f32[776,128]{1,0:T(8,128)S(1)} %collective-permute-done.2.refs_2_), channel_id=1, source_target_pairs={{0,1023},{1,0},{2,1},{3,2},{4,3},{5,4},{6,5},{7,6},{8,7},{9,8},{10... | collective-permute-start | bytes 1191944 | tf_op jit(solution)/shard_map/ppermute | solution.py:37
  71.3 12.5 %collective-permute-start.7 = (f32[776,128]{1,0:T(8,128)S(1)}, f32[776,128]{1,0:T(8,128)S(1)}, u32[]{:S(2)}, u32[]{:S(2)}) collective-permute-start(f32[776,128]{1,0:T(8,128)S(1)} %collective-permute-done.2.refs_2_), channel_id=1, source_target_pairs={{0,8},{1,9},{2,10},{3,11},{4,12},{5,13},{6,14},{7,15},{8,16},{9,17... | collective-permute-start | bytes 1191944 | tf_op jit(solution)/shard_map/ppermute | solution.py:37
  74.6 1.0 copy-start
  87.1 21.0 %collective-permute-start.14 = (f32[128,1024]{1,0:T(8,128)S(1)}, f32[128,1024]{1,0:T(8,128)S(1)}, u32[]{:S(2)}, u32[]{:S(2)}) collective-permute-start(f32[128,1024]{1,0:T(8,128)S(1)} %get-tuple-element.37), channel_id=1, source_target_pairs={{0,1023},{1,0},{2,1},{3,2},{4,3},{5,4},{6,5},{7,6},{8,7},{9,8},{10... | collective-permute-start | bytes 1572872 | tf_op jit(solution)/shard_map/ppermute | solution.py:37
  89.2 13.2 %collective-permute-start.16 = (f32[64,1024]{1,0:T(8,128)S(1)}, f32[64,1024]{1,0:T(8,128)S(1)}, u32[]{:S(2)}, u32[]{:S(2)}) collective-permute-start(f32[64,1024]{1,0:T(8,128)S(1)} %get-tuple-element.41), channel_id=1, source_target_pairs={{0,1},{1,2},{2,3},{3,4},{4,5},{5,6},{6,7},{7,8},{8,9},{9,10},{10,1... | collective-permute-start | bytes 786440 | tf_op jit(solution)/shard_map/ppermute | solution.py:37
  93.0 13.2 %collective-permute-start.10 = (f32[64,1024]{1,0:T(8,128)S(1)}, f32[64,1024]{1,0:T(8,128)S(1)}, u32[]{:S(2)}, u32[]{:S(2)}) collective-permute-start(f32[64,1024]{1,0:T(8,128)S(1)} %get-tuple-element.33), channel_id=1, source_target_pairs={{0,1},{1,2},{2,3},{3,4},{4,5},{5,6},{6,7},{7,8},{8,9},{9,10},{10,1... | collective-permute-start | bytes 786440 | tf_op jit(solution)/shard_map/ppermute | solution.py:37
  102.5 13.2 %collective-permute-start.17 = (f32[64,1024]{1,0:T(8,128)S(1)}, f32[64,1024]{1,0:T(8,128)S(1)}, u32[]{:S(2)}, u32[]{:S(2)}) collective-permute-start(f32[64,1024]{1,0:T(8,128)S(1)} %add.33), channel_id=1, source_target_pairs={{0,1},{1,2},{2,3},{3,4},{4,5},{5,6},{6,7},{7,8},{8,9},{9,10},{10,1... | collective-permute-start | bytes 786440 | tf_op jit(solution)/shard_map/ppermute | solution.py:37
  106.2 13.2 %collective-permute-start.11 = (f32[64,1024]{1,0:T(8,128)S(1)}, f32[64,1024]{1,0:T(8,128)S(1)}, u32[]{:S(2)}, u32[]{:S(2)}) collective-permute-start(f32[64,1024]{1,0:T(8,128)S(1)} %add.29), channel_id=1, source_target_pairs={{0,1},{1,2},{2,3},{3,4},{4,5},{5,6},{6,7},{7,8},{8,9},{9,10},{10,1... | collective-permute-start | bytes 786440 | tf_op jit(solution)/shard_map/ppermute | solution.py:37
  108.2 27.7 %collective-permute-start.15 = (f32[128,1024]{1,0:T(8,128)S(1)}, f32[128,1024]{1,0:T(8,128)S(1)}, u32[]{:S(2)}, u32[]{:S(2)}) collective-permute-start(f32[128,1024]{1,0:T(8,128)S(1)} %maximum_add_fusion), channel_id=1, source_target_pairs={{0,6},{1,7},{2,8},{3,9},{4,10},{5,11},{6,12},{7,13},{8,14},{9,15},... | collective-permute-start | bytes 1572872 | tf_op jit(solution)/shard_map/ppermute | solution.py:37
  115.8 15.4 %collective-permute-start.18 = (f32[64,1024]{1,0:T(8,128)S(1)}, f32[64,1024]{1,0:T(8,128)S(1)}, u32[]{:S(2)}, u32[]{:S(2)}) collective-permute-start(f32[64,1024]{1,0:T(8,128)S(1)} %add.34), channel_id=1, source_target_pairs={{0,1},{1,2},{2,3},{3,4},{4,5},{5,6},{6,7},{7,8},{8,9},{9,10},{10,1... | collective-permute-start | bytes 786440 | tf_op jit(solution)/shard_map/ppermute | solution.py:37
  119.4 14.6 %collective-permute-start.12 = (f32[64,1024]{1,0:T(8,128)S(1)}, f32[64,1024]{1,0:T(8,128)S(1)}, u32[]{:S(2)}, u32[]{:S(2)}) collective-permute-start(f32[64,1024]{1,0:T(8,128)S(1)} %add.30), channel_id=1, source_target_pairs={{0,1},{1,2},{2,3},{3,4},{4,5},{5,6},{6,7},{7,8},{8,9},{9,10},{10,1... | collective-permute-start | bytes 786440 | tf_op jit(solution)/shard_map/ppermute | solution.py:37
  131.2 13.1 %collective-permute-start.19 = (f32[64,1024]{1,0:T(8,128)S(1)}, f32[64,1024]{1,0:T(8,128)S(1)}, u32[]{:S(2)}, u32[]{:S(2)}) collective-permute-start(f32[64,1024]{1,0:T(8,128)S(1)} %add.35), channel_id=1, source_target_pairs={{0,1},{1,2},{2,3},{3,4},{4,5},{5,6},{6,7},{7,8},{8,9},{9,10},{10,1... | collective-permute-start | bytes 786440 | tf_op jit(solution)/shard_map/ppermute | solution.py:37
  134.0 13.1 %collective-permute-start.13 = (f32[64,1024]{1,0:T(8,128)S(1)}, f32[64,1024]{1,0:T(8,128)S(1)}, u32[]{:S(2)}, u32[]{:S(2)}) collective-permute-start(f32[64,1024]{1,0:T(8,128)S(1)} %add.31), channel_id=1, source_target_pairs={{0,1},{1,2},{2,3},{3,4},{4,5},{5,6},{6,7},{7,8},{8,9},{9,10},{10,1... | collective-permute-start | bytes 786440 | tf_op jit(solution)/shard_map/ppermute | solution.py:37

commit v5 on v4

--- a/solution.py
+++ b/solution.py
@@ -195,11 +195,11 @@
     n = len(ds)
     metas, xs = dict(zip(ds, refs)), refs[n : 2 * n]
     hh_ref, hl_ref, zz_ref, w_in, ww_ref, p5, p41, p40, w_ref, picked = refs[2 * n :]
-    w_ref[...] = w_in[...]
+    w_ref[...] = jnp.zeros_like(w_ref)
     for d, x_ref in zip(ds, xs):
         add_rows(d, metas[d], x_ref, hh_ref, hl_ref, w_ref)
     for f in range(NC):
-        hi, lo = split(w_ref[f])
+        hi, lo = split(w_in[f] + w_ref[f])
         ww_ref[f, :, 0 : 2 * B] = hi
         ww_ref[f, :, 2 * B :] = lo
     spread_half(5, 0, metas[5], zz_ref, ww_ref, picked.at[0], p5.at[0:B])

time: 149 us -> 149 us (level)
  no operation moved by 1% of the time
where the time goes in v5:
time: 149 us; the launch traced here: 148 us
  starting transfers between devices  80.3 us (54%)
  waiting for transfers between devices  48.5 us (33%)
  Pallas kernels  14.4 us (10%)
  local copies, waits for them, and re-layouts  3.5 us (2%)
    ppermute x20, starting transfers between devices, shift(): return lax.ppermute(x, AXES, [(i, (i + by) % size) for i in range(size)])  80.3 us
    ppermute x20, waiting for transfers between devices, shift(): return lax.ppermute(x, AXES, [(i, (i + by) % size) for i in range(size)])  48.5 us
    pallas_call x4, Pallas kernels, gather(): pl.pallas_call(functools.partial(gather_kernel, ds, first), out_shape=jax...  4.88 us
    unnamed x8, local copies, waits for them, and re-layouts  3.45 us
    pallas_call x1, Pallas kernels, finish(): pl.pallas_call(functools.partial(finish_kernel, ds), out_shape=(jax.Shape...  3.37 us
  transfers between devices with their start and end apart: 20, of which 12 were waited for; matrix products, arithmetic and copies ran while one was open for 0% of the time, Pallas kernels for 6%

profile of v5, /device:TPU:8, one launch (start us, length us, event | category | flops | bytes accessed | tf_op | source)
XLA Modules:
  0.0 148.4 jit_solution(13683520346067306246)
XLA Ops:
  0.0 0.1 pad_add_fusion.1.here_ref
  0.1 0.8 pad_add_fusion.cols
  0.9 0.0 copy-start.1
  0.9 1.1 copy-done.1
  2.0 0.0 copy-start.2
  2.0 0.8 pack.1
  2.8 5.2 %collective-permute-start.3 = (f32[776,128]{1,0:T(8,128)S(1)}, f32[776,128]{1,0:T(8,128)S(1)}, u32[]{:S(2)}, u32[]{:S(2)}) collective-permute-start(f32[776,128]{1,0:T(8,128)S(1)} %get-tuple-element.26.refs_1_), channel_id=1, source_target_pairs={{0,1},{1,2},{2,3},{3,4},{4,5},{5,6},{6,7},{7,8},{8,9},{9,10},{10,1... | collective-permute-start | bytes 1191944 | tf_op jit(solution)/shard_map/ppermute | solution.py:37
  8.0 17.2 %collective-permute-start = (f32[776,128]{1,0:T(8,128)S(1)}, f32[776,128]{1,0:T(8,128)S(1)}, u32[]{:S(2)}, u32[]{:S(2)}) collective-permute-start(f32[776,128]{1,0:T(8,128)S(1)} %get-tuple-element.26.refs_1_), channel_id=1, source_target_pairs={{0,1023},{1,0},{2,1},{3,2},{4,3},{5,4},{6,5},{7,6},{8,7},{9,8},{10... | collective-permute-start | bytes 1191944 | tf_op jit(solution)/shard_map/ppermute | solution.py:37
  25.2 0.0 copy-done.2
  25.2 0.0 copy-start.3
  25.2 1.3 copy-done.3
  26.5 1.5 prep.1
  28.0 1.0 gather.4.refs_6_
  29.0 0.0 collective-permute-done.3.refs_3_
  29.0 1.9 %collective-permute-start.4 = (f32[776,128]{1,0:T(8,128)S(1)}, f32[776,128]{1,0:T(8,128)S(1)}, u32[]{:S(2)}, u32[]{:S(2)}) collective-permute-start(f32[776,128]{1,0:T(8,128)S(1)} %collective-permute-done.3.refs_3_), channel_id=1, source_target_pairs={{0,1},{1,2},{2,3},{3,4},{4,5},{5,6},{6,7},{7,8},{8,9},{9,10},{10,1... | collective-permute-start | bytes 1191944 | tf_op jit(solution)/shard_map/ppermute | solution.py:37
  30.9 0.0 collective-permute-done.refs_2_
  31.0 9.1 %collective-permute-start.1 = (f32[776,128]{1,0:T(8,128)S(1)}, f32[776,128]{1,0:T(8,128)S(1)}, u32[]{:S(2)}, u32[]{:S(2)}) collective-permute-start(f32[776,128]{1,0:T(8,128)S(1)} %collective-permute-done.refs_2_), channel_id=1, source_target_pairs={{0,1023},{1,0},{2,1},{3,2},{4,3},{5,4},{6,5},{7,6},{8,7},{9,8},{10... | collective-permute-start | bytes 1191944 | tf_op jit(solution)/shard_map/ppermute | solution.py:37
  40.1 1.3 gather.5.refs_6_
  41.4 2.3 %collective-permute-done.4.refs_3_ = f32[776,128]{1,0:T(8,128)S(1)} collective-permute-done((f32[776,128]{1,0:T(8,128)S(1)}, f32[776,128]{1,0:T(8,128)S(1)}, u32[]{:S(2)}, u32[]{:S(2)}) %collective-permute-start.4) | collective-permute-done | bytes 397344 | tf_op jit(solution)/shard_map/ppermute | solution.py:37
  43.7 1.9 %collective-permute-start.5 = (f32[776,128]{1,0:T(8,128)S(1)}, f32[776,128]{1,0:T(8,128)S(1)}, u32[]{:S(2)}, u32[]{:S(2)}) collective-permute-start(f32[776,128]{1,0:T(8,128)S(1)} %collective-permute-done.4.refs_3_), channel_id=1, source_target_pairs={{0,1},{1,2},{2,3},{3,4},{4,5},{5,6},{6,7},{7,8},{8,9},{9,10},{10,1... | collective-permute-start | bytes 1191944 | tf_op jit(solution)/shard_map/ppermute | solution.py:37
  45.6 0.0 collective-permute-done.1.refs_2_
  45.6 9.1 %collective-permute-start.2 = (f32[776,128]{1,0:T(8,128)S(1)}, f32[776,128]{1,0:T(8,128)S(1)}, u32[]{:S(2)}, u32[]{:S(2)}) collective-permute-start(f32[776,128]{1,0:T(8,128)S(1)} %collective-permute-done.1.refs_2_), channel_id=1, source_target_pairs={{0,1023},{1,0},{2,1},{3,2},{4,3},{5,4},{6,5},{7,6},{8,7},{9,8},{10... | collective-permute-start | bytes 1191944 | tf_op jit(solution)/shard_map/ppermute | solution.py:37
  54.7 1.3 gather.6.refs_6_
  56.0 2.3 %collective-permute-done.5.refs_3_ = f32[776,128]{1,0:T(8,128)S(1)} collective-permute-done((f32[776,128]{1,0:T(8,128)S(1)}, f32[776,128]{1,0:T(8,128)S(1)}, u32[]{:S(2)}, u32[]{:S(2)}) %collective-permute-start.5) | collective-permute-done | bytes 397344 | tf_op jit(solution)/shard_map/ppermute | solution.py:37
  58.4 1.9 %collective-permute-start.6 = (f32[776,128]{1,0:T(8,128)S(1)}, f32[776,128]{1,0:T(8,128)S(1)}, u32[]{:S(2)}, u32[]{:S(2)}) collective-permute-start(f32[776,128]{1,0:T(8,128)S(1)} %pad_maximum_fusion), channel_id=1, source_target_pairs={{0,1016},{1,1017},{2,1018},{3,1019},{4,1020},{5,1021},{6,1022},{7,... | collective-permute-start | bytes 1191944 | tf_op jit(solution)/shard_map/ppermute | solution.py:37
  60.3 1.9 %collective-permute-start.8 = (f32[776,128]{1,0:T(8,128)S(1)}, f32[776,128]{1,0:T(8,128)S(1)}, u32[]{:S(2)}, u32[]{:S(2)}) collective-permute-start(f32[776,128]{1,0:T(8,128)S(1)} %collective-permute-done.5.refs_3_), channel_id=1, source_target_pairs={{0,1},{1,2},{2,3},{3,4},{4,5},{5,6},{6,7},{7,8},{8,9},{9,10},{10,1... | collective-permute-start | bytes 1191944 | tf_op jit(solution)/shard_map/ppermute | solution.py:37
  62.2 0.0 collective-permute-done.2.refs_2_
  62.3 9.1 %collective-permute-start.9 = (f32[776,128]{1,0:T(8,128)S(1)}, f32[776,128]{1,0:T(8,128)S(1)}, u32[]{:S(2)}, u32[]{:S(2)}) collective-permute-start(f32[776,128]{1,0:T(8,128)S(1)} %collective-permute-done.2.refs_2_), channel_id=1, source_target_pairs={{0,1023},{1,0},{2,1},{3,2},{4,3},{5,4},{6,5},{7,6},{8,7},{9,8},{10... | collective-permute-start | bytes 1191944 | tf_op jit(solution)/shard_map/ppermute | solution.py:37
  71.3 1.9 %collective-permute-start.7 = (f32[776,128]{1,0:T(8,128)S(1)}, f32[776,128]{1,0:T(8,128)S(1)}, u32[]{:S(2)}, u32[]{:S(2)}) collective-permute-start(f32[776,128]{1,0:T(8,128)S(1)} %collective-permute-done.2.refs_2_), channel_id=1, source_target_pairs={{0,8},{1,9},{2,10},{3,11},{4,12},{5,13},{6,14},{7,15},{8,16},{9,17... | collective-permute-start | bytes 1191944 | tf_op jit(solution)/shard_map/ppermute | solution.py:37
  73.3 1.3 gather.7.refs_11_
  74.6 0.0 copy-start
  74.6 1.0 copy-done
  75.6 0.0 collective-permute-done.6.refs_5_
  75.6 0.0 collective-permute-done.8.refs_6_
  75.6 1.0 collective-permute-done.9.refs_7_
  76.7 7.1 %collective-permute-done.7.refs_4_ = f32[776,128]{1,0:T(8,128)S(1)} collective-permute-done((f32[776,128]{1,0:T(8,128)S(1)}, f32[776,128]{1,0:T(8,128)S(1)}, u32[]{:S(2)}, u32[]{:S(2)}) %collective-permute-start.7) | collective-permute-done | bytes 397344 | tf_op jit(solution)/shard_map/ppermute | solution.py:37
  83.8 3.4 %finish.1 = (bf16[34,64,256]{2,1,0:T(8,128)(2,1)S(1)}, f32[128,1024]{1,0:T(8,128)S(1)}, f32[64,1024]{1,0:T(8,128)S(1)}, f32[64,1024]{1,0:T(8,128)S(1)}) custom-call(s32[8,128]{1,0:T(8,128)S(1)} %slice_convert_fusion.6.refs_0_, s32[8,128]{1,0:T(8,128)S(1)} %slice_convert_fusion.5.refs_1_, s32[8,128]{1,0:T(8,128)S(1)} %slice_convert_fusion.4.refs_2_, ...), custom_call_target="tpu_custom_call" | custom-call | tf_op jit(solution)/shard_map/finish/pallas_call | solution.py:213
  87.2 2.1 %collective-permute-start.14 = (f32[128,1024]{1,0:T(8,128)S(1)}, f32[128,1024]{1,0:T(8,128)S(1)}, u32[]{:S(2)}, u32[]{:S(2)}) collective-permute-start(f32[128,1024]{1,0:T(8,128)S(1)} %get-tuple-element.37), channel_id=1, source_target_pairs={{0,1023},{1,0},{2,1},{3,2},{4,3},{5,4},{6,5},{7,6},{8,7},{9,8},{10... | collective-permute-start | bytes 1572872 | tf_op jit(solution)/shard_map/ppermute | solution.py:37
  89.3 3.7 %collective-permute-start.16 = (f32[64,1024]{1,0:T(8,128)S(1)}, f32[64,1024]{1,0:T(8,128)S(1)}, u32[]{:S(2)}, u32[]{:S(2)}) collective-permute-start(f32[64,1024]{1,0:T(8,128)S(1)} %get-tuple-element.41), channel_id=1, source_target_pairs={{0,1},{1,2},{2,3},{3,4},{4,5},{5,6},{6,7},{7,8},{8,9},{9,10},{10,1... | collective-permute-start | bytes 786440 | tf_op jit(solution)/shard_map/ppermute | solution.py:37
  93.0 1.9 %collective-permute-start.10 = (f32[64,1024]{1,0:T(8,128)S(1)}, f32[64,1024]{1,0:T(8,128)S(1)}, u32[]{:S(2)}, u32[]{:S(2)}) collective-permute-start(f32[64,1024]{1,0:T(8,128)S(1)} %get-tuple-element.33), channel_id=1, source_target_pairs={{0,1},{1,2},{2,3},{3,4},{4,5},{5,6},{6,7},{7,8},{8,9},{9,10},{10,1... | collective-permute-start | bytes 786440 | tf_op jit(solution)/shard_map/ppermute | solution.py:37
  95.0 2.7 %spread.1 = (f32[64,1024]{1,0:T(8,128)S(1)}, f32[64,1024]{1,0:T(8,128)S(1)}, f32[64,1024]{1,0:T(8,128)S(1)}, f32[64,1024]{1,0:T(8,128)S(1)}, f32[64,1024]{1,0:T(...) custom-call(s32[8,128]{1,0:T(8,128)S(1)} %get-tuple-element.25.meta., ...), custom_call_target="tpu_custom_call" | custom-call | tf_op jit(solution)/shard_map/spread/pallas_call | solution.py:183
  97.6 4.9 %collective-permute-done.16 = f32[64,1024]{1,0:T(8,128)S(1)} collective-permute-done((f32[64,1024]{1,0:T(8,128)S(1)}, f32[64,1024]{1,0:T(8,128)S(1)}, u32[]{:S(2)}, u32[]{:S(2)}) %collective-permute-start.16) | collective-permute-done | bytes 262176 | tf_op jit(solution)/shard_map/ppermute | solution.py:37
  102.6 1.9 %collective-permute-start.17 = (f32[64,1024]{1,0:T(8,128)S(1)}, f32[64,1024]{1,0:T(8,128)S(1)}, u32[]{:S(2)}, u32[]{:S(2)}) collective-permute-start(f32[64,1024]{1,0:T(8,128)S(1)} %add.33), channel_id=1, source_target_pairs={{0,1},{1,2},{2,3},{3,4},{4,5},{5,6},{6,7},{7,8},{8,9},{9,10},{10,1... | collective-permute-start | bytes 786440 | tf_op jit(solution)/shard_map/ppermute | solution.py:37
  104.5 1.7 %collective-permute-done.10 = f32[64,1024]{1,0:T(8,128)S(1)} collective-permute-done((f32[64,1024]{1,0:T(8,128)S(1)}, f32[64,1024]{1,0:T(8,128)S(1)}, u32[]{:S(2)}, u32[]{:S(2)}) %collective-permute-start.10) | collective-permute-done | bytes 262176 | tf_op jit(solution)/shard_map/ppermute | solution.py:37
  106.3 1.9 %collective-permute-start.11 = (f32[64,1024]{1,0:T(8,128)S(1)}, f32[64,1024]{1,0:T(8,128)S(1)}, u32[]{:S(2)}, u32[]{:S(2)}) collective-permute-start(f32[64,1024]{1,0:T(8,128)S(1)} %add.29), channel_id=1, source_target_pairs={{0,1},{1,2},{2,3},{3,4},{4,5},{5,6},{6,7},{7,8},{8,9},{9,10},{10,1... | collective-permute-start | bytes 786440 | tf_op jit(solution)/shard_map/ppermute | solution.py:37
  108.2 0.0 collective-permute-done.14
  108.2 0.1 maximum_add_fusion
  108.3 1.9 %collective-permute-start.15 = (f32[128,1024]{1,0:T(8,128)S(1)}, f32[128,1024]{1,0:T(8,128)S(1)}, u32[]{:S(2)}, u32[]{:S(2)}) collective-permute-start(f32[128,1024]{1,0:T(8,128)S(1)} %maximum_add_fusion), channel_id=1, source_target_pairs={{0,6},{1,7},{2,8},{3,9},{4,10},{5,11},{6,12},{7,13},{8,14},{9,15},... | collective-permute-start | bytes 1572872 | tf_op jit(solution)/shard_map/ppermute | solution.py:37
  110.2 5.6 %collective-permute-done.17 = f32[64,1024]{1,0:T(8,128)S(1)} collective-permute-done((f32[64,1024]{1,0:T(8,128)S(1)}, f32[64,1024]{1,0:T(8,128)S(1)}, u32[]{:S(2)}, u32[]{:S(2)}) %collective-permute-start.17) | collective-permute-done | bytes 262176 | tf_op jit(solution)/shard_map/ppermute | solution.py:37
  115.8 1.9 %collective-permute-start.18 = (f32[64,1024]{1,0:T(8,128)S(1)}, f32[64,1024]{1,0:T(8,128)S(1)}, u32[]{:S(2)}, u32[]{:S(2)}) collective-permute-start(f32[64,1024]{1,0:T(8,128)S(1)} %add.34), channel_id=1, source_target_pairs={{0,1},{1,2},{2,3},{3,4},{4,5},{5,6},{6,7},{7,8},{8,9},{9,10},{10,1... | collective-permute-start | bytes 786440 | tf_op jit(solution)/shard_map/ppermute | solution.py:37
  117.8 1.7 %collective-permute-done.11 = f32[64,1024]{1,0:T(8,128)S(1)} collective-permute-done((f32[64,1024]{1,0:T(8,128)S(1)}, f32[64,1024]{1,0:T(8,128)S(1)}, u32[]{:S(2)}, u32[]{:S(2)}) %collective-permute-start.11) | collective-permute-done | bytes 262176 | tf_op jit(solution)/shard_map/ppermute | solution.py:37
  119.5 1.9 %collective-permute-start.12 = (f32[64,1024]{1,0:T(8,128)S(1)}, f32[64,1024]{1,0:T(8,128)S(1)}, u32[]{:S(2)}, u32[]{:S(2)}) collective-permute-start(f32[64,1024]{1,0:T(8,128)S(1)} %add.30), channel_id=1, source_target_pairs={{0,1},{1,2},{2,3},{3,4},{4,5},{5,6},{6,7},{7,8},{8,9},{9,10},{10,1... | collective-permute-start | bytes 786440 | tf_op jit(solution)/shard_map/ppermute | solution.py:37
  121.4 9.8 %collective-permute-done.18 = f32[64,1024]{1,0:T(8,128)S(1)} collective-permute-done((f32[64,1024]{1,0:T(8,128)S(1)}, f32[64,1024]{1,0:T(8,128)S(1)}, u32[]{:S(2)}, u32[]{:S(2)}) %collective-permute-start.18) | collective-permute-done | bytes 262176 | tf_op jit(solution)/shard_map/ppermute | solution.py:37
  131.2 1.9 %collective-permute-start.19 = (f32[64,1024]{1,0:T(8,128)S(1)}, f32[64,1024]{1,0:T(8,128)S(1)}, u32[]{:S(2)}, u32[]{:S(2)}) collective-permute-start(f32[64,1024]{1,0:T(8,128)S(1)} %add.35), channel_id=1, source_target_pairs={{0,1},{1,2},{2,3},{3,4},{4,5},{5,6},{6,7},{7,8},{8,9},{9,10},{10,1... | collective-permute-start | bytes 786440 | tf_op jit(solution)/shard_map/ppermute | solution.py:37
  133.2 0.8 collective-permute-done.12
  134.1 1.9 %collective-permute-start.13 = (f32[64,1024]{1,0:T(8,128)S(1)}, f32[64,1024]{1,0:T(8,128)S(1)}, u32[]{:S(2)}, u32[]{:S(2)}) collective-permute-start(f32[64,1024]{1,0:T(8,128)S(1)} %add.31), channel_id=1, source_target_pairs={{0,1},{1,2},{2,3},{3,4},{4,5},{5,6},{6,7},{7,8},{8,9},{9,10},{10,1... | collective-permute-start | bytes 786440 | tf_op jit(solution)/shard_map/ppermute | solution.py:37
  136.0 0.0 collective-permute-done.15
  136.0 8.3 %collective-permute-done.19.refs_4_ = f32[64,1024]{1,0:T(8,128)S(1)} collective-permute-done((f32[64,1024]{1,0:T(8,128)S(1)}, f32[64,1024]{1,0:T(8,128)S(1)}, u32[]{:S(2)}, u32[]{:S(2)}) %collective-permute-start.19) | collective-permute-done | bytes 262176 | tf_op jit(solution)/shard_map/ppermute | solution.py:37
  144.4 2.8 %collective-permute-done.13.refs_1_ = f32[64,1024]{1,0:T(8,128)S(1)} collective-permute-done((f32[64,1024]{1,0:T(8,128)S(1)}, f32[64,1024]{1,0:T(8,128)S(1)}, u32[]{:S(2)}, u32[]{:S(2)}) %collective-permute-start.13) | collective-permute-done | bytes 262176 | tf_op jit(solution)/shard_map/ppermute | solution.py:37
  147.2 1.2 unpack.1
  (20 shorter events, 0.3 us)
Async XLA Ops:
  0.9 1.1 copy-start.1
  2.0 23.2 %copy-start.2 = (f32[2,12,64,64]{3,2,1,0:T(8,128)S(1)}, f32[2,12,64,64]{3,2,1,0:T(8,128)}, u32[]{:S(2)}) copy-start(f32[2,12,64,64]{3,2,1,0:T(8,128)} %z_ref.1) | copy-start | bytes 1179652
  2.8 26.2 %collective-permute-start.3 = (f32[776,128]{1,0:T(8,128)S(1)}, f32[776,128]{1,0:T(8,128)S(1)}, u32[]{:S(2)}, u32[]{:S(2)}) collective-permute-start(f32[776,128]{1,0:T(8,128)S(1)} %get-tuple-element.26.refs_1_), channel_id=1, source_target_pairs={{0,1},{1,2},{2,3},{3,4},{4,5},{5,6},{6,7},{7,8},{8,9},{9,10},{10,1... | collective-permute-start | bytes 1191944 | tf_op jit(solution)/shard_map/ppermute | solution.py:37
  8.0 22.9 %collective-permute-start = (f32[776,128]{1,0:T(8,128)S(1)}, f32[776,128]{1,0:T(8,128)S(1)}, u32[]{:S(2)}, u32[]{:S(2)}) collective-permute-start(f32[776,128]{1,0:T(8,128)S(1)} %get-tuple-element.26.refs_1_), channel_id=1, source_target_pairs={{0,1023},{1,0},{2,1},{3,2},{4,3},{5,4},{6,5},{7,6},{8,7},{9,8},{10... | collective-permute-start | bytes 1191944 | tf_op jit(solution)/shard_map/ppermute | solution.py:37
  25.2 1.3 copy-start.3
  29.0 14.7 %collective-permute-start.4 = (f32[776,128]{1,0:T(8,128)S(1)}, f32[776,128]{1,0:T(8,128)S(1)}, u32[]{:S(2)}, u32[]{:S(2)}) collective-permute-start(f32[776,128]{1,0:T(8,128)S(1)} %collective-permute-done.3.refs_3_), channel_id=1, source_target_pairs={{0,1},{1,2},{2,3},{3,4},{4,5},{5,6},{6,7},{7,8},{8,9},{9,10},{10,1... | collective-permute-start | bytes 1191944 | tf_op jit(solution)/shard_map/ppermute | solution.py:37
  31.0 14.7 %collective-permute-start.1 = (f32[776,128]{1,0:T(8,128)S(1)}, f32[776,128]{1,0:T(8,128)S(1)}, u32[]{:S(2)}, u32[]{:S(2)}) collective-permute-start(f32[776,128]{1,0:T(8,128)S(1)} %collective-permute-done.refs_2_), channel_id=1, source_target_pairs={{0,1023},{1,0},{2,1},{3,2},{4,3},{5,4},{6,5},{7,6},{8,7},{9,8},{10... | collective-permute-start | bytes 1191944 | tf_op jit(solution)/shard_map/ppermute | solution.py:37
  43.7 14.7 %collective-permute-start.5 = (f32[776,128]{1,0:T(8,128)S(1)}, f32[776,128]{1,0:T(8,128)S(1)}, u32[]{:S(2)}, u32[]{:S(2)}) collective-permute-start(f32[776,128]{1,0:T(8,128)S(1)} %collective-permute-done.4.refs_3_), channel_id=1, source_target_pairs={{0,1},{1,2},{2,3},{3,4},{4,5},{5,6},{6,7},{7,8},{8,9},{9,10},{10,1... | collective-permute-start | bytes 1191944 | tf_op jit(solution)/shard_map/ppermute | solution.py:37
  45.6 16.6 %collective-permute-start.2 = (f32[776,128]{1,0:T(8,128)S(1)}, f32[776,128]{1,0:T(8,128)S(1)}, u32[]{:S(2)}, u32[]{:S(2)}) collective-permute-start(f32[776,128]{1,0:T(8,128)S(1)} %collective-permute-done.1.refs_2_), channel_id=1, source_target_pairs={{0,1023},{1,0},{2,1},{3,2},{4,3},{5,4},{6,5},{7,6},{8,7},{9,8},{10... | collective-permute-start | bytes 1191944 | tf_op jit(solution)/shard_map/ppermute | solution.py:37
  58.4 17.2 %collective-permute-start.6 = (f32[776,128]{1,0:T(8,128)S(1)}, f32[776,128]{1,0:T(8,128)S(1)}, u32[]{:S(2)}, u32[]{:S(2)}) collective-permute-start(f32[776,128]{1,0:T(8,128)S(1)} %pad_maximum_fusion), channel_id=1, source_target_pairs={{0,1016},{1,1017},{2,1018},{3,1019},{4,1020},{5,1021},{6,1022},{7,... | collective-permute-start | bytes 1191944 | tf_op jit(solution)/shard_map/ppermute | solution.py:37
  60.3 15.3 %collective-permute-start.8 = (f32[776,128]{1,0:T(8,128)S(1)}, f32[776,128]{1,0:T(8,128)S(1)}, u32[]{:S(2)}, u32[]{:S(2)}) collective-permute-start(f32[776,128]{1,0:T(8,128)S(1)} %collective-permute-done.5.refs_3_), channel_id=1, source_target_pairs={{0,1},{1,2},{2,3},{3,4},{4,5},{5,6},{6,7},{7,8},{8,9},{9,10},{10,1... | collective-permute-start | bytes 1191944 | tf_op jit(solution)/shard_map/ppermute | solution.py:37
  62.3 14.4 %collective-permute-start.9 = (f32[776,128]{1,0:T(8,128)S(1)}, f32[776,128]{1,0:T(8,128)S(1)}, u32[]{:S(2)}, u32[]{:S(2)}) collective-permute-start(f32[776,128]{1,0:T(8,128)S(1)} %collective-permute-done.2.refs_2_), channel_id=1, source_target_pairs={{0,1023},{1,0},{2,1},{3,2},{4,3},{5,4},{6,5},{7,6},{8,7},{9,8},{10... | collective-permute-start | bytes 1191944 | tf_op jit(solution)/shard_map/ppermute | solution.py:37
  71.3 12.5 %collective-permute-start.7 = (f32[776,128]{1,0:T(8,128)S(1)}, f32[776,128]{1,0:T(8,128)S(1)}, u32[]{:S(2)}, u32[]{:S(2)}) collective-permute-start(f32[776,128]{1,0:T(8,128)S(1)} %collective-permute-done.2.refs_2_), channel_id=1, source_target_pairs={{0,8},{1,9},{2,10},{3,11},{4,12},{5,13},{6,14},{7,15},{8,16},{9,17... | collective-permute-start | bytes 1191944 | tf_op jit(solution)/shard_map/ppermute | solution.py:37
  74.6 1.0 copy-start
  87.2 21.0 %collective-permute-start.14 = (f32[128,1024]{1,0:T(8,128)S(1)}, f32[128,1024]{1,0:T(8,128)S(1)}, u32[]{:S(2)}, u32[]{:S(2)}) collective-permute-start(f32[128,1024]{1,0:T(8,128)S(1)} %get-tuple-element.37), channel_id=1, source_target_pairs={{0,1023},{1,0},{2,1},{3,2},{4,3},{5,4},{6,5},{7,6},{8,7},{9,8},{10... | collective-permute-start | bytes 1572872 | tf_op jit(solution)/shard_map/ppermute | solution.py:37
  89.3 13.2 %collective-permute-start.16 = (f32[64,1024]{1,0:T(8,128)S(1)}, f32[64,1024]{1,0:T(8,128)S(1)}, u32[]{:S(2)}, u32[]{:S(2)}) collective-permute-start(f32[64,1024]{1,0:T(8,128)S(1)} %get-tuple-element.41), channel_id=1, source_target_pairs={{0,1},{1,2},{2,3},{3,4},{4,5},{5,6},{6,7},{7,8},{8,9},{9,10},{10,1... | collective-permute-start | bytes 786440 | tf_op jit(solution)/shard_map/ppermute | solution.py:37
  93.0 13.2 %collective-permute-start.10 = (f32[64,1024]{1,0:T(8,128)S(1)}, f32[64,1024]{1,0:T(8,128)S(1)}, u32[]{:S(2)}, u32[]{:S(2)}) collective-permute-start(f32[64,1024]{1,0:T(8,128)S(1)} %get-tuple-element.33), channel_id=1, source_target_pairs={{0,1},{1,2},{2,3},{3,4},{4,5},{5,6},{6,7},{7,8},{8,9},{9,10},{10,1... | collective-permute-start | bytes 786440 | tf_op jit(solution)/shard_map/ppermute | solution.py:37
  102.6 13.2 %collective-permute-start.17 = (f32[64,1024]{1,0:T(8,128)S(1)}, f32[64,1024]{1,0:T(8,128)S(1)}, u32[]{:S(2)}, u32[]{:S(2)}) collective-permute-start(f32[64,1024]{1,0:T(8,128)S(1)} %add.33), channel_id=1, source_target_pairs={{0,1},{1,2},{2,3},{3,4},{4,5},{5,6},{6,7},{7,8},{8,9},{9,10},{10,1... | collective-permute-start | bytes 786440 | tf_op jit(solution)/shard_map/ppermute | solution.py:37
  106.3 13.2 %collective-permute-start.11 = (f32[64,1024]{1,0:T(8,128)S(1)}, f32[64,1024]{1,0:T(8,128)S(1)}, u32[]{:S(2)}, u32[]{:S(2)}) collective-permute-start(f32[64,1024]{1,0:T(8,128)S(1)} %add.29), channel_id=1, source_target_pairs={{0,1},{1,2},{2,3},{3,4},{4,5},{5,6},{6,7},{7,8},{8,9},{9,10},{10,1... | collective-permute-start | bytes 786440 | tf_op jit(solution)/shard_map/ppermute | solution.py:37
  108.3 27.7 %collective-permute-start.15 = (f32[128,1024]{1,0:T(8,128)S(1)}, f32[128,1024]{1,0:T(8,128)S(1)}, u32[]{:S(2)}, u32[]{:S(2)}) collective-permute-start(f32[128,1024]{1,0:T(8,128)S(1)} %maximum_add_fusion), channel_id=1, source_target_pairs={{0,6},{1,7},{2,8},{3,9},{4,10},{5,11},{6,12},{7,13},{8,14},{9,15},... | collective-permute-start | bytes 1572872 | tf_op jit(solution)/shard_map/ppermute | solution.py:37
  115.8 15.4 %collective-permute-start.18 = (f32[64,1024]{1,0:T(8,128)S(1)}, f32[64,1024]{1,0:T(8,128)S(1)}, u32[]{:S(2)}, u32[]{:S(2)}) collective-permute-start(f32[64,1024]{1,0:T(8,128)S(1)} %add.34), channel_id=1, source_target_pairs={{0,1},{1,2},{2,3},{3,4},{4,5},{5,6},{6,7},{7,8},{8,9},{9,10},{10,1... | collective-permute-start | bytes 786440 | tf_op jit(solution)/shard_map/ppermute | solution.py:37
  119.5 14.6 %collective-permute-start.12 = (f32[64,1024]{1,0:T(8,128)S(1)}, f32[64,1024]{1,0:T(8,128)S(1)}, u32[]{:S(2)}, u32[]{:S(2)}) collective-permute-start(f32[64,1024]{1,0:T(8,128)S(1)} %add.30), channel_id=1, source_target_pairs={{0,1},{1,2},{2,3},{3,4},{4,5},{5,6},{6,7},{7,8},{8,9},{9,10},{10,1... | collective-permute-start | bytes 786440 | tf_op jit(solution)/shard_map/ppermute | solution.py:37
  131.2 13.1 %collective-permute-start.19 = (f32[64,1024]{1,0:T(8,128)S(1)}, f32[64,1024]{1,0:T(8,128)S(1)}, u32[]{:S(2)}, u32[]{:S(2)}) collective-permute-start(f32[64,1024]{1,0:T(8,128)S(1)} %add.35), channel_id=1, source_target_pairs={{0,1},{1,2},{2,3},{3,4},{4,5},{5,6},{6,7},{7,8},{8,9},{9,10},{10,1... | collective-permute-start | bytes 786440 | tf_op jit(solution)/shard_map/ppermute | solution.py:37
  134.1 13.1 %collective-permute-start.13 = (f32[64,1024]{1,0:T(8,128)S(1)}, f32[64,1024]{1,0:T(8,128)S(1)}, u32[]{:S(2)}, u32[]{:S(2)}) collective-permute-start(f32[64,1024]{1,0:T(8,128)S(1)} %add.31), channel_id=1, source_target_pairs={{0,1},{1,2},{2,3},{3,4},{4,5},{5,6},{6,7},{7,8},{8,9},{9,10},{10,1... | collective-permute-start | bytes 786440 | tf_op jit(solution)/shard_map/ppermute | solution.py:37
